TPU v7x, 32 devices: a whole 2x2x4 slice. The times are simulated.
32 devices in a mesh: dp: 4 (over y, x), ctx: 8 (over z, core).
Axes of the slice: x: 2, y: 2, z: 4, core: 2. Of those that a mesh axis runs over, the one named last changes fastest.
Arguments:
- query_rows: bfloat16 [4, 1024, 2048], P('dp', 'ctx'), may hold values from -6 to 6
- key_rows: bfloat16 [4, 1024, 2048], P('dp', 'ctx'), may hold values from -6 to 6
- value_rows: bfloat16 [4, 1024, 2048], P('dp', 'ctx'), may hold values from -6 to 6
- norm_gain: float32 [2048], replicated, may hold values from 0.1 to 1.9
- out_weight: bfloat16 [2048, 2048], P('ctx'), may hold values from -0.125 to 0.125
- cotangent: bfloat16 [4, 1024, 2048], P('dp', 'ctx'), may hold values from -6 to 6
Outputs:
- mixed: bfloat16 [4, 1024, 2048], P('dp', 'ctx')
- grad_queries: bfloat16 [4, 1024, 2048], P('dp', 'ctx')
- grad_keys: bfloat16 [4, 1024, 2048], P('dp', 'ctx')
- grad_values: bfloat16 [4, 1024, 2048], P('dp', 'ctx')
- grad_weight: float32 [2048, 2048], P('ctx')
All inputs are finite; a program needn't handle non-finite values.
Results may differ from a plain program's by a relative error of at most 0.025.
Values may be sent and summed in bfloat16 or wider, within the bound.
No kernel may reach another device: no remote copies, remote signals or barrier semaphores. Data moves between devices by JAX's collectives and lax.ppermute only.
A program may use at most 192 MiB of HBM per device.

v0:
```python
import math

import jax
import jax.numpy as jnp
from jax import lax
from jax.sharding import PartitionSpec as P

HEAD = 128


epsilon = 1e-06
highest_precision = lax.Precision.HIGHEST


def carried_in(value, axis, combine, identity):
    size, index = (lax.axis_size(axis), lax.axis_index(axis))
    everything = lax.all_gather(value, axis)
    start = jnp.broadcast_to(jnp.asarray(identity, value.dtype), value.shape)

    def carried_turn(k, before):
        reached = k < index
        new = combine(before, everything[k])
        return jnp.where(reached, new, before)

    return lax.fori_loop(0, size, carried_turn, start)


def entering(value, axis, combine, identity):
    size, index = (lax.axis_size(axis), lax.axis_index(axis))
    everything = lax.all_gather(value.astype(jnp.bfloat16), axis)
    start = jnp.broadcast_to(jnp.asarray(identity, value.dtype), value.shape)

    def entering_turn(k, before):
        at = size - 1 - k
        reached = at > index
        new = combine(before, everything[at].astype(value.dtype))
        return jnp.where(reached, new, before)

    return lax.fori_loop(0, size, entering_turn, start)


def feature(values):
    wide = values.astype(jnp.float32)
    return jnp.where(wide > 0, wide + 1.0, jnp.exp(jnp.minimum(wide, 0.0))).astype(jnp.bfloat16)


def feature_slope(values):
    wide = values.astype(jnp.float32)
    return jnp.where(wide > 0, 1.0, jnp.exp(jnp.minimum(wide, 0.0)))


def add_states(earlier, later):
    return earlier + later


def on_device(query_rows, key_rows, value_rows, norm_gain, out_weight, cotangent):
    length = query_rows.shape[1]
    width = query_rows.shape[2]
    heads = width // HEAD
    shape3 = (length, heads, HEAD)
    weight = lax.all_gather(out_weight, "ctx", axis=0, tiled=True)
    query_seq = query_rows[0]
    key_seq = key_rows[0]
    query_per_head = feature(query_seq).reshape(shape3)
    key_per_head = feature(key_seq).reshape(shape3)
    value_per_head = value_rows[0].reshape(shape3)
    local_state = jnp.einsum(
        "wmx,wmt->mxt", key_per_head, value_per_head, preferred_element_type=jnp.float32
    )
    zero_state = jnp.zeros_like(local_state)
    prefix_state = carried_in(local_state, "ctx", add_states, zero_state)
    causal = jnp.tril(jnp.ones((length, length), dtype=bool))
    scores = jnp.einsum(
        "thd,shd->hts", query_per_head, key_per_head, preferred_element_type=jnp.float32
    )
    probs = jnp.where(causal, scores, 0.0).astype(jnp.bfloat16)
    query_wide_rows = query_per_head.astype(jnp.float32)
    attended_output = jnp.einsum(
        "hts,shv->thv", probs, value_per_head, preferred_element_type=jnp.float32
    )
    attended_output = attended_output + jnp.einsum(
        "wrf,rfp->wrp", query_wide_rows, prefix_state, precision=highest_precision
    )
    inverse = lax.rsqrt(
        jnp.mean(attended_output * attended_output, axis=-1, keepdims=True) + epsilon
    )
    gain_heads = norm_gain.reshape(heads, HEAD)
    normed = (attended_output * inverse * gain_heads).reshape(length, width).astype(jnp.bfloat16)
    mixed = jnp.dot(normed, weight, preferred_element_type=jnp.float32).astype(jnp.bfloat16)
    upstream = cotangent[0]
    d_normed = lax.dot_general(
        upstream, weight, (((1,), (1,)), ((), ())), preferred_element_type=jnp.float32
    ).reshape(shape3)
    scaled = d_normed * gain_heads
    attended_gradient = (
        inverse
        * (
            scaled
            - attended_output
            * inverse
            * inverse
            * jnp.mean(scaled * attended_output, axis=-1, keepdims=True)
        )
    ).astype(jnp.bfloat16)
    grad_local = jnp.einsum(
        "ibg,ibq->bgq", query_per_head, attended_gradient, preferred_element_type=jnp.float32
    )
    suffix_state = entering(grad_local, "ctx", add_states, zero_state)
    d_scores = jnp.einsum(
        "thv,shv->hts", attended_gradient, value_per_head, preferred_element_type=jnp.float32
    )
    d_probs = jnp.where(causal, d_scores, 0.0).astype(jnp.bfloat16)
    wide_gradient = attended_gradient.astype(jnp.float32)
    value_wide_rows = value_per_head.astype(jnp.float32)
    key_wide_rows = key_per_head.astype(jnp.float32)
    query_gradient = jnp.einsum(
        "hts,shk->thk", d_probs, key_per_head, preferred_element_type=jnp.float32
    )
    query_gradient = query_gradient + jnp.einsum(
        "fxn,xpn->fxp", wide_gradient, prefix_state, precision=highest_precision
    )
    key_gradient = jnp.einsum(
        "hts,thk->shk", d_probs, query_per_head, preferred_element_type=jnp.float32
    )
    key_gradient = key_gradient + jnp.einsum(
        "mcu,cxu->mcx", value_wide_rows, suffix_state, precision=highest_precision
    )
    value_gradient = jnp.einsum(
        "hts,thv->shv", probs, attended_gradient, preferred_element_type=jnp.float32
    )
    value_gradient = value_gradient + jnp.einsum(
        "inz,nzc->inc", key_wide_rows, suffix_state, precision=highest_precision
    )
    grad_queries = (query_gradient.reshape(length, width) * feature_slope(query_seq)).astype(
        jnp.bfloat16
    )
    grad_keys = (key_gradient.reshape(length, width) * feature_slope(key_seq)).astype(jnp.bfloat16)
    grad_values = value_gradient.reshape(length, width).astype(jnp.bfloat16)
    devices_dp = lax.axis_size("dp")
    devices_ctx = lax.axis_size("ctx")
    loss_scale = 1.0 / math.sqrt(devices_dp * devices_ctx * length)
    shares = lax.psum_scatter(
        lax.dot_general(
            normed, upstream, (((0,), (0,)), ((), ())), preferred_element_type=jnp.float32
        ).astype(jnp.bfloat16),
        "ctx",
        scatter_dimension=0,
        tiled=True,
    )
    summed = lax.psum(shares, "dp").astype(jnp.float32)
    grad_weight = summed * loss_scale
    return (mixed[None], grad_queries[None], grad_keys[None], grad_values[None], grad_weight)


def solution(mesh):
    return jax.shard_map(
        on_device,
        mesh=mesh,
        in_specs=(
            P("dp", "ctx", None),
            P("dp", "ctx", None),
            P("dp", "ctx", None),
            P(),
            P("ctx", None),
            P("dp", "ctx", None),
        ),
        out_specs=(
            P("dp", "ctx", None),
            P("dp", "ctx", None),
            P("dp", "ctx", None),
            P("dp", "ctx", None),
            P("ctx", None),
        ),
        check_vma=False,
    )
```

profile of v0, /device:TPU:16, one launch (start us, length us, event | category | flops | bytes accessed | tf_op | source)
XLA Modules:
  0.0 386.3 jit_solution(14783138310372770169)
XLA Ops:
  16.5 77.3 %all-gather.8.cloned.1.call-done = f32[128,128,128]{2,1,0:T(8,128)} async-done(((f32[16,128,128]{2,1,0:T(8,128)}), f32[128,128,128]{2,1,0:T(8,128)}) %all-gather.8.cloned.1.call-update) | async-done | bytes 8388624 | tf_op jit(solution)/shard_map/all_gather | solution.py:17
  93.7 13.1 %while.30 = (s32[]{:T(128)}, f32[16,128,128]{2,1,0:T(8,128)S(1)}, s32[]{:T(128)}, f32[8,16,128,128]{3,2,1,0:T(8,128)}, s32[]{:T(128)}, /*index=5*/s32[]{:T(128)}) while((s32[]{:T(128)}, f32[16,128,128]{2,1,0:T(8,128)S(1)}, s32[]{:T(128)}, f32[8,16,128,128]{3,2,1,0:T(8,128)}, s32[]{:T(128)}, /*index=5*/s32[]{:T(128)}) %tuple.93), condition=%wide.region_1.2_spmd.clone, body=%wide.region_0.1_spmd.clone.sunk | while | flops 786436 | bytes 3145829 | solution.py:25
  101.8 1.7 add_select_fusion.4
  109.5 66.5 %all-gather.6.cloned.1.call-done = bf16[2048,2048]{1,0:T(8,128)(2,1)} async-done(((bf16[256,2048]{1,0:T(8,128)(2,1)}), bf16[2048,2048]{1,0:T(8,128)(2,1)}) %all-gather.6.cloned.1.call-update) | async-done | bytes 8388624 | tf_op jit(solution)/shard_map/all_gather | solution.py:61
  176.0 5.8 %multiply_reduce_fusion = (f32[128,16]{0,1:T(8,128)S(1)}, f32[128,16]{0,1:T(8,128)S(1)}, f32[128,16,128]{0,2,1:T(8,128)S(1)}) fusion(f32[128,16,128]{0,2,1:T(8,128)S(1)} %fusion.1, f32[16,128]{1,0:T(8,128)S(1)} %bitcast.89, bf16[16,128,2048]{2,1,0:T(8,128)(2,1)} %bitcast.69, bf16[1,128,2048]{2,1,0:T(8,128)(2,1)S(1)} %copy-done), kind=kOutput, calls=%fused_computation.38 | convolution fusion | flops 1075048448 | bytes 11034624 | tf_op jit(solution)/shard_map/dot_general | solution.py:91
  182.9 2.3 convolution_convert_fusion.2
  185.3 5.6 %convolution_convert_fusion = bf16[2048,2048]{1,0:T(8,128)(2,1)} fusion(bf16[128,2048]{0,1:T(8,128)(2,1)S(1)} %bitcast.70, bf16[1,128,2048]{2,1,0:T(8,128)(2,1)S(1)} %copy-done), kind=kOutput, calls=%fused_computation.2 | convolution fusion | flops 1077936128 | bytes 9437184 | tf_op jit(solution)/shard_map/dot_general | solution.py:143
  191.2 1.8 fusion.4
  193.0 1.7 fusion.27
  194.7 2.6 convolution_add_fusion.2
  198.9 2.5 fusion.28
  201.3 2.5 fusion.29
  203.8 2.1 fusion.10
  205.9 5.5 %fusion = bf16[1,128,2048]{2,1,0:T(8,128)(2,1)} fusion(bf16[128,2048]{0,1:T(8,128)(2,1)S(1)} %bitcast.71, bf16[2048,2048]{1,0:T(8,128)(2,1)} %all-gather.6.cloned.1.call-done), kind=kOutput, calls=%fused_computation.4 | convolution fusion | flops 1074003968 | bytes 9437184 | tf_op jit(solution)/shard_map/dot_general | solution.py:89
  211.5 19.8 %all-gather.10.cloned.1.call-done = bf16[128,128,128]{2,1,0:T(8,128)(2,1)} async-done(((bf16[16,128,128]{2,1,0:T(8,128)(2,1)}), bf16[128,128,128]{2,1,0:T(8,128)(2,1)}) %all-gather.10.cloned.1.call-update) | async-done | bytes 4194320 | tf_op jit(solution)/shard_map/all_gather | solution.py:30
  231.2 13.3 %while.31 = (s32[]{:T(128)}, f32[16,128,128]{2,1,0:T(8,128)S(1)}, s32[]{:T(128)}, bf16[8,16,128,128]{3,2,1,0:T(8,128)(2,1)}, s32[]{:T(128)}, /*index=5*/s32[]{:T(128)}, s32[]{:T(128)}, s32[]{:T(128)}) while((s32[]{:T(128)}, f32[16,128,128]{2,1,0:T(8,128)S(1)}, s32[]{:T(128)}, bf16[8,16,128,128]{3,2,1,0:T(8,128)(2,1)}, s32[]{:T(128)}, ...), condition=%wide.region_5.6_spmd.clone, body=%wide.region_4.5_spmd.clone.sunk | while | flops 1048584 | bytes 2621603 | solution.py:39
  239.5 1.7 add_select_fusion.5
  244.5 76.0 %reduce-scatter.2.cloned.1.call-done = bf16[256,2048]{1,0:T(8,128)(2,1)} async-done(((bf16[2048,2048]{1,0:T(8,128)(2,1)}), bf16[256,2048]{1,0:T(8,128)(2,1)}) %reduce-scatter.2.cloned.1.call-update) | async-done | bytes 1048592 | tf_op jit(solution)/shard_map/reduce_scatter | solution.py:142
  320.6 3.4 convolution_add_fusion.1
  324.0 2.5 copy.47
  326.5 2.2 fusion.2
  329.8 2.3 fusion.16
  332.1 44.9 %all-reduce.2.cloned.1.call-done = bf16[256,2048]{1,0:T(8,128)(2,1)} async-done(((bf16[256,2048]{1,0:T(8,128)(2,1)}), bf16[256,2048]{1,0:T(8,128)(2,1)}) %all-reduce.2.cloned.1.call-update) | async-done | bytes 1048592 | tf_op jit(solution)/shard_map/psum | solution.py:150
  376.9 2.8 convert_multiply_fusion
  (65 shorter events, 38.4 us)
Async XLA Ops:
  7.2 168.8 %copy-start = (bf16[1,128,2048]{2,1,0:T(8,128)(2,1)S(1)}, bf16[1,128,2048]{2,1,0:T(8,128)(2,1)}, u32[]{:S(2)}) copy-start(bf16[1,128,2048]{2,1,0:T(8,128)(2,1)} %param.15) | copy-start | bytes 1572868
  7.2 5.6 %copy-start.8 = (bf16[1,128,2048]{2,1,0:T(8,128)(2,1)S(1)}, bf16[1,128,2048]{2,1,0:T(8,128)(2,1)}, u32[]{:S(2)}) copy-start(bf16[1,128,2048]{2,1,0:T(8,128)(2,1)} %param.10) | copy-start | bytes 1572868
  7.2 86.5 %all-gather.8.cloned.1.call-start = ((), (), s32[]{:S(2)}) async-start(), calls=%async_computation.4 | async-start | bytes 9437184 | tf_op jit(solution)/shard_map/all_gather | solution.py:17
  8.8 85.0 %copy-start.5 = (bf16[16,8,16,128]{3,2,1,0:T(8,128)(2,1)}, bf16[16,8,16,128]{3,2,1,0:T(8,128)(2,1)S(1)}, u32[]{:S(2)}) copy-start(bf16[16,8,16,128]{3,2,1,0:T(8,128)(2,1)S(1)} %copy.57) | copy-start | bytes 1572868
  9.3 3.4 copy-start.7
  10.6 97.3 %copy-start.3 = (bf16[16,8,16,128]{3,2,1,0:T(8,128)(2,1)}, bf16[16,8,16,128]{3,2,1,0:T(8,128)(2,1)S(1)}, u32[]{:S(2)}) copy-start(bf16[16,8,16,128]{3,2,1,0:T(8,128)(2,1)S(1)} %copy.58) | copy-start | bytes 1572868
  11.9 164.0 %all-gather.6.cloned.1.call-start = ((), (), s32[]{:S(2)}) async-start(), calls=%async_computation.1 | async-start | bytes 9437184 | tf_op jit(solution)/shard_map/all_gather | solution.py:61
  12.7 218.6 %all-gather.10.cloned.1.call-start = ((), (), s32[]{:S(2)}) async-start(), calls=%async_computation.5 | async-start | bytes 4718592 | tf_op jit(solution)/shard_map/all_gather | solution.py:30
  15.1 91.8 %copy-start.1 = (bf16[1,128,2048]{1,2,0:T(8,128)(2,1)}, bf16[1,128,2048]{1,2,0:T(8,128)(2,1)S(1)}, u32[]{:S(2)}) copy-start(bf16[1,128,2048]{1,2,0:T(8,128)(2,1)S(1)} %copy.56) | copy-start | bytes 1572868
  93.7 82.2 %copy-start.11 = (f32[2048]{0:T(1024)S(1)}, f32[2048]{0:T(1024)}, u32[]{:S(2)}) copy-start(f32[2048]{0:T(1024)} %param.13) | copy-start | bytes 24580
  176.0 7.0 %copy-start.2 = (bf16[1,128,2048]{1,2,0:T(8,128)(2,1)S(1)}, bf16[1,128,2048]{1,2,0:T(8,128)(2,1)}, u32[]{:S(2)}) copy-start(bf16[1,128,2048]{1,2,0:T(8,128)(2,1)} %copy-done.1) | copy-start | bytes 1572868
  185.3 135.2 %reduce-scatter.2.cloned.1.call-start = ((), (), s32[]{:S(2)}) async-start(), calls=%async_computation.2 | async-start | bytes 9437184 | tf_op jit(solution)/shard_map/reduce_scatter | solution.py:142
  190.9 186.0 %all-reduce.2.cloned.1.call-start = ((), (), s32[]{:S(2)}) async-start(), calls=%async_computation.3 | async-start | bytes 2097152 | tf_op jit(solution)/shard_map/psum | solution.py:150
  192.9 4.4 %copy-start.10 = (bf16[16,128,128]{2,1,0:T(8,128)(2,1)}, bf16[16,128,128]{2,1,0:T(8,128)(2,1)S(1)}, u32[]{:S(2)}) copy-start(bf16[16,128,128]{2,1,0:T(8,128)(2,1)S(1)} %fusion.4) | copy-start | bytes 1572868
  211.5 109.1 %copy-start.4 = (bf16[16,8,16,128]{3,2,1,0:T(8,128)(2,1)S(1)}, bf16[16,8,16,128]{3,2,1,0:T(8,128)(2,1)}, u32[]{:S(2)}) copy-start(bf16[16,8,16,128]{3,2,1,0:T(8,128)(2,1)} %copy-done.3) | copy-start | bytes 1572868
  231.2 95.3 %copy-start.6 = (bf16[16,8,16,128]{3,2,1,0:T(8,128)(2,1)S(1)}, bf16[16,8,16,128]{3,2,1,0:T(8,128)(2,1)}, u32[]{:S(2)}) copy-start(bf16[16,8,16,128]{3,2,1,0:T(8,128)(2,1)} %copy-done.5) | copy-start | bytes 1572868
  244.5 85.2 %copy-start.9 = (bf16[1,128,2048]{2,1,0:T(8,128)(2,1)S(1)}, bf16[1,128,2048]{2,1,0:T(8,128)(2,1)}, u32[]{:S(2)}) copy-start(bf16[1,128,2048]{2,1,0:T(8,128)(2,1)} %param.11) | copy-start | bytes 1572868
Sparse Core Ops, SparseCore 0:
  12.0 81.6 all-gather.7
  95.3 80.5 all-gather.5
  185.4 45.7 all-gather.9
  233.4 87.1 reduce-scatter.1
  323.4 53.4 all-reduce.1
where the time goes:
time: 389 us; the launch traced here: 386 us
  waiting for transfers between devices  285 us (73%)
  matrix products  41.1 us (11%)
  other arithmetic  36.9 us (9%)
  between operations  14 us (4%)
  local copies, waits for them, and re-layouts  8.39 us (2%)
    all_gather x1, waiting for transfers between devices, carried_in(): everything = lax.all_gather(value, axis)  77.3 us
    reduce_scatter x1, waiting for transfers between devices, on_device(): lax.psum_scatter(lax.dot_general(normed, upstream, (((0,), (0,)), ((), ()...  76 us
    all_gather x1, waiting for transfers between devices, on_device(): weight = lax.all_gather(out_weight, 'ctx', axis=0, tiled=True)  66.5 us
    psum x1, waiting for transfers between devices, on_device(): summed = lax.psum(shares, 'dp').astype(jnp.float32)  44.9 us
    all_gather x1, waiting for transfers between devices, entering(): everything = lax.all_gather(value.astype(jnp.bfloat16), axis)  19.8 us
    select_n x8, other arithmetic, entering_turn(): return jnp.where(reached, new, before)  13.1 us
    select_n x8, other arithmetic, carried_turn(): return jnp.where(reached, new, before)  13 us
  transfers between devices with their start and end apart: 5, of which 5 were waited for; matrix products, arithmetic and copies ran while one was open for 18% of the time, Pallas kernels for 0%

commit v1 on v0

--- a/solution.py
+++ b/solution.py
@@ -1,8 +1,11 @@
+import functools
 import math
 
 import jax
 import jax.numpy as jnp
 from jax import lax
+from jax.experimental import pallas as pl
+from jax.experimental.pallas import tpu as pltpu
 from jax.sharding import PartitionSpec as P
 
 HEAD = 128
@@ -53,7 +56,7 @@
     return earlier + later
 
 
-def on_device(query_rows, key_rows, value_rows, norm_gain, out_weight, cotangent):
+def on_device_general(query_rows, key_rows, value_rows, norm_gain, out_weight, cotangent):
     length = query_rows.shape[1]
     width = query_rows.shape[2]
     heads = width // HEAD
@@ -152,6 +155,383 @@
     return (mixed[None], grad_queries[None], grad_keys[None], grad_values[None], grad_weight)
 
 
+CHIPS = 4
+COLUMNS = 4
+PAIR = 2 * HEAD
+QUARTER = PAIR // COLUMNS
+VMEM_LIMIT = 40 * 1024 * 1024
+bf16 = jnp.bfloat16
+f32 = jnp.float32
+
+
+def dims(a, b, ca, cb):
+    return lax.dot_general(a, b, (((ca,), (cb,)), ((), ())), preferred_element_type=f32)
+
+
+def call(kernel, outs, name, args, flops, grid=(), in_specs=None, out_specs=None, scratch=(), aliases=None):
+    vmem = pl.BlockSpec(memory_space=pltpu.VMEM)
+    smem = pl.BlockSpec(memory_space=pltpu.SMEM)
+    if in_specs is None:
+        in_specs = [smem if a.dtype == jnp.int32 else vmem for a in args]
+    if out_specs is None:
+        out_specs = [vmem for _ in outs]
+    moved = sum(math.prod(a.shape) * a.dtype.itemsize for a in list(args) + list(outs))
+    return pl.pallas_call(
+        kernel,
+        out_shape=list(outs),
+        grid=grid,
+        in_specs=in_specs,
+        out_specs=out_specs,
+        scratch_shapes=list(scratch),
+        input_output_aliases=aliases or {},
+        compiler_params=pltpu.CompilerParams(vmem_limit_bytes=VMEM_LIMIT),
+        cost_estimate=pl.CostEstimate(flops=flops, bytes_accessed=moved, transcendentals=0),
+        name=name,
+    )(*args)
+
+
+def like(shape, dtype):
+    return jax.ShapeDtypeStruct(shape, dtype)
+
+
+def chip_of(place, s):
+    return lax.rem(place[0] + (CHIPS - s), CHIPS)
+
+
+def head_lanes(place, chip, j):
+    return pl.ds(pl.multiple_of((2 * chip + place[1]) * PAIR + j * HEAD, HEAD), HEAD)
+
+
+def rows_of(own, sib, lanes):
+    return jnp.concatenate([own[:, lanes], sib[:, lanes]], axis=0)
+
+
+def causal_mask(place, rows, transposed=False):
+    core = place[1]
+
+    def position(axis):
+        at = lax.broadcasted_iota(jnp.int32, (rows, rows), axis)
+        half = rows // 2
+        return jnp.where(at < half, at + core * half, at - core * half)
+
+    query, key = (1, 0) if transposed else (0, 1)
+    return position(key) <= position(query)
+
+
+def states_kernel(place, k_own, k_sib, v_own, v_sib, state):
+    for chip in range(CHIPS):
+        for j in range(2):
+            lanes = head_lanes(place, chip, j)
+            fk = feature(rows_of(k_own, k_sib, lanes))
+            state[2 * chip + j] = dims(fk, rows_of(v_own, v_sib, lanes), 0, 0).astype(bf16)
+
+
+def attend_kernel(place, q_own, q_sib, k_own, k_sib, v_own, v_sib, near, far, gain, attended, n0, n1, n2, n3):
+    rows = 2 * q_own.shape[0]
+    mask = causal_mask(place, rows)
+    column = place[2]
+    low = lax.broadcasted_iota(jnp.int32, (rows, HEAD), 1) < HEAD // 2
+    turned = lax.rem(column, 2) == 1
+    swapped = column >= 2
+    packs = (n0, n1, n2, n3)
+    for t in range(CHIPS // 2):
+        pieces = []
+        for s in (2 * t, 2 * t + 1):
+            chip = chip_of(place, s)
+            normed = []
+            for j in range(2):
+                lanes = head_lanes(place, chip, j)
+                fq = feature(rows_of(q_own, q_sib, lanes))
+                fk = feature(rows_of(k_own, k_sib, lanes))
+                value = rows_of(v_own, v_sib, lanes)
+                probs = jnp.where(mask, dims(fq, fk, 1, 1), 0.0).astype(bf16)
+                prefix = (near[2 * chip + j].astype(f32) + far[2 * chip + j].astype(f32)).astype(bf16)
+                out = dims(probs, value, 1, 0) + dims(fq, prefix, 1, 0)
+                attended[:, pl.ds(s * PAIR + j * HEAD, HEAD)] = out
+                inverse = lax.rsqrt(jnp.mean(out * out, axis=-1, keepdims=True) + epsilon)
+                normed.append(out * inverse * gain[:, lanes])
+            first = jnp.where(swapped, normed[1], normed[0])
+            second = jnp.where(swapped, normed[0], normed[1])
+            pieces.append([jnp.where(turned, pltpu.roll(x, HEAD // 2, 1), x) for x in (first, second)])
+        for i in range(2):
+            a, b = pieces[0][i], pieces[1][i]
+            at = pl.ds(t * HEAD, HEAD)
+            packs[2 * i][:, at] = jnp.where(low, a, pltpu.roll(b, HEAD // 2, 1)).astype(bf16)
+            packs[2 * i + 1][:, at] = jnp.where(low, pltpu.roll(a, HEAD // 2, 1), b).astype(bf16)
+
+
+def d_normed_kernel(w, *refs):
+    cots, outs = refs[: 2 * COLUMNS], refs[2 * COLUMNS :]
+    half = cots[0].shape[0]
+    weight = w[...]
+    for m in range(COLUMNS):
+        outs[m][:half] = dims(cots[2 * m][...], weight, 1, 1).astype(bf16)
+        outs[m][half:] = dims(cots[2 * m + 1][...], weight, 1, 1).astype(bf16)
+
+
+def d_attend_kernel(place, q_own, q_sib, attended, gain, r0, r1, r2, r3, d_attended, state):
+    rows = 2 * q_own.shape[0]
+    column = place[2]
+    low = lax.broadcasted_iota(jnp.int32, (rows, HEAD), 1) < HEAD // 2
+    turned = lax.rem(column, 2) == 1
+    swapped = column >= 2
+    packs = (r0, r1, r2, r3)
+    for t in range(CHIPS // 2):
+        at = pl.ds(t * HEAD, HEAD)
+        pieces = [[], []]
+        for i in range(2):
+            a, b = packs[2 * i][:, at].astype(f32), packs[2 * i + 1][:, at].astype(f32)
+            both = (
+                jnp.where(low, a, pltpu.roll(b, HEAD // 2, 1)),
+                jnp.where(low, pltpu.roll(a, HEAD // 2, 1), b),
+            )
+            for which in range(2):
+                x = both[which]
+                pieces[which].append(jnp.where(turned, pltpu.roll(x, HEAD // 2, 1), x))
+        for which in range(2):
+            s = 2 * t + which
+            chip = chip_of(place, s)
+            first, second = pieces[which]
+            by_head = (jnp.where(swapped, second, first), jnp.where(swapped, first, second))
+            for j in range(2):
+                lanes = head_lanes(place, chip, j)
+                fq = feature(rows_of(q_own, q_sib, lanes))
+                here = pl.ds(s * PAIR + j * HEAD, HEAD)
+                out = attended[:, here]
+                inverse = lax.rsqrt(jnp.mean(out * out, axis=-1, keepdims=True) + epsilon)
+                scaled = by_head[j] * gain[:, lanes]
+                share = jnp.mean(scaled * out, axis=-1, keepdims=True)
+                grad = (inverse * (scaled - out * (inverse * inverse * share))).astype(bf16)
+                d_attended[:, here] = grad
+                state[2 * chip + j] = dims(fq, grad, 0, 0).astype(bf16)
+
+
+def inner_kernel(
+    place, q_own, q_sib, k_own, k_sib, v_own, v_sib, near, far, d_attended, gq, gq_sib, part_k, part_v
+):
+    half = q_own.shape[0]
+    mask = causal_mask(place, 2 * half)
+    mask_t = causal_mask(place, 2 * half, True)
+    for s in range(CHIPS):
+        chip = chip_of(place, s)
+        for j in range(2):
+            lanes = head_lanes(place, chip, j)
+            here = pl.ds(s * PAIR + j * HEAD, HEAD)
+            query = rows_of(q_own, q_sib, lanes)
+            fq = feature(query)
+            fk = feature(rows_of(k_own, k_sib, lanes))
+            value = rows_of(v_own, v_sib, lanes)
+            grad = d_attended[:, here]
+            prefix = (near[2 * chip + j].astype(f32) + far[2 * chip + j].astype(f32)).astype(bf16)
+            d_probs = jnp.where(mask, dims(grad, value, 1, 1), 0.0).astype(bf16)
+            d_probs_t = jnp.where(mask_t, dims(value, grad, 1, 1), 0.0).astype(bf16)
+            probs_t = jnp.where(mask_t, dims(fk, fq, 1, 1), 0.0).astype(bf16)
+            d_fq = dims(d_probs, fk, 1, 0) + dims(grad, prefix, 1, 1)
+            out = (d_fq * feature_slope(query)).astype(bf16)
+            gq[:, lanes] = out[:half]
+            gq_sib[:, pl.ds(pl.multiple_of(chip * PAIR + j * HEAD, HEAD), HEAD)] = out[half:]
+            part_k[:, here] = dims(d_probs_t, fq, 1, 0)
+            part_v[:, here] = dims(probs_t, grad, 1, 0)
+
+
+def outer_kernel(place, k_own, k_sib, v_own, v_sib, near, far, part_k, part_v, gk, gv, sent):
+    half = k_own.shape[0]
+    for s in range(CHIPS):
+        chip = chip_of(place, s)
+        for j in range(2):
+            lanes = head_lanes(place, chip, j)
+            here = pl.ds(s * PAIR + j * HEAD, HEAD)
+            there = pl.ds(pl.multiple_of(chip * PAIR + j * HEAD, HEAD), HEAD)
+            key = rows_of(k_own, k_sib, lanes)
+            value = rows_of(v_own, v_sib, lanes)
+            suffix = (near[2 * chip + j].astype(f32) + far[2 * chip + j].astype(f32)).astype(bf16)
+            d_fk = part_k[:, here] + dims(value, suffix, 1, 1)
+            out_k = (d_fk * feature_slope(key)).astype(bf16)
+            out_v = (part_v[:, here] + dims(feature(key), suffix, 1, 0)).astype(bf16)
+            gk[:, lanes] = out_k[:half]
+            gv[:, lanes] = out_v[:half]
+            sent[0, :, there] = out_k[half:]
+            sent[1, :, there] = out_v[half:]
+
+
+def fill_kernel(place, *refs):
+    n = (len(refs) + 1) // 3
+    got, held, outs = refs[:n], refs[n : 2 * n], refs[2 * n :]
+    for chip in range(CHIPS):
+        pair = pl.ds(chip * PAIR, PAIR)
+        own = pl.ds(pl.multiple_of((2 * chip + place[1]) * PAIR, PAIR), PAIR)
+        other = pl.ds(pl.multiple_of((2 * chip + 1 - place[1]) * PAIR, PAIR), PAIR)
+        for a, b, o in zip(got, held, outs):
+            o[:, own] = b[:, own]
+            o[:, other] = a[:, pair]
+
+
+def mixed_kernel(n0, n1, n2, n3, nx, w_own, w_sib, m0, m1, m2, m3):
+    half = nx.shape[1]
+    for m, (n, out) in enumerate(zip((n0, n1, n2, n3), (m0, m1, m2, m3))):
+        out[...] = (dims(n[:half, :], w_own[...], 1, 0) + dims(nx[m], w_sib[...], 1, 0)).astype(out.dtype)
+
+
+def weight_kernel(*refs):
+    packs, cots, outs = refs[:COLUMNS], refs[COLUMNS : 3 * COLUMNS], refs[3 * COLUMNS :]
+    half = cots[0].shape[0]
+    total = None
+    for m in range(COLUMNS):
+        for part in range(2):
+            term = dims(packs[m][pl.ds(part * half, half), :], cots[2 * m + part][...], 0, 0)
+            total = term if total is None else total + term
+    for s in range(CHIPS):
+        outs[s][...] = total[s * QUARTER : (s + 1) * QUARTER].astype(outs[s].dtype)
+
+
+def gathered_kernel(scale, place, t0, t1, t2, t3, out):
+    for m, t in enumerate((t0, t1, t2, t3)):
+        column = lax.bitwise_xor(place[2], m)
+        out[pl.ds(pl.multiple_of(column * QUARTER, QUARTER), QUARTER), :] = t[...].astype(f32) * scale
+
+
+def on_device_planned(query_rows, key_rows, value_rows, norm_gain, out_weight, cotangent):
+    query, key, value, cot = query_rows[0], key_rows[0], value_rows[0], cotangent[0]
+    half, width = query.shape
+    here, column = lax.axis_index("ctx"), lax.axis_index("dp")
+    place = jnp.stack([here // 2, here % 2, column]).astype(jnp.int32)
+    gain = norm_gain.reshape(1, width)
+
+    def to_sib(x):
+        return lax.ppermute(x, "ctx", [(i, i ^ 1) for i in range(2 * CHIPS)])
+
+    def around(x, s):
+        pairs = [(2 * c + e, 2 * ((c + s) % CHIPS) + e) for c in range(CHIPS) for e in range(2)]
+        return lax.ppermute(x, "ctx", pairs)
+
+    def along(x, s):
+        pairs = [(2 * c + e, 2 * (c + s) + e) for c in range(CHIPS) for e in range(2) if 0 <= c + s < CHIPS]
+        return lax.ppermute(x, "ctx", pairs)
+
+    def across(x, m):
+        return x if m == 0 else lax.ppermute(x, "dp", [(d, d ^ m) for d in range(COLUMNS)])
+
+    key_sib, value_sib, query_sib = to_sib(key), to_sib(value), to_sib(query)
+    heads = 2 * CHIPS
+    state_shape = like((heads, HEAD, HEAD), bf16)
+    state_flops = 2 * heads * 2 * half * HEAD * HEAD
+
+    state = call(states_kernel, [state_shape], "states", (place, key, key_sib, value, value_sib), state_flops)[0]
+    near = along(state, 1)
+    far = along(state + near, 2)
+
+    quarter = lax.dynamic_slice(out_weight, (column * QUARTER, 0), (QUARTER, width))
+    weight = jnp.concatenate([quarter] + [around(quarter, s) for s in range(1, CHIPS)], axis=0)
+    weight_sib = to_sib(weight)
+    cots = [across(cot, m) for m in range(COLUMNS)]
+    cot_parts = [x for c in cots for x in (c, to_sib(c))]
+
+    pack = like((2 * half, PAIR), bf16)
+    attended, *packs = call(
+        attend_kernel,
+        [like((2 * half, heads * HEAD), f32)] + [pack] * COLUMNS,
+        "attend",
+        (place, query, query_sib, key, key_sib, value, value_sib, near, far, gain),
+        8 * state_flops,
+    )
+    d_packs = call(
+        d_normed_kernel, [pack] * COLUMNS, "d_normed", (weight, *cot_parts), 2 * 8 * half * PAIR * width
+    )
+    d_got = [across(d_packs[m], m) for m in range(COLUMNS)]
+    n_got = [across(packs[m], m) for m in range(COLUMNS)]
+
+    d_attended, d_state = call(
+        d_attend_kernel,
+        [like((2 * half, heads * HEAD), bf16), state_shape],
+        "d_attend",
+        (place, query, query_sib, attended, gain, *d_got),
+        2 * state_flops,
+    )
+    d_near = along(d_state, -1)
+    d_far = along(d_state + d_near, -2)
+
+    term = like((QUARTER, width), bf16)
+    column_spec = lambda rows, step: pl.BlockSpec((rows, step), lambda i: (0, i))
+    fixed = lambda shape: pl.BlockSpec(shape, lambda i: (0,) * len(shape))
+    step = 512
+    terms = call(
+        weight_kernel,
+        [like((QUARTER, width), f32)] + [term] * (CHIPS - 1),
+        "weight_terms",
+        (*n_got, *cot_parts),
+        2 * 8 * half * PAIR * width,
+        grid=(width // step,),
+        in_specs=[fixed((2 * half, PAIR))] * COLUMNS + [column_spec(half, step)] * (2 * COLUMNS),
+        out_specs=[column_spec(QUARTER, step)] * CHIPS,
+    )
+    arrived = [around(terms[s], -s) for s in range(1, CHIPS)]
+    share = terms[0]
+    for x in arrived:
+        share = share + x.astype(f32)
+    share = share.astype(bf16)
+    devices = lax.axis_size("dp") * lax.axis_size("ctx")
+    scale = 1.0 / math.sqrt(devices * half)
+
+    n_sib = to_sib(jnp.stack([n[half:] for n in n_got]))
+    outs = call(
+        mixed_kernel,
+        [like((half, width), f32)] + [like((half, width), bf16)] * (COLUMNS - 1),
+        "mixed_terms",
+        (*n_got, n_sib, weight, weight_sib),
+        2 * 4 * half * 2 * PAIR * width,
+        grid=(width // step,),
+        in_specs=[fixed((2 * half, PAIR))] * COLUMNS
+        + [fixed((COLUMNS, half, PAIR))]
+        + [column_spec(PAIR, step)] * 2,
+        out_specs=[column_spec(half, step)] * COLUMNS,
+    )
+    mixed = outs[0]
+    for m in range(1, COLUMNS):
+        mixed = mixed + across(outs[m], m).astype(f32)
+    mixed = mixed.astype(bf16)
+
+    full = like((half, width), bf16)
+    gq, gq_sent, part_k, part_v = call(
+        inner_kernel,
+        [full, like((half, width // 2), bf16)] + [like((2 * half, heads * HEAD), f32)] * 2,
+        "inner",
+        (place, query, query_sib, key, key_sib, value, value_sib, near, far, d_attended),
+        14 * state_flops,
+    )
+    gk, gv, kv_sent = call(
+        outer_kernel,
+        [full, full, like((2, half, width // 2), bf16)],
+        "outer",
+        (place, key, key_sib, value, value_sib, d_near, d_far, part_k, part_v),
+        2 * state_flops,
+    )
+    gq_got, kv_got = to_sib(gq_sent), to_sib(kv_sent)
+    grad_queries, = call(fill_kernel, [full], "fill_q", (place, gq_got, gq), 0)
+    grad_keys, grad_values = call(fill_kernel, [full] * 2, "fill_kv", (place, kv_got[0], kv_got[1], gk, gv), 0)
+
+    shares = [across(share, m) for m in range(COLUMNS)]
+    grad_weight, = call(
+        functools.partial(gathered_kernel, scale),
+        [like(out_weight.shape, f32)],
+        "grad_weight",
+        (place, *shares),
+        0,
+    )
+    return (mixed[None], grad_queries[None], grad_keys[None], grad_values[None], grad_weight)
+
+
+def on_device(query_rows, key_rows, value_rows, norm_gain, out_weight, cotangent):
+    fits = (
+        lax.axis_size("dp") == COLUMNS
+        and lax.axis_size("ctx") == 2 * CHIPS
+        and out_weight.shape[0] == PAIR
+        and out_weight.shape[1] == 2 * CHIPS * PAIR
+        and query_rows.shape[1] == HEAD
+    )
+    path = on_device_planned if fits else on_device_general
+    return path(query_rows, key_rows, value_rows, norm_gain, out_weight, cotangent)
+
+
 def solution(mesh):
     return jax.shard_map(
         on_device,

time: 389 us -> 145 us (0.37)
  waiting for transfers between devices: 285 us -> 63.8 us
  starting transfers between devices: 0.38 us -> 47.1 us
  matrix products: 41.1 us -> 0 us
  other arithmetic: 36.9 us -> 2.5 us
  Pallas kernels: 0 us -> 25.2 us
  between operations: 14 us -> 0.95 us
  local copies, waits for them, and re-layouts: 8.39 us -> 2.84 us
    all_gather x3 -> x0, waiting for transfers between devices: 164 us -> none  [the longest x1 77.3 us: carried_in(): everything = lax.all_gather(value, axis)]
    reduce_scatter x1 -> x0, waiting for transfers between devices: 76 us -> none  [on_device(): lax.psum_scatter(lax.dot_general(normed, upstream, (((0,), (0,)), ((), ()...]
    ppermute x0 -> x36, waiting for transfers between devices: none -> 63.8 us  [the longest x6 29.4 us: around(): return lax.ppermute(x, 'ctx', pairs)]
    ppermute x0 -> x36, starting transfers between devices: none -> 47.1 us  [the longest x15 20 us: across(): lax.ppermute(x, 'dp', [(d, d ^ m) for d in range(COLUMNS)])]
    psum x1 -> x0, waiting for transfers between devices: 44.9 us -> none  [on_device(): summed = lax.psum(shares, 'dp').astype(jnp.float32)]
    dot_general x15 -> x0, matrix products: 41.1 us -> none  [the longest x1 5.81 us: on_device(): lax.dot_general(upstream, weight, (((1,), (1,)), ((), ())), preferred_ele...]
    select_n x16 -> x0, other arithmetic: 26.1 us -> none  [the longest x8 13.1 us: entering_turn(): return jnp.where(reached, new, before)]
    pallas_call x0 -> x11, Pallas kernels: none -> 25.2 us  [call(): pl.pallas_call(kernel, out_shape=list(outs), grid=grid, in_specs=in_specs...]
  transfers between devices with their start and end apart: 5 -> 36, of which waited for: 5 -> 14; matrix products, arithmetic and copies ran while one was open for 18% -> 2% of each run, Pallas kernels for 0% -> 17%
where the time goes in v1:
time: 145 us; the launch traced here: 142 us
  waiting for transfers between devices  63.8 us (44%)
  starting transfers between devices  47.1 us (32%)
  Pallas kernels  25.2 us (17%)
  local copies, waits for them, and re-layouts  2.84 us (2%)
  other arithmetic  2.5 us (2%)
    ppermute x6, waiting for transfers between devices, around(): return lax.ppermute(x, 'ctx', pairs)  29.4 us
    pallas_call x11, Pallas kernels, call(): pl.pallas_call(kernel, out_shape=list(outs), grid=grid, in_specs=in_specs...  25.2 us
    ppermute x15, waiting for transfers between devices, across(): lax.ppermute(x, 'dp', [(d, d ^ m) for d in range(COLUMNS)])  20.1 us
    ppermute x15, starting transfers between devices, across(): lax.ppermute(x, 'dp', [(d, d ^ m) for d in range(COLUMNS)])  20 us
    ppermute x4, waiting for transfers between devices, along(): return lax.ppermute(x, 'ctx', pairs)  14.4 us
    ppermute x4, starting transfers between devices, along(): return lax.ppermute(x, 'ctx', pairs)  14.1 us
    ppermute x6, starting transfers between devices, around(): return lax.ppermute(x, 'ctx', pairs)  11.6 us
  transfers between devices with their start and end apart: 36, of which 14 were waited for; matrix products, arithmetic and copies ran while one was open for 2% of the time, Pallas kernels for 17%

profile of v1, /device:TPU:16, one launch (start us, length us, event | category | flops | bytes accessed | tf_op | source)
XLA Modules:
  0.0 142.4 jit_solution(15128356165310119628)
XLA Ops:
  2.4 3.5 %collective-permute-start.10 = (bf16[64,2048]{1,0:T(8,128)(2,1)S(1)}, bf16[64,2048]{1,0:T(8,128)(2,1)S(1)}, u32[]{:S(2)}, u32[]{:S(2)}) collective-permute-start(bf16[64,2048]{1,0:T(8,128)(2,1)S(1)} %constant_dynamic-slice_fusion), channel_id=1, source_target_pairs={{0,4},{1,5},{2,6},{3,7},{4,0},{5,1},{6,2},{7,3},{8,12},{9,13},{10,... | collective-permute-start | bytes 786440 | tf_op jit(solution)/shard_map/ppermute | solution.py:405
  7.4 3.8 %collective-permute-done.11 = bf16[64,2048]{1,0:T(8,128)(2,1)S(1)} collective-permute-done((bf16[64,2048]{1,0:T(8,128)(2,1)S(1)}, bf16[64,2048]{1,0:T(8,128)(2,1)S(1)}, u32[]{:S(2)}, u32[]{:S(2)}) %collective-permute-start.11) | collective-permute-done | bytes 262176 | tf_op jit(solution)/shard_map/ppermute | solution.py:405
  12.7 6.5 %collective-permute-done.10 = bf16[64,2048]{1,0:T(8,128)(2,1)S(1)} collective-permute-done((bf16[64,2048]{1,0:T(8,128)(2,1)S(1)}, bf16[64,2048]{1,0:T(8,128)(2,1)S(1)}, u32[]{:S(2)}, u32[]{:S(2)}) %collective-permute-start.10) | collective-permute-done | bytes 262176 | tf_op jit(solution)/shard_map/ppermute | solution.py:405
  19.2 2.4 %collective-permute-start.21 = (bf16[128,2048]{1,0:T(8,128)(2,1)}, bf16[128,2048]{1,0:T(8,128)(2,1)}, u32[]{:S(2)}, u32[]{:S(2)}) collective-permute-start(bf16[128,2048]{1,0:T(8,128)(2,1)} %bitcast.41), channel_id=1, source_target_pairs={{0,24},{8,16},{16,8},{24,0},{1,25},{9,17},{17,9},{25,1},{2,26},{10... | collective-permute-start | bytes 1572872 | tf_op jit(solution)/shard_map/ppermute | solution.py:412
  21.6 4.7 %collective-permute-start.9 = (bf16[64,2048]{1,0:T(8,128)(2,1)S(1)}, bf16[64,2048]{1,0:T(8,128)(2,1)}, u32[]{:S(2)}, u32[]{:S(2)}) collective-permute-start(bf16[64,2048]{1,0:T(8,128)(2,1)S(1)} %constant_dynamic-slice_fusion), channel_id=1, source_target_pairs={{0,2},{1,3},{2,4},{3,5},{4,6},{5,7},{6,0},{7,1},{8,10},{9,11},{10,... | collective-permute-start | bytes 786440 | tf_op jit(solution)/shard_map/ppermute | solution.py:405
  31.1 4.5 %collective-permute-start.3 = (bf16[8,128,128]{2,1,0:T(8,128)(2,1)S(1)}, bf16[8,128,128]{2,1,0:T(8,128)(2,1)S(1)}, u32[]{:S(2)}, u32[]{:S(2)}) collective-permute-start(bf16[8,128,128]{2,1,0:T(8,128)(2,1)S(1)} %states.1), channel_id=1, source_target_pairs={{0,2},{1,3},{2,4},{3,5},{4,6},{5,7},{8,10},{9,11},{10,12},{11,13},... | collective-permute-start | bytes 786440 | tf_op jit(solution)/shard_map/ppermute | solution.py:409
  36.2 4.0 %collective-permute-done.3.near = bf16[8,128,128]{2,1,0:T(8,128)(2,1)S(1)} collective-permute-done((bf16[8,128,128]{2,1,0:T(8,128)(2,1)S(1)}, bf16[8,128,128]{2,1,0:T(8,128)(2,1)S(1)}, u32[]{:S(2)}, u32[]{:S(2)}) %collective-permute-start.3) | collective-permute-done | bytes 262176 | tf_op jit(solution)/shard_map/ppermute | solution.py:409
  42.7 9.2 %collective-permute-done.4.far = bf16[8,128,128]{2,1,0:T(8,128)(2,1)S(1)} collective-permute-done((bf16[8,128,128]{2,1,0:T(8,128)(2,1)S(1)}, bf16[8,128,128]{2,1,0:T(8,128)(2,1)S(1)}, u32[]{:S(2)}, u32[]{:S(2)}) %collective-permute-start.4) | collective-permute-done | bytes 262176 | tf_op jit(solution)/shard_map/ppermute | solution.py:409
  52.0 2.4 %attend.1 = (f32[256,1024]{1,0:T(8,128)S(1)}, bf16[256,256]{1,0:T(8,128)(2,1)S(1)}, bf16[256,256]{1,0:T(8,128)(2,1)S(1)}, bf16[256,256]{1,0:T(8,128)(2,1)S(1)}, bf16[256,256]{1,0:T(8,128)(2,1)S(1)}) custom-call(s32[3]{0:T(128)S(1)} %pad_add_fusion.place, bf16[128,2048]{1,0:T(8,128)(2,1)S(1)} %bitcast.36, bf16[128,2048]{1,0:T(8,128)(2,1)S(1)} %collective-permute-done.q_sib, ...), custom_call_target="tpu_custom_call" | custom-call | flops 536870912 | bytes 5251084 | tf_op jit(solution)/shard_map/attend/pallas_call | solution.py:179
  55.7 2.3 %collective-permute-start.7 = (bf16[256,256]{1,0:T(8,128)(2,1)S(1)}, bf16[256,256]{1,0:T(8,128)(2,1)S(1)}, u32[]{:S(2)}, u32[]{:S(2)}) collective-permute-start(bf16[256,256]{1,0:T(8,128)(2,1)S(1)} %get-tuple-element.36), channel_id=1, source_target_pairs={{0,24},{8,16},{16,8},{24,0},{1,25},{9,17},{17,9},{25,1},{2,26},{10... | collective-permute-start | bytes 393224 | tf_op jit(solution)/shard_map/ppermute | solution.py:412
  58.0 4.0 %d_normed.1 = (bf16[256,256]{1,0:T(8,128)(2,1)S(1)}, bf16[256,256]{1,0:T(8,128)(2,1)S(1)}, bf16[256,256]{1,0:T(8,128)(2,1)S(1)}, bf16[256,256]{1,0:T(8,128)(2,1)S(1)}) custom-call(bf16[256,2048]{1,0:T(8,128)(2,1)S(1)} %pad_maximum_fusion.w_own.w, bf16[128,2048]{1,0:T(8,128)(2,1)S(1)} %bitcast.43, ...), custom_call_target="tpu_custom_call" | custom-call | flops 1073741824 | bytes 5767168 | tf_op jit(solution)/shard_map/d_normed/pallas_call | solution.py:179
  65.8 1.6 %collective-permute-done.23.r1 = bf16[256,256]{1,0:T(8,128)(2,1)S(1)} collective-permute-done((bf16[256,256]{1,0:T(8,128)(2,1)S(1)}, bf16[256,256]{1,0:T(8,128)(2,1)S(1)}, u32[]{:S(2)}, u32[]{:S(2)}) %collective-permute-start.23) | collective-permute-done | bytes 131104 | tf_op jit(solution)/shard_map/ppermute | solution.py:412
  67.4 3.7 %collective-permute-done.24.r2 = bf16[256,256]{1,0:T(8,128)(2,1)S(1)} collective-permute-done((bf16[256,256]{1,0:T(8,128)(2,1)S(1)}, bf16[256,256]{1,0:T(8,128)(2,1)S(1)}, u32[]{:S(2)}, u32[]{:S(2)}) %collective-permute-start.24) | collective-permute-done | bytes 131104 | tf_op jit(solution)/shard_map/ppermute | solution.py:412
  71.1 2.1 %d_attend.1 = (bf16[256,1024]{1,0:T(8,128)(2,1)S(1)}, bf16[8,128,128]{2,1,0:T(8,128)(2,1)S(1)}) custom-call(s32[3]{0:T(128)S(1)} %pad_add_fusion.place, bf16[128,2048]{1,0:T(8,128)(2,1)S(1)} %bitcast.37, bf16[128,2048]{1,0:T(8,128)(2,1)S(1)} %collective-permute-done.q_sib, f32[256,1024]{1,0:T(8,128)S(1)} %get-tuple-element.41.attended, ...), custom_call_target="tpu_custom_call" | custom-call | flops 134217728 | bytes 3416076 | tf_op jit(solution)/shard_map/d_attend/pallas_call | solution.py:179
  73.2 7.1 %collective-permute-start.27 = (bf16[8,128,128]{2,1,0:T(8,128)(2,1)S(1)}, bf16[8,128,128]{2,1,0:T(8,128)(2,1)S(1)}, u32[]{:S(2)}, u32[]{:S(2)}) collective-permute-start(bf16[8,128,128]{2,1,0:T(8,128)(2,1)S(1)} %get-tuple-element.49), channel_id=1, source_target_pairs={{2,0},{3,1},{4,2},{5,3},{6,4},{7,5},{10,8},{11,9},{12,10},{13,11},... | collective-permute-start | bytes 786440 | tf_op jit(solution)/shard_map/ppermute | solution.py:409
  80.3 4.5 %weight_terms.1 = (f32[64,2048]{1,0:T(8,128)S(1)}, bf16[64,2048]{1,0:T(8,128)(2,1)S(1)}, bf16[64,2048]{1,0:T(8,128)(2,1)S(1)}, bf16[64,2048]{1,0:T(8,128)(2,1)S(1)}) custom-call(bf16[256,256]{1,0:T(8,128)(2,1)S(1)} %get-tuple-element.33.n0.refs_0_, bf16[256,256]{1,0:T(8,128)(2,1)S(1)} %collective-permute-done.5.n1.refs_1_, ...), custom_call_target="tpu_custom_call" | custom-call | flops 1073741824 | bytes 6029312 | tf_op jit(solution)/shard_map/weight_terms/pallas_call | solution.py:179
  87.6 2.7 %inner.1 = (bf16[128,2048]{1,0:T(8,128)(2,1)S(1)}, bf16[128,1024]{1,0:T(8,128)(2,1)S(1)}, f32[256,1024]{1,0:T(8,128)S(1)}, f32[256,1024]{1,0:T(8,128)S(1)}) custom-call(s32[3]{0:T(128)S(1)} %pad_add_fusion.place, bf16[128,2048]{1,0:T(8,128)(2,1)S(1)} %bitcast.38, bf16[128,2048]{1,0:T(8,128)(2,1)S(1)} %collective-permute-done.q_sib, ...), custom_call_target="tpu_custom_call" | custom-call | flops 939524096 | bytes 7077900 | tf_op jit(solution)/shard_map/inner/pallas_call | solution.py:179
  90.4 2.1 %mixed_terms.1 = (f32[128,2048]{1,0:T(8,128)S(1)}, bf16[128,2048]{1,0:T(8,128)(2,1)S(1)}, bf16[128,2048]{1,0:T(8,128)(2,1)S(1)}, bf16[128,2048]{1,0:T(8,128)(2,1)S(1)}) custom-call(bf16[256,256]{1,0:T(8,128)(2,1)S(1)} %get-tuple-element.33.n0.refs_0_, bf16[256,256]{1,0:T(8,128)(2,1)S(1)} %collective-permute-done.5.n1.refs_1_, ...), custom_call_target="tpu_custom_call" | custom-call | flops 1073741824 | bytes 5505024 | tf_op jit(solution)/shard_map/mixed_terms/pallas_call | solution.py:179
  94.2 10.5 %collective-permute-done.32 = bf16[64,2048]{1,0:T(8,128)(2,1)S(1)} collective-permute-done((bf16[64,2048]{1,0:T(8,128)(2,1)S(1)}, bf16[64,2048]{1,0:T(8,128)(2,1)S(1)}, u32[]{:S(2)}, u32[]{:S(2)}) %collective-permute-start.32) | collective-permute-done | bytes 262176 | tf_op jit(solution)/shard_map/ppermute | solution.py:405
  106.0 7.1 %collective-permute-done.30 = bf16[64,2048]{1,0:T(8,128)(2,1)S(1)} collective-permute-done((bf16[64,2048]{1,0:T(8,128)(2,1)S(1)}, bf16[64,2048]{1,0:T(8,128)(2,1)S(1)}, u32[]{:S(2)}, u32[]{:S(2)}) %collective-permute-start.30) | collective-permute-done | bytes 262176 | tf_op jit(solution)/shard_map/ppermute | solution.py:405
  119.4 3.2 %collective-permute-done.33.t1 = bf16[64,2048]{1,0:T(8,128)(2,1)S(1)} collective-permute-done((bf16[64,2048]{1,0:T(8,128)(2,1)S(1)}, bf16[64,2048]{1,0:T(8,128)(2,1)S(1)}, u32[]{:S(2)}, u32[]{:S(2)}) %collective-permute-start.33) | collective-permute-done | bytes 262176 | tf_op jit(solution)/shard_map/ppermute | solution.py:412
  126.7 9.3 %collective-permute-done.34.t2 = bf16[64,2048]{1,0:T(8,128)(2,1)S(1)} collective-permute-done((bf16[64,2048]{1,0:T(8,128)(2,1)S(1)}, bf16[64,2048]{1,0:T(8,128)(2,1)S(1)}, u32[]{:S(2)}, u32[]{:S(2)}) %collective-permute-start.34) | collective-permute-done | bytes 262176 | tf_op jit(solution)/shard_map/ppermute | solution.py:412
  137.6 2.0 %grad_weight.1 = f32[256,2048]{1,0:T(8,128)} custom-call(s32[3]{0:T(128)S(1)} %pad_add_fusion.place, bf16[64,2048]{1,0:T(8,128)(2,1)S(1)} %add_convert_fusion.1.t0, bf16[64,2048]{1,0:T(8,128)(2,1)S(1)} %collective-permute-done.33.t1, bf16[64,2048]{1,0:T(8,128)(2,1)S(1)} %collective-permute-done.34.t2, bf16[64,2048]{1,0:T(8,128)(2,1)S(1)} %collective-permute-done.35.t3), custom_call_target="tpu_custom_call" | custom-call | bytes 3145740 | tf_op jit(solution)/shard_map/grad_weight/pallas_call | solution.py:179
  140.7 1.6 %fill_kv.1 = (bf16[128,2048]{1,0:T(8,128)(2,1)}, bf16[128,2048]{1,0:T(8,128)(2,1)}) custom-call(s32[3]{0:T(128)S(1)} %pad_add_fusion.place, bf16[128,1024]{1,0:T(8,128)(2,1)S(1)} %get-tuple-element.62.refs_0_, bf16[128,1024]{1,0:T(8,128)(2,1)S(1)} %get-tuple-element.61.refs_1_, bf16[128,2048]{1,0:T(8,128)(2,1)S(1)} %get-tuple-element.53.refs_2_, ...), custom_call_target="tpu_custom_call" | custom-call | bytes 2621452 | tf_op jit(solution)/shard_map/fill_kv/pallas_call | solution.py:179
  (96 shorter events, 36.5 us)
Async XLA Ops:
  0.7 21.0 %collective-permute-start.1 = (bf16[128,2048]{1,0:T(8,128)(2,1)}, bf16[128,2048]{1,0:T(8,128)(2,1)S(1)}, u32[]{:S(2)}, u32[]{:S(2)}) collective-permute-start(bf16[128,2048]{1,0:T(8,128)(2,1)} %bitcast.25), channel_id=1, source_target_pairs={{0,1},{1,0},{2,3},{3,2},{4,5},{5,4},{6,7},{7,6},{8,9},{9,8},{10,11... | collective-permute-start | bytes 1572872 | tf_op jit(solution)/shard_map/ppermute | solution.py:401
  0.7 25.6 %collective-permute-start.2 = (bf16[128,2048]{1,0:T(8,128)(2,1)}, bf16[128,2048]{1,0:T(8,128)(2,1)S(1)}, u32[]{:S(2)}, u32[]{:S(2)}) collective-permute-start(bf16[128,2048]{1,0:T(8,128)(2,1)} %bitcast.30), channel_id=1, source_target_pairs={{0,1},{1,0},{2,3},{3,2},{4,5},{5,4},{6,7},{7,6},{8,9},{9,8},{10,11... | collective-permute-start | bytes 1572872 | tf_op jit(solution)/shard_map/ppermute | solution.py:401
  2.4 16.8 %collective-permute-start.10 = (bf16[64,2048]{1,0:T(8,128)(2,1)S(1)}, bf16[64,2048]{1,0:T(8,128)(2,1)S(1)}, u32[]{:S(2)}, u32[]{:S(2)}) collective-permute-start(bf16[64,2048]{1,0:T(8,128)(2,1)S(1)} %constant_dynamic-slice_fusion), channel_id=1, source_target_pairs={{0,4},{1,5},{2,6},{3,7},{4,0},{5,1},{6,2},{7,3},{8,12},{9,13},{10,... | collective-permute-start | bytes 786440 | tf_op jit(solution)/shard_map/ppermute | solution.py:405
  5.9 29.7 %collective-permute-start.17 = (bf16[128,2048]{1,0:T(8,128)(2,1)}, bf16[128,2048]{1,0:T(8,128)(2,1)S(1)}, u32[]{:S(2)}, u32[]{:S(2)}) collective-permute-start(bf16[128,2048]{1,0:T(8,128)(2,1)} %bitcast.39), channel_id=1, source_target_pairs={{0,8},{8,0},{16,24},{24,16},{1,9},{9,1},{17,25},{25,17},{2,10},{10... | collective-permute-start | bytes 1572872 | tf_op jit(solution)/shard_map/ppermute | solution.py:412
  11.1 24.5 %collective-permute-start.19 = (bf16[128,2048]{1,0:T(8,128)(2,1)}, bf16[128,2048]{1,0:T(8,128)(2,1)}, u32[]{:S(2)}, u32[]{:S(2)}) collective-permute-start(bf16[128,2048]{1,0:T(8,128)(2,1)} %bitcast.40), channel_id=1, source_target_pairs={{0,16},{8,24},{16,0},{24,8},{1,17},{9,25},{17,1},{25,9},{2,18},{10... | collective-permute-start | bytes 1572872 | tf_op jit(solution)/shard_map/ppermute | solution.py:412
  19.2 17.0 %collective-permute-start.21 = (bf16[128,2048]{1,0:T(8,128)(2,1)}, bf16[128,2048]{1,0:T(8,128)(2,1)}, u32[]{:S(2)}, u32[]{:S(2)}) collective-permute-start(bf16[128,2048]{1,0:T(8,128)(2,1)} %bitcast.41), channel_id=1, source_target_pairs={{0,24},{8,16},{16,8},{24,0},{1,25},{9,17},{17,9},{25,1},{2,26},{10... | collective-permute-start | bytes 1572872 | tf_op jit(solution)/shard_map/ppermute | solution.py:412
  26.4 14.0 %collective-permute-start = (bf16[128,2048]{1,0:T(8,128)(2,1)}, bf16[128,2048]{1,0:T(8,128)(2,1)S(1)}, u32[]{:S(2)}, u32[]{:S(2)}) collective-permute-start(bf16[128,2048]{1,0:T(8,128)(2,1)} %bitcast.35), channel_id=1, source_target_pairs={{0,1},{1,0},{2,3},{3,2},{4,5},{5,4},{6,7},{7,6},{8,9},{9,8},{10,11... | collective-permute-start | bytes 1572872 | tf_op jit(solution)/shard_map/ppermute | solution.py:401
  35.6 18.8 %collective-permute-start.16 = (bf16[128,2048]{1,0:T(8,128)(2,1)S(1)}, bf16[128,2048]{1,0:T(8,128)(2,1)S(1)}, u32[]{:S(2)}, u32[]{:S(2)}) collective-permute-start(bf16[128,2048]{1,0:T(8,128)(2,1)S(1)} %bitcast.42), channel_id=1, source_target_pairs={{0,1},{1,0},{2,3},{3,2},{4,5},{5,4},{6,7},{7,6},{8,9},{9,8},{10,11... | collective-permute-start | bytes 1572872 | tf_op jit(solution)/shard_map/ppermute | solution.py:401
  35.7 19.3 %collective-permute-start.18 = (bf16[128,2048]{1,0:T(8,128)(2,1)S(1)}, bf16[128,2048]{1,0:T(8,128)(2,1)S(1)}, u32[]{:S(2)}, u32[]{:S(2)}) collective-permute-start(bf16[128,2048]{1,0:T(8,128)(2,1)S(1)} %collective-permute-done.17.refs_2_.refs_6_), channel_id=1, source_target_pairs={{0,1},{1,0},{2,3},{3,2},{4,5},{5,4},{6,7},{7,6},{8,9},{9,8},{10,11... | collective-permute-start | bytes 1572872 | tf_op jit(solution)/shard_map/ppermute | solution.py:401
  36.2 19.5 %collective-permute-start.20 = (bf16[128,2048]{1,0:T(8,128)(2,1)}, bf16[128,2048]{1,0:T(8,128)(2,1)S(1)}, u32[]{:S(2)}, u32[]{:S(2)}) collective-permute-start(bf16[128,2048]{1,0:T(8,128)(2,1)} %collective-permute-done.19.refs_4_.refs_8_), channel_id=1, source_target_pairs={{0,1},{1,0},{2,3},{3,2},{4,5},{5,4},{6,7},{7,6},{8,9},{9,8},{10,11... | collective-permute-start | bytes 1572872 | tf_op jit(solution)/shard_map/ppermute | solution.py:401
  40.3 17.7 %collective-permute-start.22 = (bf16[128,2048]{1,0:T(8,128)(2,1)}, bf16[128,2048]{1,0:T(8,128)(2,1)S(1)}, u32[]{:S(2)}, u32[]{:S(2)}) collective-permute-start(bf16[128,2048]{1,0:T(8,128)(2,1)} %collective-permute-done.21.refs_6_.refs_10_), channel_id=1, source_target_pairs={{0,1},{1,0},{2,3},{3,2},{4,5},{5,4},{6,7},{7,6},{8,9},{9,8},{10,11... | collective-permute-start | bytes 1572872 | tf_op jit(solution)/shard_map/ppermute | solution.py:401
  52.0 34.3 %collective-permute-start.12 = (bf16[256,2048]{1,0:T(8,128)(2,1)S(1)}, bf16[256,2048]{1,0:T(8,128)(2,1)S(1)}, u32[]{:S(2)}, u32[]{:S(2)}) collective-permute-start(bf16[256,2048]{1,0:T(8,128)(2,1)S(1)} %pad_maximum_fusion.w_own.w), channel_id=1, source_target_pairs={{0,1},{1,0},{2,3},{3,2},{4,5},{5,4},{6,7},{7,6},{8,9},{9,8},{10,11... | collective-permute-start | bytes 3145736 | tf_op jit(solution)/shard_map/ppermute | solution.py:401
  65.7 24.6 %collective-permute-start.8 = (bf16[4,128,256]{2,1,0:T(8,128)(2,1)S(1)}, bf16[4,128,256]{2,1,0:T(8,128)(2,1)S(1)}, u32[]{:S(2)}, u32[]{:S(2)}) collective-permute-start(bf16[4,128,256]{2,1,0:T(8,128)(2,1)S(1)} %pad_maximum_fusion.1), channel_id=1, source_target_pairs={{0,1},{1,0},{2,3},{3,2},{4,5},{5,4},{6,7},{7,6},{8,9},{9,8},{10,11... | collective-permute-start | bytes 786440 | tf_op jit(solution)/shard_map/ppermute | solution.py:401
  73.2 19.3 %collective-permute-start.27 = (bf16[8,128,128]{2,1,0:T(8,128)(2,1)S(1)}, bf16[8,128,128]{2,1,0:T(8,128)(2,1)S(1)}, u32[]{:S(2)}, u32[]{:S(2)}) collective-permute-start(bf16[8,128,128]{2,1,0:T(8,128)(2,1)S(1)} %get-tuple-element.49), channel_id=1, source_target_pairs={{2,0},{3,1},{4,2},{5,3},{6,4},{7,5},{10,8},{11,9},{12,10},{13,11},... | collective-permute-start | bytes 786440 | tf_op jit(solution)/shard_map/ppermute | solution.py:409
  84.8 19.9 %collective-permute-start.32 = (bf16[64,2048]{1,0:T(8,128)(2,1)S(1)}, bf16[64,2048]{1,0:T(8,128)(2,1)S(1)}, u32[]{:S(2)}, u32[]{:S(2)}) collective-permute-start(bf16[64,2048]{1,0:T(8,128)(2,1)S(1)} %get-tuple-element.60), channel_id=1, source_target_pairs={{0,2},{1,3},{2,4},{3,5},{4,6},{5,7},{6,0},{7,1},{8,10},{9,11},{10,... | collective-permute-start | bytes 786440 | tf_op jit(solution)/shard_map/ppermute | solution.py:405
  86.1 19.9 %collective-permute-start.31 = (bf16[64,2048]{1,0:T(8,128)(2,1)S(1)}, bf16[64,2048]{1,0:T(8,128)(2,1)S(1)}, u32[]{:S(2)}, u32[]{:S(2)}) collective-permute-start(bf16[64,2048]{1,0:T(8,128)(2,1)S(1)} %get-tuple-element.59), channel_id=1, source_target_pairs={{0,4},{1,5},{2,6},{3,7},{4,0},{5,1},{6,2},{7,3},{8,12},{9,13},{10,... | collective-permute-start | bytes 786440 | tf_op jit(solution)/shard_map/ppermute | solution.py:405
  86.3 26.9 %collective-permute-start.30 = (bf16[64,2048]{1,0:T(8,128)(2,1)S(1)}, bf16[64,2048]{1,0:T(8,128)(2,1)S(1)}, u32[]{:S(2)}, u32[]{:S(2)}) collective-permute-start(bf16[64,2048]{1,0:T(8,128)(2,1)S(1)} %get-tuple-element.58), channel_id=1, source_target_pairs={{0,6},{1,7},{2,0},{3,1},{4,2},{5,3},{6,4},{7,5},{8,14},{9,15},{10,... | collective-permute-start | bytes 786440 | tf_op jit(solution)/shard_map/ppermute | solution.py:405
  90.3 25.0 %collective-permute-start.26 = (bf16[128,1024]{1,0:T(8,128)(2,1)S(1)}, bf16[128,1024]{1,0:T(8,128)(2,1)S(1)}, u32[]{:S(2)}, u32[]{:S(2)}) collective-permute-start(bf16[128,1024]{1,0:T(8,128)(2,1)S(1)} %get-tuple-element.47), channel_id=1, source_target_pairs={{0,1},{1,0},{2,3},{3,2},{4,5},{5,4},{6,7},{7,6},{8,9},{9,8},{10,11... | collective-permute-start | bytes 786440 | tf_op jit(solution)/shard_map/ppermute | solution.py:401
  92.6 47.0 %collective-permute-start.15 = (bf16[128,2048]{1,0:T(8,128)(2,1)S(1)}, bf16[128,2048]{1,0:T(8,128)(2,1)S(1)}, u32[]{:S(2)}, u32[]{:S(2)}) collective-permute-start(bf16[128,2048]{1,0:T(8,128)(2,1)S(1)} %get-tuple-element.40), channel_id=1, source_target_pairs={{0,24},{8,16},{16,8},{24,0},{1,25},{9,17},{17,9},{25,1},{2,26},{10... | collective-permute-start | bytes 1572872 | tf_op jit(solution)/shard_map/ppermute | solution.py:412
  104.7 13.2 %collective-permute-start.28 = (bf16[8,128,128]{2,1,0:T(8,128)(2,1)S(1)}, bf16[8,128,128]{2,1,0:T(8,128)(2,1)S(1)}, u32[]{:S(2)}, u32[]{:S(2)}) collective-permute-start(bf16[8,128,128]{2,1,0:T(8,128)(2,1)S(1)} %add.38), channel_id=1, source_target_pairs={{4,0},{5,1},{6,2},{7,3},{12,8},{13,9},{14,10},{15,11},{20,16},{21,... | collective-permute-start | bytes 786440 | tf_op jit(solution)/shard_map/ppermute | solution.py:409
  114.2 25.4 %collective-permute-start.14 = (bf16[128,2048]{1,0:T(8,128)(2,1)S(1)}, bf16[128,2048]{1,0:T(8,128)(2,1)S(1)}, u32[]{:S(2)}, u32[]{:S(2)}) collective-permute-start(bf16[128,2048]{1,0:T(8,128)(2,1)S(1)} %get-tuple-element.39), channel_id=1, source_target_pairs={{0,16},{8,24},{16,0},{24,8},{1,17},{9,25},{17,1},{25,9},{2,18},{10... | collective-permute-start | bytes 1572872 | tf_op jit(solution)/shard_map/ppermute | solution.py:412
  115.3 24.3 %collective-permute-start.13 = (bf16[128,2048]{1,0:T(8,128)(2,1)S(1)}, bf16[128,2048]{1,0:T(8,128)(2,1)S(1)}, u32[]{:S(2)}, u32[]{:S(2)}) collective-permute-start(bf16[128,2048]{1,0:T(8,128)(2,1)S(1)} %get-tuple-element.38), channel_id=1, source_target_pairs={{0,8},{8,0},{16,24},{24,16},{1,9},{9,1},{17,25},{25,17},{2,10},{10... | collective-permute-start | bytes 1572872 | tf_op jit(solution)/shard_map/ppermute | solution.py:412
  117.9 18.1 %collective-permute-start.34 = (bf16[64,2048]{1,0:T(8,128)(2,1)S(1)}, bf16[64,2048]{1,0:T(8,128)(2,1)S(1)}, u32[]{:S(2)}, u32[]{:S(2)}) collective-permute-start(bf16[64,2048]{1,0:T(8,128)(2,1)S(1)} %add_convert_fusion.1.t0), channel_id=1, source_target_pairs={{0,16},{8,24},{16,0},{24,8},{1,17},{9,25},{17,1},{25,9},{2,18},{10... | collective-permute-start | bytes 786440 | tf_op jit(solution)/shard_map/ppermute | solution.py:412
  122.6 15.0 %collective-permute-start.35 = (bf16[64,2048]{1,0:T(8,128)(2,1)S(1)}, bf16[64,2048]{1,0:T(8,128)(2,1)S(1)}, u32[]{:S(2)}, u32[]{:S(2)}) collective-permute-start(bf16[64,2048]{1,0:T(8,128)(2,1)S(1)} %add_convert_fusion.1.t0), channel_id=1, source_target_pairs={{0,24},{8,16},{16,8},{24,0},{1,25},{9,17},{17,9},{25,1},{2,26},{10... | collective-permute-start | bytes 786440 | tf_op jit(solution)/shard_map/ppermute | solution.py:412
  (24 other events, 254.9 us)

commit v2 on v1

--- a/solution.py
+++ b/solution.py
@@ -156,6 +156,7 @@
 
 
 CHIPS = 4
+ORDER = (0, 2, 1, 3)
 COLUMNS = 4
 PAIR = 2 * HEAD
 QUARTER = PAIR // COLUMNS
@@ -168,7 +169,7 @@
     return lax.dot_general(a, b, (((ca,), (cb,)), ((), ())), preferred_element_type=f32)
 
 
-def call(kernel, outs, name, args, flops, grid=(), in_specs=None, out_specs=None, scratch=(), aliases=None):
+def call(kernel, outs, name, args, flops, grid=(), in_specs=None, out_specs=None, scratch=(), hint=1):
     vmem = pl.BlockSpec(memory_space=pltpu.VMEM)
     smem = pl.BlockSpec(memory_space=pltpu.SMEM)
     if in_specs is None:
@@ -183,9 +184,8 @@
         in_specs=in_specs,
         out_specs=out_specs,
         scratch_shapes=list(scratch),
-        input_output_aliases=aliases or {},
         compiler_params=pltpu.CompilerParams(vmem_limit_bytes=VMEM_LIMIT),
-        cost_estimate=pl.CostEstimate(flops=flops, bytes_accessed=moved, transcendentals=0),
+        cost_estimate=pl.CostEstimate(flops=flops * hint, bytes_accessed=moved * hint, transcendentals=0),
         name=name,
     )(*args)
 
@@ -195,11 +195,16 @@
 
 
 def chip_of(place, s):
-    return lax.rem(place[0] + (CHIPS - s), CHIPS)
+    return lax.bitwise_xor(place[0], ORDER[s])
 
 
 def head_lanes(place, chip, j):
     return pl.ds(pl.multiple_of((2 * chip + place[1]) * PAIR + j * HEAD, HEAD), HEAD)
+
+
+def entering_state(near, far, at, takes_near):
+    first = jnp.where(takes_near, near[at].astype(f32), 0.0)
+    return (first + far[at].astype(f32)).astype(bf16)
 
 
 def rows_of(own, sib, lanes):
@@ -229,6 +234,7 @@
 def attend_kernel(place, q_own, q_sib, k_own, k_sib, v_own, v_sib, near, far, gain, attended, n0, n1, n2, n3):
     rows = 2 * q_own.shape[0]
     mask = causal_mask(place, rows)
+    odd = lax.rem(place[0], 2) == 1
     column = place[2]
     low = lax.broadcasted_iota(jnp.int32, (rows, HEAD), 1) < HEAD // 2
     turned = lax.rem(column, 2) == 1
@@ -245,7 +251,7 @@
                 fk = feature(rows_of(k_own, k_sib, lanes))
                 value = rows_of(v_own, v_sib, lanes)
                 probs = jnp.where(mask, dims(fq, fk, 1, 1), 0.0).astype(bf16)
-                prefix = (near[2 * chip + j].astype(f32) + far[2 * chip + j].astype(f32)).astype(bf16)
+                prefix = entering_state(near, far, 2 * chip + j, odd)
                 out = dims(probs, value, 1, 0) + dims(fq, prefix, 1, 0)
                 attended[:, pl.ds(s * PAIR + j * HEAD, HEAD)] = out
                 inverse = lax.rsqrt(jnp.mean(out * out, axis=-1, keepdims=True) + epsilon)
@@ -260,10 +266,10 @@
             packs[2 * i + 1][:, at] = jnp.where(low, pltpu.roll(a, HEAD // 2, 1), b).astype(bf16)
 
 
-def d_normed_kernel(w, *refs):
+def d_normed_kernel(w_first, w_second, *refs):
     cots, outs = refs[: 2 * COLUMNS], refs[2 * COLUMNS :]
     half = cots[0].shape[0]
-    weight = w[...]
+    weight = jnp.concatenate([w_first[...], w_second[...]], axis=0)
     for m in range(COLUMNS):
         outs[m][:half] = dims(cots[2 * m][...], weight, 1, 1).astype(bf16)
         outs[m][half:] = dims(cots[2 * m + 1][...], weight, 1, 1).astype(bf16)
@@ -307,69 +313,72 @@
 
 
 def inner_kernel(
-    place, q_own, q_sib, k_own, k_sib, v_own, v_sib, near, far, d_attended, gq, gq_sib, part_k, part_v
+    place, q_own, q_sib, k_own, k_sib, v_own, v_sib, near, far, d_attended, gq, part_k, part_v, sent
 ):
     half = q_own.shape[0]
     mask = causal_mask(place, 2 * half)
     mask_t = causal_mask(place, 2 * half, True)
-    for s in range(CHIPS):
-        chip = chip_of(place, s)
-        for j in range(2):
-            lanes = head_lanes(place, chip, j)
-            here = pl.ds(s * PAIR + j * HEAD, HEAD)
-            query = rows_of(q_own, q_sib, lanes)
-            fq = feature(query)
-            fk = feature(rows_of(k_own, k_sib, lanes))
-            value = rows_of(v_own, v_sib, lanes)
-            grad = d_attended[:, here]
-            prefix = (near[2 * chip + j].astype(f32) + far[2 * chip + j].astype(f32)).astype(bf16)
-            d_probs = jnp.where(mask, dims(grad, value, 1, 1), 0.0).astype(bf16)
-            d_probs_t = jnp.where(mask_t, dims(value, grad, 1, 1), 0.0).astype(bf16)
-            probs_t = jnp.where(mask_t, dims(fk, fq, 1, 1), 0.0).astype(bf16)
-            d_fq = dims(d_probs, fk, 1, 0) + dims(grad, prefix, 1, 1)
-            out = (d_fq * feature_slope(query)).astype(bf16)
-            gq[:, lanes] = out[:half]
-            gq_sib[:, pl.ds(pl.multiple_of(chip * PAIR + j * HEAD, HEAD), HEAD)] = out[half:]
-            part_k[:, here] = dims(d_probs_t, fq, 1, 0)
-            part_v[:, here] = dims(probs_t, grad, 1, 0)
-
-
-def outer_kernel(place, k_own, k_sib, v_own, v_sib, near, far, part_k, part_v, gk, gv, sent):
-    half = k_own.shape[0]
+    odd = lax.rem(place[0], 2) == 1
     for s in range(CHIPS):
         chip = chip_of(place, s)
         for j in range(2):
             lanes = head_lanes(place, chip, j)
             here = pl.ds(s * PAIR + j * HEAD, HEAD)
             there = pl.ds(pl.multiple_of(chip * PAIR + j * HEAD, HEAD), HEAD)
-            key = rows_of(k_own, k_sib, lanes)
+            query = rows_of(q_own, q_sib, lanes)
+            fq = feature(query)
+            fk = feature(rows_of(k_own, k_sib, lanes))
             value = rows_of(v_own, v_sib, lanes)
-            suffix = (near[2 * chip + j].astype(f32) + far[2 * chip + j].astype(f32)).astype(bf16)
-            d_fk = part_k[:, here] + dims(value, suffix, 1, 1)
-            out_k = (d_fk * feature_slope(key)).astype(bf16)
-            out_v = (part_v[:, here] + dims(feature(key), suffix, 1, 0)).astype(bf16)
-            gk[:, lanes] = out_k[:half]
-            gv[:, lanes] = out_v[:half]
-            sent[0, :, there] = out_k[half:]
-            sent[1, :, there] = out_v[half:]
-
-
-def fill_kernel(place, *refs):
-    n = (len(refs) + 1) // 3
-    got, held, outs = refs[:n], refs[n : 2 * n], refs[2 * n :]
+            grad = d_attended[:, here]
+            prefix = entering_state(near, far, 2 * chip + j, odd)
+            d_probs = jnp.where(mask, dims(grad, value, 1, 1), 0.0).astype(bf16)
+            d_probs_t = jnp.where(mask_t, dims(value, grad, 1, 1), 0.0).astype(bf16)
+            probs_t = jnp.where(mask_t, dims(fk, fq, 1, 1), 0.0).astype(bf16)
+            d_fq = dims(d_probs, fk, 1, 0) + dims(grad, prefix, 1, 1)
+            out = (d_fq * feature_slope(query)).astype(bf16)
+            from_k = dims(d_probs_t, fq, 1, 0)
+            from_v = dims(probs_t, grad, 1, 0)
+            gq[:, lanes] = out[:half]
+            part_k[:, there] = from_k[:half]
+            part_v[:, there] = from_v[:half]
+            sent[0, :, there] = out[half:]
+            sent[1, :, there] = from_k[half:].astype(bf16)
+            sent[2, :, there] = from_v[half:].astype(bf16)
+
+
+def outer_kernel(place, k_own, v_own, near, near_sib, far, far_sib, part_k, part_v, got, gk, gv):
+    odd = lax.rem(place[0], 2) == 1
+    for chip in range(CHIPS):
+        for j in range(2):
+            there = pl.ds(chip * PAIR + j * HEAD, HEAD)
+            for other in range(2):
+                block = 2 * chip + (1 - place[1] if other else place[1])
+                lanes = pl.ds(pl.multiple_of(block * PAIR + j * HEAD, HEAD), HEAD)
+                states = (near_sib, far_sib) if other else (near, far)
+                suffix = entering_state(*states, 2 * chip + j, jnp.logical_not(odd))
+                from_k = got[1, :, there].astype(f32) if other else part_k[:, there]
+                from_v = got[2, :, there].astype(f32) if other else part_v[:, there]
+                key = k_own[:, lanes]
+                d_fk = from_k + dims(v_own[:, lanes], suffix, 1, 1)
+                gk[:, lanes] = (d_fk * feature_slope(key)).astype(bf16)
+                gv[:, lanes] = (from_v + dims(feature(key), suffix, 1, 0)).astype(bf16)
+
+
+def fill_kernel(place, got, held, out):
     for chip in range(CHIPS):
         pair = pl.ds(chip * PAIR, PAIR)
         own = pl.ds(pl.multiple_of((2 * chip + place[1]) * PAIR, PAIR), PAIR)
         other = pl.ds(pl.multiple_of((2 * chip + 1 - place[1]) * PAIR, PAIR), PAIR)
-        for a, b, o in zip(got, held, outs):
-            o[:, own] = b[:, own]
-            o[:, other] = a[:, pair]
+        out[:, own] = held[:, own]
+        out[:, other] = got[0, :, pair]
 
 
 def mixed_kernel(n0, n1, n2, n3, nx, w_own, w_sib, m0, m1, m2, m3):
     half = nx.shape[1]
+    weight = jnp.concatenate([w_own[...], w_sib[...]], axis=0)
     for m, (n, out) in enumerate(zip((n0, n1, n2, n3), (m0, m1, m2, m3))):
-        out[...] = (dims(n[:half, :], w_own[...], 1, 0) + dims(nx[m], w_sib[...], 1, 0)).astype(out.dtype)
+        rows = jnp.concatenate([n[:half, :], nx[m]], axis=1)
+        out[...] = dims(rows, weight, 1, 0).astype(out.dtype)
 
 
 def weight_kernel(*refs):
@@ -380,14 +389,18 @@
         for part in range(2):
             term = dims(packs[m][pl.ds(part * half, half), :], cots[2 * m + part][...], 0, 0)
             total = term if total is None else total + term
-    for s in range(CHIPS):
-        outs[s][...] = total[s * QUARTER : (s + 1) * QUARTER].astype(outs[s].dtype)
+    outs[0][...] = total[: 2 * QUARTER]
+    outs[1][...] = total[2 * QUARTER :].astype(bf16)
 
 
 def gathered_kernel(scale, place, t0, t1, t2, t3, out):
     for m, t in enumerate((t0, t1, t2, t3)):
         column = lax.bitwise_xor(place[2], m)
         out[pl.ds(pl.multiple_of(column * QUARTER, QUARTER), QUARTER), :] = t[...].astype(f32) * scale
+
+
+def after(x, *earlier):
+    return lax.optimization_barrier((x, *earlier))[0]
 
 
 def on_device_planned(query_rows, key_rows, value_rows, norm_gain, out_weight, cotangent):
@@ -396,50 +409,114 @@
     here, column = lax.axis_index("ctx"), lax.axis_index("dp")
     place = jnp.stack([here // 2, here % 2, column]).astype(jnp.int32)
     gain = norm_gain.reshape(1, width)
-
-    def to_sib(x):
-        return lax.ppermute(x, "ctx", [(i, i ^ 1) for i in range(2 * CHIPS)])
-
-    def around(x, s):
-        pairs = [(2 * c + e, 2 * ((c + s) % CHIPS) + e) for c in range(CHIPS) for e in range(2)]
-        return lax.ppermute(x, "ctx", pairs)
-
-    def along(x, s):
-        pairs = [(2 * c + e, 2 * (c + s) + e) for c in range(CHIPS) for e in range(2) if 0 <= c + s < CHIPS]
-        return lax.ppermute(x, "ctx", pairs)
-
-    def across(x, m):
-        return x if m == 0 else lax.ppermute(x, "dp", [(d, d ^ m) for d in range(COLUMNS)])
-
-    key_sib, value_sib, query_sib = to_sib(key), to_sib(value), to_sib(query)
     heads = 2 * CHIPS
     state_shape = like((heads, HEAD, HEAD), bf16)
     state_flops = 2 * heads * 2 * half * HEAD * HEAD
-
-    state = call(states_kernel, [state_shape], "states", (place, key, key_sib, value, value_sib), state_flops)[0]
-    near = along(state, 1)
-    far = along(state + near, 2)
-
-    quarter = lax.dynamic_slice(out_weight, (column * QUARTER, 0), (QUARTER, width))
-    weight = jnp.concatenate([quarter] + [around(quarter, s) for s in range(1, CHIPS)], axis=0)
-    weight_sib = to_sib(weight)
-    cots = [across(cot, m) for m in range(COLUMNS)]
-    cot_parts = [x for c in cots for x in (c, to_sib(c))]
-
-    pack = like((2 * half, PAIR), bf16)
+    pack, full = like((2 * half, PAIR), bf16), like((half, width), bf16)
+    part = like((half, width // 2), f32)
+    step = 512
+
+    def column_spec(rows, columns):
+        return pl.BlockSpec((rows, columns), lambda i: (0, i))
+
+    def fixed(shape):
+        return pl.BlockSpec(shape, lambda i: (0,) * len(shape))
+
+    def sent(x, name, axis, pairs):
+        with jax.named_scope("send_" + name):
+            return lax.ppermute(x, axis, pairs)
+
+    def to_sib(x, name):
+        return sent(x, name, "ctx", [(i, i ^ 1) for i in range(2 * CHIPS)])
+
+    def swapped(x, s, name):
+        pairs = [(2 * c + e, 2 * (c ^ s) + e) for c in range(CHIPS) for e in range(2)]
+        return sent(x, name, "ctx", pairs)
+
+    def halfway(x, s, name):
+        pairs = [(2 * c + e, 2 * (c + s) + e) for c in range(CHIPS) for e in range(2) if 0 <= c + s < CHIPS]
+        return sent(x, name, "ctx", pairs)
+
+    def across(x, m, name):
+        return sent(x, name, "dp", [(d, d ^ m) for d in range(COLUMNS)])
+
+    key_sib = to_sib(key, "key")
+    value_sib = to_sib(value, "value")
+    state = call(
+        states_kernel, [state_shape], "states", (place, key, key_sib, value, value_sib), state_flops
+    )[0]
+    query_sib = to_sib(after(query, state), "query")
+    near = swapped(state, 1, "near")
+    pair_state = state + near
+    far = halfway(pair_state, 2, "far")
     attended, *packs = call(
         attend_kernel,
         [like((2 * half, heads * HEAD), f32)] + [pack] * COLUMNS,
         "attend",
         (place, query, query_sib, key, key_sib, value, value_sib, near, far, gain),
         8 * state_flops,
-    )
+        hint=0,
+    )
+    quarter = lax.dynamic_slice(out_weight, (column * QUARTER, 0), (QUARTER, width))
+    w2 = swapped(quarter, 2, "w2")
+    w_first = jnp.concatenate([quarter, w2], axis=0)
+    w_second = swapped(w_first, 1, "w_second")
+    sib0 = to_sib(after(cot, state), "sib0")
+    cot1 = across(cot, 1, "cot1")
+    sib1 = to_sib(cot1, "sib1")
+    cot2 = across(cot, 2, "cot2")
+    sib2 = to_sib(after(cot2, far), "sib2")
+    cot3 = across(after(cot, near), 3, "cot3")
+    sib3 = to_sib(cot3, "sib3")
+    cot_parts = [cot, sib0, cot1, sib1, cot2, sib2, cot3, sib3]
     d_packs = call(
-        d_normed_kernel, [pack] * COLUMNS, "d_normed", (weight, *cot_parts), 2 * 8 * half * PAIR * width
-    )
-    d_got = [across(d_packs[m], m) for m in range(COLUMNS)]
-    n_got = [across(packs[m], m) for m in range(COLUMNS)]
-
+        d_normed_kernel,
+        [pack] * COLUMNS,
+        "d_normed",
+        (w_first, w_second, *cot_parts),
+        2 * 8 * half * PAIR * width,
+    )
+    n1 = after(across(packs[1], 1, "n1"), *d_packs)
+    n2 = after(across(packs[2], 2, "n2"), *d_packs)
+    n3 = after(across(packs[3], 3, "n3"), *d_packs)
+    n_got = (packs[0], n1, n2, n3)
+    kept, given = call(
+        weight_kernel,
+        [like((2 * QUARTER, width), f32), like((2 * QUARTER, width), bf16)],
+        "weight_terms",
+        (*n_got, *cot_parts),
+        2 * 8 * half * PAIR * width,
+        grid=(width // step,),
+        in_specs=[fixed((2 * half, PAIR))] * COLUMNS + [column_spec(half, step)] * (2 * COLUMNS),
+        out_specs=[column_spec(2 * QUARTER, step)] * 2,
+    )
+    n_sib = to_sib(after(jnp.stack([n[half:] for n in n_got]), given), "n_sib")
+    weight = jnp.concatenate([w_first, w_second], axis=0)
+    w_sib = to_sib(after(weight, given), "w_sib")
+    outs = call(
+        mixed_kernel,
+        [like((half, width), f32)] + [like((half, width), bf16)] * (COLUMNS - 1),
+        "mixed_terms",
+        (*n_got, n_sib, weight, w_sib),
+        2 * 4 * half * 2 * PAIR * width,
+        grid=(width // step,),
+        in_specs=[fixed((2 * half, PAIR))] * COLUMNS
+        + [fixed((COLUMNS, half, PAIR))]
+        + [column_spec(PAIR, step)] * 2,
+        out_specs=[column_spec(half, step)] * COLUMNS,
+    )
+    mixed1 = across(outs[1], 1, "mixed1")
+    mixed2 = across(outs[2], 2, "mixed2")
+    mixed3 = across(outs[3], 3, "mixed3")
+    mixed_got = [mixed1, mixed2, mixed3]
+    mixed = outs[0]
+    for x in mixed_got:
+        mixed = mixed + x.astype(f32)
+    mixed = mixed.astype(bf16)
+    d1 = across(after(d_packs[1], given), 1, "d1")
+    d2 = across(after(d_packs[2], given), 2, "d2")
+    d3 = across(after(d_packs[3], given), 3, "d3")
+    d_got = (d_packs[0], d1, d2, d3)
     d_attended, d_state = call(
         d_attend_kernel,
         [like((2 * half, heads * HEAD), bf16), state_shape],
@@ -447,77 +524,43 @@
         (place, query, query_sib, attended, gain, *d_got),
         2 * state_flops,
     )
-    d_near = along(d_state, -1)
-    d_far = along(d_state + d_near, -2)
-
-    term = like((QUARTER, width), bf16)
-    column_spec = lambda rows, step: pl.BlockSpec((rows, step), lambda i: (0, i))
-    fixed = lambda shape: pl.BlockSpec(shape, lambda i: (0,) * len(shape))
-    step = 512
-    terms = call(
-        weight_kernel,
-        [like((QUARTER, width), f32)] + [term] * (CHIPS - 1),
-        "weight_terms",
-        (*n_got, *cot_parts),
-        2 * 8 * half * PAIR * width,
-        grid=(width // step,),
-        in_specs=[fixed((2 * half, PAIR))] * COLUMNS + [column_spec(half, step)] * (2 * COLUMNS),
-        out_specs=[column_spec(QUARTER, step)] * CHIPS,
-    )
-    arrived = [around(terms[s], -s) for s in range(1, CHIPS)]
-    share = terms[0]
-    for x in arrived:
-        share = share + x.astype(f32)
-    share = share.astype(bf16)
-    devices = lax.axis_size("dp") * lax.axis_size("ctx")
-    scale = 1.0 / math.sqrt(devices * half)
-
-    n_sib = to_sib(jnp.stack([n[half:] for n in n_got]))
-    outs = call(
-        mixed_kernel,
-        [like((half, width), f32)] + [like((half, width), bf16)] * (COLUMNS - 1),
-        "mixed_terms",
-        (*n_got, n_sib, weight, weight_sib),
-        2 * 4 * half * 2 * PAIR * width,
-        grid=(width // step,),
-        in_specs=[fixed((2 * half, PAIR))] * COLUMNS
-        + [fixed((COLUMNS, half, PAIR))]
-        + [column_spec(PAIR, step)] * 2,
-        out_specs=[column_spec(half, step)] * COLUMNS,
-    )
-    mixed = outs[0]
-    for m in range(1, COLUMNS):
-        mixed = mixed + across(outs[m], m).astype(f32)
-    mixed = mixed.astype(bf16)
-
-    full = like((half, width), bf16)
-    gq, gq_sent, part_k, part_v = call(
+    gq, part_k, part_v, parts_sent = call(
         inner_kernel,
-        [full, like((half, width // 2), bf16)] + [like((2 * half, heads * HEAD), f32)] * 2,
+        [full, part, part, like((3, half, width // 2), bf16)],
         "inner",
-        (place, query, query_sib, key, key_sib, value, value_sib, near, far, d_attended),
+        (place, query, query_sib, key, key_sib, value, value_sib, near, far, after(d_attended, mixed)),
         14 * state_flops,
     )
-    gk, gv, kv_sent = call(
+    parts_got = to_sib(parts_sent, "parts")
+    grad_queries = call(fill_kernel, [full], "fill_q", (place, parts_got, gq), 0)[0]
+    terms = swapped(given, 1, "terms")
+    d_near = swapped(after(d_state, terms), 1, "d_near")
+    d_near_sib = to_sib(d_near, "d_near_sib")
+    d_pair_state = d_state + d_near
+    d_far = halfway(d_pair_state, -2, "d_far")
+    d_far_sib = to_sib(d_far, "d_far_sib")
+    grad_kv = call(
         outer_kernel,
-        [full, full, like((2, half, width // 2), bf16)],
+        [full, full],
         "outer",
-        (place, key, key_sib, value, value_sib, d_near, d_far, part_k, part_v),
+        (place, key, value, d_near, d_near_sib, d_far, d_far_sib, part_k, part_v, parts_got),
         2 * state_flops,
     )
-    gq_got, kv_got = to_sib(gq_sent), to_sib(kv_sent)
-    grad_queries, = call(fill_kernel, [full], "fill_q", (place, gq_got, gq), 0)
-    grad_keys, grad_values = call(fill_kernel, [full] * 2, "fill_kv", (place, kv_got[0], kv_got[1], gk, gv), 0)
-
-    shares = [across(share, m) for m in range(COLUMNS)]
-    grad_weight, = call(
+    pair = kept + terms.astype(f32)
+    pair_terms = after(swapped(pair[QUARTER:].astype(bf16), 2, "pair_terms"), gq)
+    share = (pair[:QUARTER] + pair_terms.astype(f32)).astype(bf16)
+    share1 = across(share, 1, "share1")
+    share2 = across(share, 2, "share2")
+    share3 = across(share, 3, "share3")
+    scale = 1.0 / math.sqrt(lax.axis_size("dp") * lax.axis_size("ctx") * half)
+    grad_weight = call(
         functools.partial(gathered_kernel, scale),
         [like(out_weight.shape, f32)],
         "grad_weight",
-        (place, *shares),
+        (place, *(share, share1, share2, share3)),
         0,
-    )
-    return (mixed[None], grad_queries[None], grad_keys[None], grad_values[None], grad_weight)
+    )[0]
+    return (mixed[None], grad_queries[None], grad_kv[0][None], grad_kv[1][None], grad_weight)
 
 
 def on_device(query_rows, key_rows, value_rows, norm_gain, out_weight, cotangent):

time: 145 us -> 114 us (0.79)
  waiting for transfers between devices: 63.8 us -> 47.5 us
  starting transfers between devices: 47.1 us -> 37.7 us
  Pallas kernels: 25.2 us -> 22.3 us
    ppermute x36 -> x35, waiting for transfers between devices: 63.8 us -> 47.5 us  [sent(): return lax.ppermute(x, axis, pairs)]
    ppermute x36 -> x35, starting transfers between devices: 47.1 us -> 37.7 us  [sent(): return lax.ppermute(x, axis, pairs)]
    pallas_call x11 -> x10, Pallas kernels: 25.2 us -> 22.3 us  [call(): pl.pallas_call(kernel, out_shape=list(outs), grid=grid, in_specs=in_specs...]
  transfers between devices with their start and end apart: 36 -> 35, of which waited for: 14 -> 12; matrix products, arithmetic and copies ran while one was open for 2% -> 2% of each run, Pallas kernels for 17% -> 15%
where the time goes in v2:
time: 114 us; the launch traced here: 112 us
  waiting for transfers between devices  47.5 us (42%)
  starting transfers between devices  37.7 us (33%)
  Pallas kernels  22.3 us (20%)
  local copies, waits for them, and re-layouts  2.18 us (2%)
  other arithmetic  1.65 us (1%)
    ppermute x35, waiting for transfers between devices, sent(): return lax.ppermute(x, axis, pairs)  47.5 us
    ppermute x35, starting transfers between devices, sent(): return lax.ppermute(x, axis, pairs)  37.7 us
    pallas_call x10, Pallas kernels, call(): pl.pallas_call(kernel, out_shape=list(outs), grid=grid, in_specs=in_specs...  22.3 us
  transfers between devices with their start and end apart: 35, of which 12 were waited for; matrix products, arithmetic and copies ran while one was open for 2% of the time, Pallas kernels for 15%

profile of v2, /device:TPU:16, one launch (start us, length us, event | category | flops | bytes accessed | tf_op | source)
XLA Modules:
  0.0 112.2 jit_solution(7601564174752307688)
XLA Ops:
  1.2 1.5 %collective-permute-start.11 = (bf16[128,2048]{1,0:T(8,128)(2,1)}, bf16[128,2048]{1,0:T(8,128)(2,1)S(1)}, u32[]{:S(2)}, u32[]{:S(2)}) collective-permute-start(bf16[128,2048]{1,0:T(8,128)(2,1)} %bitcast.34), channel_id=1, source_target_pairs={{0,16},{8,24},{16,0},{24,8},{1,17},{9,25},{17,1},{25,9},{2,18},{10... | collective-permute-start | bytes 1572872 | tf_op jit(solution)/shard_map/send_cot2/ppermute | solution.py:427
  2.7 1.5 %collective-permute-start.9 = (bf16[128,2048]{1,0:T(8,128)(2,1)}, bf16[128,2048]{1,0:T(8,128)(2,1)S(1)}, u32[]{:S(2)}, u32[]{:S(2)}) collective-permute-start(bf16[128,2048]{1,0:T(8,128)(2,1)} %bitcast.35), channel_id=1, source_target_pairs={{0,8},{8,0},{16,24},{24,16},{1,9},{9,1},{17,25},{25,17},{2,10},{10... | collective-permute-start | bytes 1572872 | tf_op jit(solution)/shard_map/send_cot1/ppermute | solution.py:427
  7.5 1.6 %collective-permute-start.3 = (bf16[8,128,128]{2,1,0:T(8,128)(2,1)S(1)}, bf16[8,128,128]{2,1,0:T(8,128)(2,1)S(1)}, u32[]{:S(2)}, u32[]{:S(2)}) collective-permute-start(bf16[8,128,128]{2,1,0:T(8,128)(2,1)S(1)} %states.1), channel_id=1, source_target_pairs={{0,2},{1,3},{2,0},{3,1},{4,6},{5,7},{6,4},{7,5},{8,10},{9,11},{10,... | collective-permute-start | bytes 786440 | tf_op jit(solution)/shard_map/send_near/ppermute | solution.py:427
  9.6 9.1 %collective-permute-done.3.near = bf16[8,128,128]{2,1,0:T(8,128)(2,1)S(1)} collective-permute-done((bf16[8,128,128]{2,1,0:T(8,128)(2,1)S(1)}, bf16[8,128,128]{2,1,0:T(8,128)(2,1)S(1)}, u32[]{:S(2)}, u32[]{:S(2)}) %collective-permute-start.3) | collective-permute-done | bytes 262176 | tf_op jit(solution)/shard_map/send_near/ppermute | solution.py:427
  18.7 2.3 %collective-permute-start.13 = (bf16[128,2048]{1,0:T(8,128)(2,1)S(1)}, bf16[128,2048]{1,0:T(8,128)(2,1)S(1)}, u32[]{:S(2)}, u32[]{:S(2)}) collective-permute-start(bf16[128,2048]{1,0:T(8,128)(2,1)S(1)} %bitcast.36), channel_id=1, source_target_pairs={{0,24},{8,16},{16,8},{24,0},{1,25},{9,17},{17,9},{25,1},{2,26},{10... | collective-permute-start | bytes 1572872 | tf_op jit(solution)/shard_map/send_cot3/ppermute | solution.py:427
  22.5 2.7 %collective-permute-start.7 = (bf16[128,2048]{1,0:T(8,128)(2,1)S(1)}, bf16[128,2048]{1,0:T(8,128)(2,1)S(1)}, u32[]{:S(2)}, u32[]{:S(2)}) collective-permute-start(bf16[128,2048]{1,0:T(8,128)(2,1)S(1)} %pad_maximum_fusion.1.w_first), channel_id=1, source_target_pairs={{0,2},{1,3},{2,0},{3,1},{4,6},{5,7},{6,4},{7,5},{8,10},{9,11},{10,... | collective-permute-start | bytes 1572872 | tf_op jit(solution)/shard_map/send_w_second/ppermute | solution.py:427
  25.1 8.1 %collective-permute-done.4.far = bf16[8,128,128]{2,1,0:T(8,128)(2,1)S(1)} collective-permute-done((bf16[8,128,128]{2,1,0:T(8,128)(2,1)S(1)}, bf16[8,128,128]{2,1,0:T(8,128)(2,1)S(1)}, u32[]{:S(2)}, u32[]{:S(2)}) %collective-permute-start.4) | collective-permute-done | bytes 262176 | tf_op jit(solution)/shard_map/send_far/ppermute | solution.py:427
  33.8 2.4 %attend.1 = (f32[256,1024]{1,0:T(8,128)S(1)}, bf16[256,256]{1,0:T(8,128)(2,1)S(1)}, bf16[256,256]{1,0:T(8,128)(2,1)S(1)}, bf16[256,256]{1,0:T(8,128)(2,1)S(1)}, bf16[256,256]{1,0:T(8,128)(2,1)S(1)}) custom-call(s32[3]{0:T(128)S(1)} %pad_add_fusion.place, bf16[128,2048]{1,0:T(8,128)(2,1)S(1)} %bitcast.31, bf16[128,2048]{1,0:T(8,128)(2,1)S(1)} %collective-permute-done.2.q_sib, ...), custom_call_target="tpu_custom_call" | custom-call | tf_op jit(solution)/shard_map/attend/pallas_call | solution.py:180
  36.2 4.8 %collective-permute-done.7.w_second = bf16[128,2048]{1,0:T(8,128)(2,1)S(1)} collective-permute-done((bf16[128,2048]{1,0:T(8,128)(2,1)S(1)}, bf16[128,2048]{1,0:T(8,128)(2,1)S(1)}, u32[]{:S(2)}, u32[]{:S(2)}) %collective-permute-start.7) | collective-permute-done | bytes 524320 | tf_op jit(solution)/shard_map/send_w_second/ppermute | solution.py:427
  41.0 2.4 %collective-permute-start.16 = (bf16[256,256]{1,0:T(8,128)(2,1)S(1)}, bf16[256,256]{1,0:T(8,128)(2,1)S(1)}, u32[]{:S(2)}, u32[]{:S(2)}) collective-permute-start(bf16[256,256]{1,0:T(8,128)(2,1)S(1)} %get-tuple-element.56), channel_id=1, source_target_pairs={{0,24},{8,16},{16,8},{24,0},{1,25},{9,17},{17,9},{25,1},{2,26},{10... | collective-permute-start | bytes 393224 | tf_op jit(solution)/shard_map/send_n3/ppermute | solution.py:427
  44.6 2.8 %d_normed.1 = (bf16[256,256]{1,0:T(8,128)(2,1)S(1)}, bf16[256,256]{1,0:T(8,128)(2,1)S(1)}, bf16[256,256]{1,0:T(8,128)(2,1)S(1)}, bf16[256,256]{1,0:T(8,128)(2,1)S(1)}) custom-call(bf16[128,2048]{1,0:T(8,128)(2,1)S(1)} %pad_maximum_fusion.1.w_first, bf16[128,2048]{1,0:T(8,128)(2,1)S(1)} %collective-permute-done.7.w_second, bf16[128,2048]{1,0:T(8,128)(2,1)S(1)} %bitcast.38, ...), custom_call_target="tpu_custom_call" | custom-call | flops 1073741824 | bytes 5767168 | tf_op jit(solution)/shard_map/d_normed/pallas_call | solution.py:180
  49.0 3.4 %weight_terms.1 = (f32[128,2048]{1,0:T(8,128)S(1)}, bf16[128,2048]{1,0:T(8,128)(2,1)S(1)}) custom-call(bf16[256,256]{1,0:T(8,128)(2,1)S(1)} %get-tuple-element.44.refs_0_.n0, bf16[256,256]{1,0:T(8,128)(2,1)S(1)} %collective-permute-done.5.refs_1_.n1, bf16[256,256]{1,0:T(8,128)(2,1)S(1)} %collective-permute-done.15.refs_2_.n2, ...), custom_call_target="tpu_custom_call" | custom-call | flops 1073741824 | bytes 6291456 | tf_op jit(solution)/shard_map/weight_terms/pallas_call | solution.py:180
  52.5 2.6 %collective-permute-start.26 = (bf16[128,2048]{1,0:T(8,128)(2,1)S(1)}, bf16[128,2048]{1,0:T(8,128)(2,1)S(1)}, u32[]{:S(2)}, u32[]{:S(2)}) collective-permute-start(bf16[128,2048]{1,0:T(8,128)(2,1)S(1)} %get-tuple-element.58), channel_id=1, source_target_pairs={{0,2},{1,3},{2,0},{3,1},{4,6},{5,7},{6,4},{7,5},{8,10},{9,11},{10,... | collective-permute-start | bytes 1572872 | tf_op jit(solution)/shard_map/send_terms/ppermute | solution.py:427
  58.8 2.1 %mixed_terms.1 = (f32[128,2048]{1,0:T(8,128)S(1)}, bf16[128,2048]{1,0:T(8,128)(2,1)S(1)}, bf16[128,2048]{1,0:T(8,128)(2,1)S(1)}, bf16[128,2048]{1,0:T(8,128)(2,1)S(1)}) custom-call(bf16[256,256]{1,0:T(8,128)(2,1)S(1)} %get-tuple-element.44.refs_0_.n0, bf16[256,256]{1,0:T(8,128)(2,1)S(1)} %collective-permute-done.5.refs_1_.n1, ...), custom_call_target="tpu_custom_call" | custom-call | flops 1073741824 | bytes 5505024 | tf_op jit(solution)/shard_map/mixed_terms/pallas_call | solution.py:180
  66.2 2.1 %d_attend.1 = (bf16[256,1024]{1,0:T(8,128)(2,1)S(1)}, bf16[8,128,128]{2,1,0:T(8,128)(2,1)S(1)}) custom-call(s32[3]{0:T(128)S(1)} %pad_add_fusion.place, bf16[128,2048]{1,0:T(8,128)(2,1)S(1)} %bitcast.32, bf16[128,2048]{1,0:T(8,128)(2,1)S(1)} %collective-permute-done.2.q_sib, f32[256,1024]{1,0:T(8,128)S(1)} %get-tuple-element.65.attended, ...), custom_call_target="tpu_custom_call" | custom-call | flops 134217728 | bytes 3416076 | tf_op jit(solution)/shard_map/d_attend/pallas_call | solution.py:180
  70.5 8.2 %collective-permute-done.27.near = bf16[8,128,128]{2,1,0:T(8,128)(2,1)S(1)} collective-permute-done((bf16[8,128,128]{2,1,0:T(8,128)(2,1)S(1)}, bf16[8,128,128]{2,1,0:T(8,128)(2,1)S(1)}, u32[]{:S(2)}, u32[]{:S(2)}) %collective-permute-start.27) | collective-permute-done | bytes 262176 | tf_op jit(solution)/shard_map/send_d_near/ppermute | solution.py:427
  78.8 6.0 %collective-permute-start.29 = (bf16[8,128,128]{2,1,0:T(8,128)(2,1)S(1)}, bf16[8,128,128]{2,1,0:T(8,128)(2,1)S(1)}, u32[]{:S(2)}, u32[]{:S(2)}) collective-permute-start(bf16[8,128,128]{2,1,0:T(8,128)(2,1)S(1)} %add.35), channel_id=1, source_target_pairs={{4,0},{5,1},{6,2},{7,3},{12,8},{13,9},{14,10},{15,11},{20,16},{21,... | collective-permute-start | bytes 786440 | tf_op jit(solution)/shard_map/send_d_far/ppermute | solution.py:427
  84.8 2.5 %collective-permute-done.21 = bf16[128,2048]{1,0:T(8,128)(2,1)S(1)} collective-permute-done((bf16[128,2048]{1,0:T(8,128)(2,1)S(1)}, bf16[128,2048]{1,0:T(8,128)(2,1)S(1)}, u32[]{:S(2)}, u32[]{:S(2)}) %collective-permute-start.21) | collective-permute-done | bytes 524320 | tf_op jit(solution)/shard_map/send_mixed3/ppermute | solution.py:427
  88.4 2.7 %inner.1 = (bf16[128,2048]{1,0:T(8,128)(2,1)S(1)}, f32[128,1024]{1,0:T(8,128)S(1)}, f32[128,1024]{1,0:T(8,128)S(1)}, bf16[3,128,1024]{2,1,0:T(8,128)(2,1)S(1)}) custom-call(s32[3]{0:T(128)S(1)} %pad_add_fusion.place, bf16[128,2048]{1,0:T(8,128)(2,1)S(1)} %bitcast.33, bf16[128,2048]{1,0:T(8,128)(2,1)S(1)} %collective-permute-done.2.q_sib, ...), custom_call_target="tpu_custom_call" | custom-call | flops 939524096 | bytes 6553612 | tf_op jit(solution)/shard_map/inner/pallas_call | solution.py:180
  93.2 1.6 %collective-permute-start.34 = (bf16[64,2048]{1,0:T(8,128)(2,1)S(1)}, bf16[64,2048]{1,0:T(8,128)(2,1)S(1)}, u32[]{:S(2)}, u32[]{:S(2)}) collective-permute-start(bf16[64,2048]{1,0:T(8,128)(2,1)S(1)} %fusion.t0), channel_id=1, source_target_pairs={{0,24},{8,16},{16,8},{24,0},{1,25},{9,17},{17,9},{25,1},{2,26},{10... | collective-permute-start | bytes 786440 | tf_op jit(solution)/shard_map/send_share3/ppermute | solution.py:427
  94.8 5.6 %collective-permute-done.32.t1 = bf16[64,2048]{1,0:T(8,128)(2,1)S(1)} collective-permute-done((bf16[64,2048]{1,0:T(8,128)(2,1)S(1)}, bf16[64,2048]{1,0:T(8,128)(2,1)S(1)}, u32[]{:S(2)}, u32[]{:S(2)}) %collective-permute-start.32) | collective-permute-done | bytes 262176 | tf_op jit(solution)/shard_map/send_share1/ppermute | solution.py:427
  100.8 5.6 %collective-permute-done.34.t3 = bf16[64,2048]{1,0:T(8,128)(2,1)S(1)} collective-permute-done((bf16[64,2048]{1,0:T(8,128)(2,1)S(1)}, bf16[64,2048]{1,0:T(8,128)(2,1)S(1)}, u32[]{:S(2)}, u32[]{:S(2)}) %collective-permute-start.34) | collective-permute-done | bytes 262176 | tf_op jit(solution)/shard_map/send_share3/ppermute | solution.py:427
  106.5 2.0 %grad_weight.1 = f32[256,2048]{1,0:T(8,128)} custom-call(s32[3]{0:T(128)S(1)} %pad_add_fusion.place, bf16[64,2048]{1,0:T(8,128)(2,1)S(1)} %fusion.t0, bf16[64,2048]{1,0:T(8,128)(2,1)S(1)} %collective-permute-done.32.t1, bf16[64,2048]{1,0:T(8,128)(2,1)S(1)} %collective-permute-done.33.t2, bf16[64,2048]{1,0:T(8,128)(2,1)S(1)} %collective-permute-done.34.t3), custom_call_target="tpu_custom_call" | custom-call | bytes 3145740 | tf_op jit(solution)/shard_map/grad_weight/pallas_call | solution.py:180
  109.9 2.3 %outer.1 = (bf16[128,2048]{1,0:T(8,128)(2,1)}, bf16[128,2048]{1,0:T(8,128)(2,1)}) custom-call(s32[3]{0:T(128)S(1)} %pad_add_fusion.place, bf16[128,2048]{1,0:T(8,128)(2,1)S(1)} %bitcast.24, bf16[128,2048]{1,0:T(8,128)(2,1)S(1)} %bitcast.29, bf16[8,128,128]{2,1,0:T(8,128)(2,1)S(1)} %collective-permute-done.27.near, ...), custom_call_target="tpu_custom_call" | custom-call | flops 134217728 | bytes 4980748 | tf_op jit(solution)/shard_map/outer/pallas_call | solution.py:180
  (86 shorter events, 25.3 us)
Async XLA Ops:
  1.2 21.2 %collective-permute-start.11 = (bf16[128,2048]{1,0:T(8,128)(2,1)}, bf16[128,2048]{1,0:T(8,128)(2,1)S(1)}, u32[]{:S(2)}, u32[]{:S(2)}) collective-permute-start(bf16[128,2048]{1,0:T(8,128)(2,1)} %bitcast.34), channel_id=1, source_target_pairs={{0,16},{8,24},{16,0},{24,8},{1,17},{9,25},{17,1},{25,9},{2,18},{10... | collective-permute-start | bytes 1572872 | tf_op jit(solution)/shard_map/send_cot2/ppermute | solution.py:427
  2.7 22.4 %collective-permute-start.9 = (bf16[128,2048]{1,0:T(8,128)(2,1)}, bf16[128,2048]{1,0:T(8,128)(2,1)S(1)}, u32[]{:S(2)}, u32[]{:S(2)}) collective-permute-start(bf16[128,2048]{1,0:T(8,128)(2,1)} %bitcast.35), channel_id=1, source_target_pairs={{0,8},{8,0},{16,24},{24,16},{1,9},{9,1},{17,25},{25,17},{2,10},{10... | collective-permute-start | bytes 1572872 | tf_op jit(solution)/shard_map/send_cot1/ppermute | solution.py:427
  7.5 11.2 %collective-permute-start.3 = (bf16[8,128,128]{2,1,0:T(8,128)(2,1)S(1)}, bf16[8,128,128]{2,1,0:T(8,128)(2,1)S(1)}, u32[]{:S(2)}, u32[]{:S(2)}) collective-permute-start(bf16[8,128,128]{2,1,0:T(8,128)(2,1)S(1)} %states.1), channel_id=1, source_target_pairs={{0,2},{1,3},{2,0},{3,1},{4,6},{5,7},{6,4},{7,5},{8,10},{9,11},{10,... | collective-permute-start | bytes 786440 | tf_op jit(solution)/shard_map/send_near/ppermute | solution.py:427
  9.2 11.9 %collective-permute-start.6 = (bf16[64,2048]{1,0:T(8,128)(2,1)S(1)}, bf16[64,2048]{1,0:T(8,128)(2,1)S(1)}, u32[]{:S(2)}, u32[]{:S(2)}) collective-permute-start(bf16[64,2048]{1,0:T(8,128)(2,1)S(1)} %constant_dynamic-slice_fusion), channel_id=1, source_target_pairs={{0,4},{1,5},{2,6},{3,7},{4,0},{5,1},{6,2},{7,3},{8,12},{9,13},{10,... | collective-permute-start | bytes 786440 | tf_op jit(solution)/shard_map/send_w2/ppermute | solution.py:427
  9.6 23.6 %collective-permute-start.2 = (bf16[128,2048]{1,0:T(8,128)(2,1)S(1)}, bf16[128,2048]{1,0:T(8,128)(2,1)S(1)}, u32[]{:S(2)}, u32[]{:S(2)}) collective-permute-start(bf16[128,2048]{1,0:T(8,128)(2,1)S(1)} %bitcast.30), channel_id=1, source_target_pairs={{0,1},{1,0},{2,3},{3,2},{4,5},{5,4},{6,7},{7,6},{8,9},{9,8},{10,11... | collective-permute-start | bytes 1572872 | tf_op jit(solution)/shard_map/send_query/ppermute | solution.py:427
  18.7 15.0 %collective-permute-start.13 = (bf16[128,2048]{1,0:T(8,128)(2,1)S(1)}, bf16[128,2048]{1,0:T(8,128)(2,1)S(1)}, u32[]{:S(2)}, u32[]{:S(2)}) collective-permute-start(bf16[128,2048]{1,0:T(8,128)(2,1)S(1)} %bitcast.36), channel_id=1, source_target_pairs={{0,24},{8,16},{16,8},{24,0},{1,25},{9,17},{17,9},{25,1},{2,26},{10... | collective-permute-start | bytes 1572872 | tf_op jit(solution)/shard_map/send_cot3/ppermute | solution.py:427
  21.1 12.1 %collective-permute-start.4 = (bf16[8,128,128]{2,1,0:T(8,128)(2,1)S(1)}, bf16[8,128,128]{2,1,0:T(8,128)(2,1)S(1)}, u32[]{:S(2)}, u32[]{:S(2)}) collective-permute-start(bf16[8,128,128]{2,1,0:T(8,128)(2,1)S(1)} %add.30), channel_id=1, source_target_pairs={{0,4},{1,5},{2,6},{3,7},{8,12},{9,13},{10,14},{11,15},{16,20},{17,... | collective-permute-start | bytes 786440 | tf_op jit(solution)/shard_map/send_far/ppermute | solution.py:427
  22.5 18.5 %collective-permute-start.7 = (bf16[128,2048]{1,0:T(8,128)(2,1)S(1)}, bf16[128,2048]{1,0:T(8,128)(2,1)S(1)}, u32[]{:S(2)}, u32[]{:S(2)}) collective-permute-start(bf16[128,2048]{1,0:T(8,128)(2,1)S(1)} %pad_maximum_fusion.1.w_first), channel_id=1, source_target_pairs={{0,2},{1,3},{2,0},{3,1},{4,6},{5,7},{6,4},{7,5},{8,10},{9,11},{10,... | collective-permute-start | bytes 1572872 | tf_op jit(solution)/shard_map/send_w_second/ppermute | solution.py:427
  25.1 18.3 %collective-permute-start.8 = (bf16[128,2048]{1,0:T(8,128)(2,1)S(1)}, bf16[128,2048]{1,0:T(8,128)(2,1)S(1)}, u32[]{:S(2)}, u32[]{:S(2)}) collective-permute-start(bf16[128,2048]{1,0:T(8,128)(2,1)S(1)} %bitcast.37), channel_id=1, source_target_pairs={{0,1},{1,0},{2,3},{3,2},{4,5},{5,4},{6,7},{7,6},{8,9},{9,8},{10,11... | collective-permute-start | bytes 1572872 | tf_op jit(solution)/shard_map/send_sib0/ppermute | solution.py:427
  33.2 10.8 %collective-permute-start.10 = (bf16[128,2048]{1,0:T(8,128)(2,1)S(1)}, bf16[128,2048]{1,0:T(8,128)(2,1)S(1)}, u32[]{:S(2)}, u32[]{:S(2)}) collective-permute-start(bf16[128,2048]{1,0:T(8,128)(2,1)S(1)} %collective-permute-done.9.refs_2_.refs_6_), channel_id=1, source_target_pairs={{0,1},{1,0},{2,3},{3,2},{4,5},{5,4},{6,7},{7,6},{8,9},{9,8},{10,11... | collective-permute-start | bytes 1572872 | tf_op jit(solution)/shard_map/send_sib1/ppermute | solution.py:427
  33.2 11.4 %collective-permute-start.12 = (bf16[128,2048]{1,0:T(8,128)(2,1)S(1)}, bf16[128,2048]{1,0:T(8,128)(2,1)S(1)}, u32[]{:S(2)}, u32[]{:S(2)}) collective-permute-start(bf16[128,2048]{1,0:T(8,128)(2,1)S(1)} %collective-permute-done.11.refs_4_.refs_8_), channel_id=1, source_target_pairs={{0,1},{1,0},{2,3},{3,2},{4,5},{5,4},{6,7},{7,6},{8,9},{9,8},{10,11... | collective-permute-start | bytes 1572872 | tf_op jit(solution)/shard_map/send_sib2/ppermute | solution.py:427
  33.7 10.9 %collective-permute-start.14 = (bf16[128,2048]{1,0:T(8,128)(2,1)S(1)}, bf16[128,2048]{1,0:T(8,128)(2,1)S(1)}, u32[]{:S(2)}, u32[]{:S(2)}) collective-permute-start(bf16[128,2048]{1,0:T(8,128)(2,1)S(1)} %collective-permute-done.13.refs_6_.refs_10_), channel_id=1, source_target_pairs={{0,1},{1,0},{2,3},{3,2},{4,5},{5,4},{6,7},{7,6},{8,9},{9,8},{10,11... | collective-permute-start | bytes 1572872 | tf_op jit(solution)/shard_map/send_sib3/ppermute | solution.py:427
  52.5 15.9 %collective-permute-start.26 = (bf16[128,2048]{1,0:T(8,128)(2,1)S(1)}, bf16[128,2048]{1,0:T(8,128)(2,1)S(1)}, u32[]{:S(2)}, u32[]{:S(2)}) collective-permute-start(bf16[128,2048]{1,0:T(8,128)(2,1)S(1)} %get-tuple-element.58), channel_id=1, source_target_pairs={{0,2},{1,3},{2,0},{3,1},{4,6},{5,7},{6,4},{7,5},{8,10},{9,11},{10,... | collective-permute-start | bytes 1572872 | tf_op jit(solution)/shard_map/send_terms/ppermute | solution.py:427
  61.0 23.8 %collective-permute-start.19 = (bf16[128,2048]{1,0:T(8,128)(2,1)S(1)}, bf16[128,2048]{1,0:T(8,128)(2,1)S(1)}, u32[]{:S(2)}, u32[]{:S(2)}) collective-permute-start(bf16[128,2048]{1,0:T(8,128)(2,1)S(1)} %get-tuple-element.62), channel_id=1, source_target_pairs={{0,8},{8,0},{16,24},{24,16},{1,9},{9,1},{17,25},{25,17},{2,10},{10... | collective-permute-start | bytes 1572872 | tf_op jit(solution)/shard_map/send_mixed1/ppermute | solution.py:427
  62.6 22.2 %collective-permute-start.20 = (bf16[128,2048]{1,0:T(8,128)(2,1)S(1)}, bf16[128,2048]{1,0:T(8,128)(2,1)S(1)}, u32[]{:S(2)}, u32[]{:S(2)}) collective-permute-start(bf16[128,2048]{1,0:T(8,128)(2,1)S(1)} %get-tuple-element.63), channel_id=1, source_target_pairs={{0,16},{8,24},{16,0},{24,8},{1,17},{9,25},{17,1},{25,9},{2,18},{10... | collective-permute-start | bytes 1572872 | tf_op jit(solution)/shard_map/send_mixed2/ppermute | solution.py:427
  64.9 22.4 %collective-permute-start.21 = (bf16[128,2048]{1,0:T(8,128)(2,1)S(1)}, bf16[128,2048]{1,0:T(8,128)(2,1)S(1)}, u32[]{:S(2)}, u32[]{:S(2)}) collective-permute-start(bf16[128,2048]{1,0:T(8,128)(2,1)S(1)} %get-tuple-element.64), channel_id=1, source_target_pairs={{0,24},{8,16},{16,8},{24,0},{1,25},{9,17},{17,9},{25,1},{2,26},{10... | collective-permute-start | bytes 1572872 | tf_op jit(solution)/shard_map/send_mixed3/ppermute | solution.py:427
  68.4 10.3 %collective-permute-start.27 = (bf16[8,128,128]{2,1,0:T(8,128)(2,1)S(1)}, bf16[8,128,128]{2,1,0:T(8,128)(2,1)S(1)}, u32[]{:S(2)}, u32[]{:S(2)}) collective-permute-start(bf16[8,128,128]{2,1,0:T(8,128)(2,1)S(1)} %get-tuple-element.74), channel_id=1, source_target_pairs={{0,2},{1,3},{2,0},{3,1},{4,6},{5,7},{6,4},{7,5},{8,10},{9,11},{10,... | collective-permute-start | bytes 786440 | tf_op jit(solution)/shard_map/send_d_near/ppermute | solution.py:427
  69.5 21.6 %collective-permute-start.31 = (bf16[64,2048]{1,0:T(8,128)(2,1)S(1)}, bf16[64,2048]{1,0:T(8,128)(2,1)S(1)}, u32[]{:S(2)}, u32[]{:S(2)}) collective-permute-start(bf16[64,2048]{1,0:T(8,128)(2,1)S(1)} %slice.35), channel_id=1, source_target_pairs={{0,4},{1,5},{2,6},{3,7},{4,0},{5,1},{6,2},{7,3},{8,12},{9,13},{10,... | collective-permute-start | bytes 786440 | tf_op jit(solution)/shard_map/send_pair_terms/ppermute | solution.py:427
  78.8 16.0 %collective-permute-start.29 = (bf16[8,128,128]{2,1,0:T(8,128)(2,1)S(1)}, bf16[8,128,128]{2,1,0:T(8,128)(2,1)S(1)}, u32[]{:S(2)}, u32[]{:S(2)}) collective-permute-start(bf16[8,128,128]{2,1,0:T(8,128)(2,1)S(1)} %add.35), channel_id=1, source_target_pairs={{4,0},{5,1},{6,2},{7,3},{12,8},{13,9},{14,10},{15,11},{20,16},{21,... | collective-permute-start | bytes 786440 | tf_op jit(solution)/shard_map/send_d_far/ppermute | solution.py:427
  91.1 17.4 %collective-permute-start.25 = (bf16[3,128,1024]{2,1,0:T(8,128)(2,1)S(1)}, bf16[3,128,1024]{2,1,0:T(8,128)(2,1)S(1)}, u32[]{:S(2)}, u32[]{:S(2)}) collective-permute-start(bf16[3,128,1024]{2,1,0:T(8,128)(2,1)S(1)} %get-tuple-element.71), channel_id=1, source_target_pairs={{0,1},{1,0},{2,3},{3,2},{4,5},{5,4},{6,7},{7,6},{8,9},{9,8},{10,11... | collective-permute-start | bytes 2359304 | tf_op jit(solution)/shard_map/send_parts/ppermute | solution.py:427
  91.2 9.2 %collective-permute-start.32 = (bf16[64,2048]{1,0:T(8,128)(2,1)S(1)}, bf16[64,2048]{1,0:T(8,128)(2,1)S(1)}, u32[]{:S(2)}, u32[]{:S(2)}) collective-permute-start(bf16[64,2048]{1,0:T(8,128)(2,1)S(1)} %fusion.t0), channel_id=1, source_target_pairs={{0,8},{8,0},{16,24},{24,16},{1,9},{9,1},{17,25},{25,17},{2,10},{10... | collective-permute-start | bytes 786440 | tf_op jit(solution)/shard_map/send_share1/ppermute | solution.py:427
  93.2 13.2 %collective-permute-start.34 = (bf16[64,2048]{1,0:T(8,128)(2,1)S(1)}, bf16[64,2048]{1,0:T(8,128)(2,1)S(1)}, u32[]{:S(2)}, u32[]{:S(2)}) collective-permute-start(bf16[64,2048]{1,0:T(8,128)(2,1)S(1)} %fusion.t0), channel_id=1, source_target_pairs={{0,24},{8,16},{16,8},{24,0},{1,25},{9,17},{17,9},{25,1},{2,26},{10... | collective-permute-start | bytes 786440 | tf_op jit(solution)/shard_map/send_share3/ppermute | solution.py:427
  94.8 15.1 %collective-permute-start.28 = (bf16[8,128,128]{2,1,0:T(8,128)(2,1)S(1)}, bf16[8,128,128]{2,1,0:T(8,128)(2,1)S(1)}, u32[]{:S(2)}, u32[]{:S(2)}) collective-permute-start(bf16[8,128,128]{2,1,0:T(8,128)(2,1)S(1)} %collective-permute-done.27.near), channel_id=1, source_target_pairs={{0,1},{1,0},{2,3},{3,2},{4,5},{5,4},{6,7},{7,6},{8,9},{9,8},{10,11... | collective-permute-start | bytes 786440 | tf_op jit(solution)/shard_map/send_d_near_sib/ppermute | solution.py:427
  100.4 9.5 %collective-permute-start.30 = (bf16[8,128,128]{2,1,0:T(8,128)(2,1)S(1)}, bf16[8,128,128]{2,1,0:T(8,128)(2,1)S(1)}, u32[]{:S(2)}, u32[]{:S(2)}) collective-permute-start(bf16[8,128,128]{2,1,0:T(8,128)(2,1)S(1)} %collective-permute-done.29.far), channel_id=1, source_target_pairs={{0,1},{1,0},{2,3},{3,2},{4,5},{5,4},{6,7},{7,6},{8,9},{9,8},{10,11... | collective-permute-start | bytes 786440 | tf_op jit(solution)/shard_map/send_d_far_sib/ppermute | solution.py:427
  (19 other events, 157.9 us)

commit v3 on v2

--- a/solution.py
+++ b/solution.py
@@ -449,24 +449,24 @@
     near = swapped(state, 1, "near")
     pair_state = state + near
     far = halfway(pair_state, 2, "far")
-    attended, *packs = call(
+    sib0 = to_sib(after(cot, state), "sib0")
+    attended, *packs = after(call(
         attend_kernel,
         [like((2 * half, heads * HEAD), f32)] + [pack] * COLUMNS,
         "attend",
         (place, query, query_sib, key, key_sib, value, value_sib, near, far, gain),
         8 * state_flops,
         hint=0,
-    )
+    ), sib0)
     quarter = lax.dynamic_slice(out_weight, (column * QUARTER, 0), (QUARTER, width))
     w2 = swapped(quarter, 2, "w2")
     w_first = jnp.concatenate([quarter, w2], axis=0)
     w_second = swapped(w_first, 1, "w_second")
-    sib0 = to_sib(after(cot, state), "sib0")
     cot1 = across(cot, 1, "cot1")
     sib1 = to_sib(cot1, "sib1")
     cot2 = across(cot, 2, "cot2")
     sib2 = to_sib(after(cot2, far), "sib2")
-    cot3 = across(after(cot, near), 3, "cot3")
+    cot3 = across(after(cot, cot2), 3, "cot3")
     sib3 = to_sib(cot3, "sib3")
     cot_parts = [cot, sib0, cot1, sib1, cot2, sib2, cot3, sib3]
     d_packs = call(

time: 114 us -> 111 us (0.974); the launches traced: 112 us -> 111 us
  no operation moved by 1% of the time
where the time goes in v3:
time: 111 us
  waiting for transfers between devices  46.5 us (42%)
  starting transfers between devices  37.6 us (34%)
  Pallas kernels  22.3 us (20%)
  local copies, waits for them, and re-layouts  2.18 us (2%)
  other arithmetic  1.65 us (1%)
    ppermute x35, waiting for transfers between devices, sent(): return lax.ppermute(x, axis, pairs)  46.5 us
    ppermute x35, starting transfers between devices, sent(): return lax.ppermute(x, axis, pairs)  37.6 us
    pallas_call x10, Pallas kernels, call(): pl.pallas_call(kernel, out_shape=list(outs), grid=grid, in_specs=in_specs...  22.3 us
  transfers between devices with their start and end apart: 35, of which 12 were waited for; matrix products, arithmetic and copies ran while one was open for 2% of the time, Pallas kernels for 15%

profile of v3, /device:TPU:16, one launch (start us, length us, event | category | flops | bytes accessed | tf_op | source)
XLA Modules:
  0.0 111.1 jit_solution(14382808969386819095)
XLA Ops:
  7.5 1.6 %collective-permute-start.3 = (bf16[8,128,128]{2,1,0:T(8,128)(2,1)S(1)}, bf16[8,128,128]{2,1,0:T(8,128)(2,1)S(1)}, u32[]{:S(2)}, u32[]{:S(2)}) collective-permute-start(bf16[8,128,128]{2,1,0:T(8,128)(2,1)S(1)} %states.1), channel_id=1, source_target_pairs={{0,2},{1,3},{2,0},{3,1},{4,6},{5,7},{6,4},{7,5},{8,10},{9,11},{10,... | collective-permute-start | bytes 786440 | tf_op jit(solution)/shard_map/send_near/ppermute | solution.py:427
  9.6 5.8 %collective-permute-done.11.refs_4_.refs_8_ = bf16[128,2048]{1,0:T(8,128)(2,1)S(1)} collective-permute-done((bf16[128,2048]{1,0:T(8,128)(2,1)}, bf16[128,2048]{1,0:T(8,128)(2,1)S(1)}, u32[]{:S(2)}, u32[]{:S(2)}) %collective-permute-start.11) | collective-permute-done | bytes 524320 | tf_op jit(solution)/shard_map/send_cot2/ppermute | solution.py:427
  15.3 2.4 %collective-permute-start.13 = (bf16[128,2048]{1,0:T(8,128)(2,1)S(1)}, bf16[128,2048]{1,0:T(8,128)(2,1)S(1)}, u32[]{:S(2)}, u32[]{:S(2)}) collective-permute-start(bf16[128,2048]{1,0:T(8,128)(2,1)S(1)} %bitcast.36), channel_id=1, source_target_pairs={{0,24},{8,16},{16,8},{24,0},{1,25},{9,17},{17,9},{25,1},{2,26},{10... | collective-permute-start | bytes 1572872 | tf_op jit(solution)/shard_map/send_cot3/ppermute | solution.py:427
  21.0 2.9 %collective-permute-start.8 = (bf16[128,2048]{1,0:T(8,128)(2,1)S(1)}, bf16[128,2048]{1,0:T(8,128)(2,1)S(1)}, u32[]{:S(2)}, u32[]{:S(2)}) collective-permute-start(bf16[128,2048]{1,0:T(8,128)(2,1)S(1)} %pad_maximum_fusion.1.w_first), channel_id=1, source_target_pairs={{0,2},{1,3},{2,0},{3,1},{4,6},{5,7},{6,4},{7,5},{8,10},{9,11},{10,... | collective-permute-start | bytes 1572872 | tf_op jit(solution)/shard_map/send_w_second/ppermute | solution.py:427
  23.8 7.0 %collective-permute-done.4.far = bf16[8,128,128]{2,1,0:T(8,128)(2,1)S(1)} collective-permute-done((bf16[8,128,128]{2,1,0:T(8,128)(2,1)S(1)}, bf16[8,128,128]{2,1,0:T(8,128)(2,1)S(1)}, u32[]{:S(2)}, u32[]{:S(2)}) %collective-permute-start.4) | collective-permute-done | bytes 262176 | tf_op jit(solution)/shard_map/send_far/ppermute | solution.py:427
  31.4 2.4 %attend.1 = (f32[256,1024]{1,0:T(8,128)S(1)}, bf16[256,256]{1,0:T(8,128)(2,1)S(1)}, bf16[256,256]{1,0:T(8,128)(2,1)S(1)}, bf16[256,256]{1,0:T(8,128)(2,1)S(1)}, bf16[256,256]{1,0:T(8,128)(2,1)S(1)}) custom-call(s32[3]{0:T(128)S(1)} %pad_add_fusion.place, bf16[128,2048]{1,0:T(8,128)(2,1)S(1)} %bitcast.31, bf16[128,2048]{1,0:T(8,128)(2,1)S(1)} %collective-permute-done.2.q_sib, ...), custom_call_target="tpu_custom_call" | custom-call | tf_op jit(solution)/shard_map/attend/pallas_call | solution.py:180
  33.8 2.4 %collective-permute-start.16 = (bf16[256,256]{1,0:T(8,128)(2,1)S(1)}, bf16[256,256]{1,0:T(8,128)(2,1)S(1)}, u32[]{:S(2)}, u32[]{:S(2)}) collective-permute-start(bf16[256,256]{1,0:T(8,128)(2,1)S(1)} %get-tuple-element.66), channel_id=1, source_target_pairs={{0,24},{8,16},{16,8},{24,0},{1,25},{9,17},{17,9},{25,1},{2,26},{10... | collective-permute-start | bytes 393224 | tf_op jit(solution)/shard_map/send_n3/ppermute | solution.py:427
  36.2 5.0 %collective-permute-done.8.w_second = bf16[128,2048]{1,0:T(8,128)(2,1)S(1)} collective-permute-done((bf16[128,2048]{1,0:T(8,128)(2,1)S(1)}, bf16[128,2048]{1,0:T(8,128)(2,1)S(1)}, u32[]{:S(2)}, u32[]{:S(2)}) %collective-permute-start.8) | collective-permute-done | bytes 524320 | tf_op jit(solution)/shard_map/send_w_second/ppermute | solution.py:427
  44.2 2.8 %d_normed.1 = (bf16[256,256]{1,0:T(8,128)(2,1)S(1)}, bf16[256,256]{1,0:T(8,128)(2,1)S(1)}, bf16[256,256]{1,0:T(8,128)(2,1)S(1)}, bf16[256,256]{1,0:T(8,128)(2,1)S(1)}) custom-call(bf16[128,2048]{1,0:T(8,128)(2,1)S(1)} %pad_maximum_fusion.1.w_first, bf16[128,2048]{1,0:T(8,128)(2,1)S(1)} %collective-permute-done.8.w_second, bf16[128,2048]{1,0:T(8,128)(2,1)S(1)} %bitcast.38, ...), custom_call_target="tpu_custom_call" | custom-call | flops 1073741824 | bytes 5767168 | tf_op jit(solution)/shard_map/d_normed/pallas_call | solution.py:180
  47.6 3.3 %weight_terms.1 = (f32[128,2048]{1,0:T(8,128)S(1)}, bf16[128,2048]{1,0:T(8,128)(2,1)S(1)}) custom-call(bf16[256,256]{1,0:T(8,128)(2,1)S(1)} %get-tuple-element.55.refs_0_.n0, bf16[256,256]{1,0:T(8,128)(2,1)S(1)} %collective-permute-done.6.refs_1_.n1, bf16[256,256]{1,0:T(8,128)(2,1)S(1)} %collective-permute-done.15.refs_2_.n2, ...), custom_call_target="tpu_custom_call" | custom-call | flops 1073741824 | bytes 6291456 | tf_op jit(solution)/shard_map/weight_terms/pallas_call | solution.py:180
  51.0 2.6 %collective-permute-start.26 = (bf16[128,2048]{1,0:T(8,128)(2,1)S(1)}, bf16[128,2048]{1,0:T(8,128)(2,1)S(1)}, u32[]{:S(2)}, u32[]{:S(2)}) collective-permute-start(bf16[128,2048]{1,0:T(8,128)(2,1)S(1)} %get-tuple-element.68), channel_id=1, source_target_pairs={{0,2},{1,3},{2,0},{3,1},{4,6},{5,7},{6,4},{7,5},{8,10},{9,11},{10,... | collective-permute-start | bytes 1572872 | tf_op jit(solution)/shard_map/send_terms/ppermute | solution.py:427
  57.4 2.1 %mixed_terms.1 = (f32[128,2048]{1,0:T(8,128)S(1)}, bf16[128,2048]{1,0:T(8,128)(2,1)S(1)}, bf16[128,2048]{1,0:T(8,128)(2,1)S(1)}, bf16[128,2048]{1,0:T(8,128)(2,1)S(1)}) custom-call(bf16[256,256]{1,0:T(8,128)(2,1)S(1)} %get-tuple-element.55.refs_0_.n0, bf16[256,256]{1,0:T(8,128)(2,1)S(1)} %collective-permute-done.6.refs_1_.n1, ...), custom_call_target="tpu_custom_call" | custom-call | flops 1073741824 | bytes 5505024 | tf_op jit(solution)/shard_map/mixed_terms/pallas_call | solution.py:180
  59.5 1.5 %collective-permute-start.19 = (bf16[128,2048]{1,0:T(8,128)(2,1)S(1)}, bf16[128,2048]{1,0:T(8,128)(2,1)S(1)}, u32[]{:S(2)}, u32[]{:S(2)}) collective-permute-start(bf16[128,2048]{1,0:T(8,128)(2,1)S(1)} %get-tuple-element.72), channel_id=1, source_target_pairs={{0,8},{8,0},{16,24},{24,16},{1,9},{9,1},{17,25},{25,17},{2,10},{10... | collective-permute-start | bytes 1572872 | tf_op jit(solution)/shard_map/send_mixed1/ppermute | solution.py:427
  61.6 1.8 %collective-permute-done.23.r2 = bf16[256,256]{1,0:T(8,128)(2,1)S(1)} collective-permute-done((bf16[256,256]{1,0:T(8,128)(2,1)S(1)}, bf16[256,256]{1,0:T(8,128)(2,1)S(1)}, u32[]{:S(2)}, u32[]{:S(2)}) %collective-permute-start.23) | collective-permute-done | bytes 131104 | tf_op jit(solution)/shard_map/send_d2/ppermute | solution.py:427
  64.8 2.1 %d_attend.1 = (bf16[256,1024]{1,0:T(8,128)(2,1)S(1)}, bf16[8,128,128]{2,1,0:T(8,128)(2,1)S(1)}) custom-call(s32[3]{0:T(128)S(1)} %pad_add_fusion.place, bf16[128,2048]{1,0:T(8,128)(2,1)S(1)} %bitcast.32, bf16[128,2048]{1,0:T(8,128)(2,1)S(1)} %collective-permute-done.2.q_sib, f32[256,1024]{1,0:T(8,128)S(1)} %get-tuple-element.75.attended, ...), custom_call_target="tpu_custom_call" | custom-call | flops 134217728 | bytes 3416076 | tf_op jit(solution)/shard_map/d_attend/pallas_call | solution.py:180
  68.1 8.2 %collective-permute-done.27.near = bf16[8,128,128]{2,1,0:T(8,128)(2,1)S(1)} collective-permute-done((bf16[8,128,128]{2,1,0:T(8,128)(2,1)S(1)}, bf16[8,128,128]{2,1,0:T(8,128)(2,1)S(1)}, u32[]{:S(2)}, u32[]{:S(2)}) %collective-permute-start.27) | collective-permute-done | bytes 262176 | tf_op jit(solution)/shard_map/send_d_near/ppermute | solution.py:427
  76.3 5.2 %collective-permute-start.29 = (bf16[8,128,128]{2,1,0:T(8,128)(2,1)S(1)}, bf16[8,128,128]{2,1,0:T(8,128)(2,1)S(1)}, u32[]{:S(2)}, u32[]{:S(2)}) collective-permute-start(bf16[8,128,128]{2,1,0:T(8,128)(2,1)S(1)} %add.35), channel_id=1, source_target_pairs={{4,0},{5,1},{6,2},{7,3},{12,8},{13,9},{14,10},{15,11},{20,16},{21,... | collective-permute-start | bytes 786440 | tf_op jit(solution)/shard_map/send_d_far/ppermute | solution.py:427
  81.6 4.3 %collective-permute-done.21 = bf16[128,2048]{1,0:T(8,128)(2,1)S(1)} collective-permute-done((bf16[128,2048]{1,0:T(8,128)(2,1)S(1)}, bf16[128,2048]{1,0:T(8,128)(2,1)S(1)}, u32[]{:S(2)}, u32[]{:S(2)}) %collective-permute-start.21) | collective-permute-done | bytes 524320 | tf_op jit(solution)/shard_map/send_mixed3/ppermute | solution.py:427
  86.9 2.7 %inner.1 = (bf16[128,2048]{1,0:T(8,128)(2,1)S(1)}, f32[128,1024]{1,0:T(8,128)S(1)}, f32[128,1024]{1,0:T(8,128)S(1)}, bf16[3,128,1024]{2,1,0:T(8,128)(2,1)S(1)}) custom-call(s32[3]{0:T(128)S(1)} %pad_add_fusion.place, bf16[128,2048]{1,0:T(8,128)(2,1)S(1)} %bitcast.33, bf16[128,2048]{1,0:T(8,128)(2,1)S(1)} %collective-permute-done.2.q_sib, ...), custom_call_target="tpu_custom_call" | custom-call | flops 939524096 | bytes 6553612 | tf_op jit(solution)/shard_map/inner/pallas_call | solution.py:180
  89.8 1.6 %collective-permute-start.32 = (bf16[64,2048]{1,0:T(8,128)(2,1)S(1)}, bf16[64,2048]{1,0:T(8,128)(2,1)S(1)}, u32[]{:S(2)}, u32[]{:S(2)}) collective-permute-start(bf16[64,2048]{1,0:T(8,128)(2,1)S(1)} %fusion.t0), channel_id=1, source_target_pairs={{0,8},{8,0},{16,24},{24,16},{1,9},{9,1},{17,25},{25,17},{2,10},{10... | collective-permute-start | bytes 786440 | tf_op jit(solution)/shard_map/send_share1/ppermute | solution.py:427
  93.3 5.6 %collective-permute-done.32.t1 = bf16[64,2048]{1,0:T(8,128)(2,1)S(1)} collective-permute-done((bf16[64,2048]{1,0:T(8,128)(2,1)S(1)}, bf16[64,2048]{1,0:T(8,128)(2,1)S(1)}, u32[]{:S(2)}, u32[]{:S(2)}) %collective-permute-start.32) | collective-permute-done | bytes 262176 | tf_op jit(solution)/shard_map/send_share1/ppermute | solution.py:427
  99.0 6.4 %collective-permute-done.33.t2 = bf16[64,2048]{1,0:T(8,128)(2,1)S(1)} collective-permute-done((bf16[64,2048]{1,0:T(8,128)(2,1)S(1)}, bf16[64,2048]{1,0:T(8,128)(2,1)S(1)}, u32[]{:S(2)}, u32[]{:S(2)}) %collective-permute-start.33) | collective-permute-done | bytes 262176 | tf_op jit(solution)/shard_map/send_share2/ppermute | solution.py:427
  105.4 2.0 %grad_weight.1 = f32[256,2048]{1,0:T(8,128)} custom-call(s32[3]{0:T(128)S(1)} %pad_add_fusion.place, bf16[64,2048]{1,0:T(8,128)(2,1)S(1)} %fusion.t0, bf16[64,2048]{1,0:T(8,128)(2,1)S(1)} %collective-permute-done.32.t1, bf16[64,2048]{1,0:T(8,128)(2,1)S(1)} %collective-permute-done.33.t2, bf16[64,2048]{1,0:T(8,128)(2,1)S(1)} %collective-permute-done.34.t3), custom_call_target="tpu_custom_call" | custom-call | bytes 3145740 | tf_op jit(solution)/shard_map/grad_weight/pallas_call | solution.py:180
  108.8 2.3 %outer.1 = (bf16[128,2048]{1,0:T(8,128)(2,1)}, bf16[128,2048]{1,0:T(8,128)(2,1)}) custom-call(s32[3]{0:T(128)S(1)} %pad_add_fusion.place, bf16[128,2048]{1,0:T(8,128)(2,1)S(1)} %bitcast.24, bf16[128,2048]{1,0:T(8,128)(2,1)S(1)} %bitcast.29, bf16[8,128,128]{2,1,0:T(8,128)(2,1)S(1)} %collective-permute-done.27.near, ...), custom_call_target="tpu_custom_call" | custom-call | flops 134217728 | bytes 4980748 | tf_op jit(solution)/shard_map/outer/pallas_call | solution.py:180
  (86 shorter events, 26.2 us)
Async XLA Ops:
  1.2 14.1 %collective-permute-start.11 = (bf16[128,2048]{1,0:T(8,128)(2,1)}, bf16[128,2048]{1,0:T(8,128)(2,1)S(1)}, u32[]{:S(2)}, u32[]{:S(2)}) collective-permute-start(bf16[128,2048]{1,0:T(8,128)(2,1)} %bitcast.34), channel_id=1, source_target_pairs={{0,16},{8,24},{16,0},{24,8},{1,17},{9,25},{17,1},{25,9},{2,18},{10... | collective-permute-start | bytes 1572872 | tf_op jit(solution)/shard_map/send_cot2/ppermute | solution.py:427
  2.7 18.2 %collective-permute-start.9 = (bf16[128,2048]{1,0:T(8,128)(2,1)}, bf16[128,2048]{1,0:T(8,128)(2,1)S(1)}, u32[]{:S(2)}, u32[]{:S(2)}) collective-permute-start(bf16[128,2048]{1,0:T(8,128)(2,1)} %bitcast.35), channel_id=1, source_target_pairs={{0,8},{8,0},{16,24},{24,16},{1,9},{9,1},{17,25},{25,17},{2,10},{10... | collective-permute-start | bytes 1572872 | tf_op jit(solution)/shard_map/send_cot1/ppermute | solution.py:427
  7.5 11.2 %collective-permute-start.3 = (bf16[8,128,128]{2,1,0:T(8,128)(2,1)S(1)}, bf16[8,128,128]{2,1,0:T(8,128)(2,1)S(1)}, u32[]{:S(2)}, u32[]{:S(2)}) collective-permute-start(bf16[8,128,128]{2,1,0:T(8,128)(2,1)S(1)} %states.1), channel_id=1, source_target_pairs={{0,2},{1,3},{2,0},{3,1},{4,6},{5,7},{6,4},{7,5},{8,10},{9,11},{10,... | collective-permute-start | bytes 786440 | tf_op jit(solution)/shard_map/send_near/ppermute | solution.py:427
  9.2 11.7 %collective-permute-start.7 = (bf16[64,2048]{1,0:T(8,128)(2,1)S(1)}, bf16[64,2048]{1,0:T(8,128)(2,1)S(1)}, u32[]{:S(2)}, u32[]{:S(2)}) collective-permute-start(bf16[64,2048]{1,0:T(8,128)(2,1)S(1)} %constant_dynamic-slice_fusion), channel_id=1, source_target_pairs={{0,4},{1,5},{2,6},{3,7},{4,0},{5,1},{6,2},{7,3},{8,12},{9,13},{10,... | collective-permute-start | bytes 786440 | tf_op jit(solution)/shard_map/send_w2/ppermute | solution.py:427
  15.3 15.5 %collective-permute-start.13 = (bf16[128,2048]{1,0:T(8,128)(2,1)S(1)}, bf16[128,2048]{1,0:T(8,128)(2,1)S(1)}, u32[]{:S(2)}, u32[]{:S(2)}) collective-permute-start(bf16[128,2048]{1,0:T(8,128)(2,1)S(1)} %bitcast.36), channel_id=1, source_target_pairs={{0,24},{8,16},{16,8},{24,0},{1,25},{9,17},{17,9},{25,1},{2,26},{10... | collective-permute-start | bytes 1572872 | tf_op jit(solution)/shard_map/send_cot3/ppermute | solution.py:427
  17.8 13.6 %collective-permute-start.2 = (bf16[128,2048]{1,0:T(8,128)(2,1)S(1)}, bf16[128,2048]{1,0:T(8,128)(2,1)S(1)}, u32[]{:S(2)}, u32[]{:S(2)}) collective-permute-start(bf16[128,2048]{1,0:T(8,128)(2,1)S(1)} %bitcast.30), channel_id=1, source_target_pairs={{0,1},{1,0},{2,3},{3,2},{4,5},{5,4},{6,7},{7,6},{8,9},{9,8},{10,11... | collective-permute-start | bytes 1572872 | tf_op jit(solution)/shard_map/send_query/ppermute | solution.py:427
  18.8 12.1 %collective-permute-start.4 = (bf16[8,128,128]{2,1,0:T(8,128)(2,1)S(1)}, bf16[8,128,128]{2,1,0:T(8,128)(2,1)S(1)}, u32[]{:S(2)}, u32[]{:S(2)}) collective-permute-start(bf16[8,128,128]{2,1,0:T(8,128)(2,1)S(1)} %add.30), channel_id=1, source_target_pairs={{0,4},{1,5},{2,6},{3,7},{8,12},{9,13},{10,14},{11,15},{16,20},{17,... | collective-permute-start | bytes 786440 | tf_op jit(solution)/shard_map/send_far/ppermute | solution.py:427
  20.9 12.9 %collective-permute-start.5 = (bf16[128,2048]{1,0:T(8,128)(2,1)S(1)}, bf16[128,2048]{1,0:T(8,128)(2,1)S(1)}, u32[]{:S(2)}, u32[]{:S(2)}) collective-permute-start(bf16[128,2048]{1,0:T(8,128)(2,1)S(1)} %bitcast.37), channel_id=1, source_target_pairs={{0,1},{1,0},{2,3},{3,2},{4,5},{5,4},{6,7},{7,6},{8,9},{9,8},{10,11... | collective-permute-start | bytes 1572872 | tf_op jit(solution)/shard_map/send_sib0/ppermute | solution.py:427
  21.0 20.2 %collective-permute-start.8 = (bf16[128,2048]{1,0:T(8,128)(2,1)S(1)}, bf16[128,2048]{1,0:T(8,128)(2,1)S(1)}, u32[]{:S(2)}, u32[]{:S(2)}) collective-permute-start(bf16[128,2048]{1,0:T(8,128)(2,1)S(1)} %pad_maximum_fusion.1.w_first), channel_id=1, source_target_pairs={{0,2},{1,3},{2,0},{3,1},{4,6},{5,7},{6,4},{7,5},{8,10},{9,11},{10,... | collective-permute-start | bytes 1572872 | tf_op jit(solution)/shard_map/send_w_second/ppermute | solution.py:427
  30.8 11.8 %collective-permute-start.10 = (bf16[128,2048]{1,0:T(8,128)(2,1)S(1)}, bf16[128,2048]{1,0:T(8,128)(2,1)S(1)}, u32[]{:S(2)}, u32[]{:S(2)}) collective-permute-start(bf16[128,2048]{1,0:T(8,128)(2,1)S(1)} %collective-permute-done.9.refs_2_.refs_6_), channel_id=1, source_target_pairs={{0,1},{1,0},{2,3},{3,2},{4,5},{5,4},{6,7},{7,6},{8,9},{9,8},{10,11... | collective-permute-start | bytes 1572872 | tf_op jit(solution)/shard_map/send_sib1/ppermute | solution.py:427
  30.8 13.4 %collective-permute-start.12 = (bf16[128,2048]{1,0:T(8,128)(2,1)S(1)}, bf16[128,2048]{1,0:T(8,128)(2,1)S(1)}, u32[]{:S(2)}, u32[]{:S(2)}) collective-permute-start(bf16[128,2048]{1,0:T(8,128)(2,1)S(1)} %collective-permute-done.11.refs_4_.refs_8_), channel_id=1, source_target_pairs={{0,1},{1,0},{2,3},{3,2},{4,5},{5,4},{6,7},{7,6},{8,9},{9,8},{10,11... | collective-permute-start | bytes 1572872 | tf_op jit(solution)/shard_map/send_sib2/ppermute | solution.py:427
  31.4 12.9 %collective-permute-start.14 = (bf16[128,2048]{1,0:T(8,128)(2,1)S(1)}, bf16[128,2048]{1,0:T(8,128)(2,1)S(1)}, u32[]{:S(2)}, u32[]{:S(2)}) collective-permute-start(bf16[128,2048]{1,0:T(8,128)(2,1)S(1)} %collective-permute-done.13.refs_6_.refs_10_), channel_id=1, source_target_pairs={{0,1},{1,0},{2,3},{3,2},{4,5},{5,4},{6,7},{7,6},{8,9},{9,8},{10,11... | collective-permute-start | bytes 1572872 | tf_op jit(solution)/shard_map/send_sib3/ppermute | solution.py:427
  33.8 13.2 %collective-permute-start.16 = (bf16[256,256]{1,0:T(8,128)(2,1)S(1)}, bf16[256,256]{1,0:T(8,128)(2,1)S(1)}, u32[]{:S(2)}, u32[]{:S(2)}) collective-permute-start(bf16[256,256]{1,0:T(8,128)(2,1)S(1)} %get-tuple-element.66), channel_id=1, source_target_pairs={{0,24},{8,16},{16,8},{24,0},{1,25},{9,17},{17,9},{25,1},{2,26},{10... | collective-permute-start | bytes 393224 | tf_op jit(solution)/shard_map/send_n3/ppermute | solution.py:427
  51.0 15.9 %collective-permute-start.26 = (bf16[128,2048]{1,0:T(8,128)(2,1)S(1)}, bf16[128,2048]{1,0:T(8,128)(2,1)S(1)}, u32[]{:S(2)}, u32[]{:S(2)}) collective-permute-start(bf16[128,2048]{1,0:T(8,128)(2,1)S(1)} %get-tuple-element.68), channel_id=1, source_target_pairs={{0,2},{1,3},{2,0},{3,1},{4,6},{5,7},{6,4},{7,5},{8,10},{9,11},{10,... | collective-permute-start | bytes 1572872 | tf_op jit(solution)/shard_map/send_terms/ppermute | solution.py:427
  59.5 22.0 %collective-permute-start.19 = (bf16[128,2048]{1,0:T(8,128)(2,1)S(1)}, bf16[128,2048]{1,0:T(8,128)(2,1)S(1)}, u32[]{:S(2)}, u32[]{:S(2)}) collective-permute-start(bf16[128,2048]{1,0:T(8,128)(2,1)S(1)} %get-tuple-element.72), channel_id=1, source_target_pairs={{0,8},{8,0},{16,24},{24,16},{1,9},{9,1},{17,25},{25,17},{2,10},{10... | collective-permute-start | bytes 1572872 | tf_op jit(solution)/shard_map/send_mixed1/ppermute | solution.py:427
  61.1 20.4 %collective-permute-start.20 = (bf16[128,2048]{1,0:T(8,128)(2,1)S(1)}, bf16[128,2048]{1,0:T(8,128)(2,1)S(1)}, u32[]{:S(2)}, u32[]{:S(2)}) collective-permute-start(bf16[128,2048]{1,0:T(8,128)(2,1)S(1)} %get-tuple-element.73), channel_id=1, source_target_pairs={{0,16},{8,24},{16,0},{24,8},{1,17},{9,25},{17,1},{25,9},{2,18},{10... | collective-permute-start | bytes 1572872 | tf_op jit(solution)/shard_map/send_mixed2/ppermute | solution.py:427
  63.4 22.4 %collective-permute-start.21 = (bf16[128,2048]{1,0:T(8,128)(2,1)S(1)}, bf16[128,2048]{1,0:T(8,128)(2,1)S(1)}, u32[]{:S(2)}, u32[]{:S(2)}) collective-permute-start(bf16[128,2048]{1,0:T(8,128)(2,1)S(1)} %get-tuple-element.74), channel_id=1, source_target_pairs={{0,24},{8,16},{16,8},{24,0},{1,25},{9,17},{17,9},{25,1},{2,26},{10... | collective-permute-start | bytes 1572872 | tf_op jit(solution)/shard_map/send_mixed3/ppermute | solution.py:427
  68.0 21.6 %collective-permute-start.31 = (bf16[64,2048]{1,0:T(8,128)(2,1)S(1)}, bf16[64,2048]{1,0:T(8,128)(2,1)S(1)}, u32[]{:S(2)}, u32[]{:S(2)}) collective-permute-start(bf16[64,2048]{1,0:T(8,128)(2,1)S(1)} %slice.35), channel_id=1, source_target_pairs={{0,4},{1,5},{2,6},{3,7},{4,0},{5,1},{6,2},{7,3},{8,12},{9,13},{10,... | collective-permute-start | bytes 786440 | tf_op jit(solution)/shard_map/send_pair_terms/ppermute | solution.py:427
  76.3 17.0 %collective-permute-start.29 = (bf16[8,128,128]{2,1,0:T(8,128)(2,1)S(1)}, bf16[8,128,128]{2,1,0:T(8,128)(2,1)S(1)}, u32[]{:S(2)}, u32[]{:S(2)}) collective-permute-start(bf16[8,128,128]{2,1,0:T(8,128)(2,1)S(1)} %add.35), channel_id=1, source_target_pairs={{4,0},{5,1},{6,2},{7,3},{12,8},{13,9},{14,10},{15,11},{20,16},{21,... | collective-permute-start | bytes 786440 | tf_op jit(solution)/shard_map/send_d_far/ppermute | solution.py:427
  89.6 17.7 %collective-permute-start.25 = (bf16[3,128,1024]{2,1,0:T(8,128)(2,1)S(1)}, bf16[3,128,1024]{2,1,0:T(8,128)(2,1)S(1)}, u32[]{:S(2)}, u32[]{:S(2)}) collective-permute-start(bf16[3,128,1024]{2,1,0:T(8,128)(2,1)S(1)} %get-tuple-element.81), channel_id=1, source_target_pairs={{0,1},{1,0},{2,3},{3,2},{4,5},{5,4},{6,7},{7,6},{8,9},{9,8},{10,11... | collective-permute-start | bytes 2359304 | tf_op jit(solution)/shard_map/send_parts/ppermute | solution.py:427
  91.3 14.0 %collective-permute-start.33 = (bf16[64,2048]{1,0:T(8,128)(2,1)S(1)}, bf16[64,2048]{1,0:T(8,128)(2,1)S(1)}, u32[]{:S(2)}, u32[]{:S(2)}) collective-permute-start(bf16[64,2048]{1,0:T(8,128)(2,1)S(1)} %fusion.t0), channel_id=1, source_target_pairs={{0,16},{8,24},{16,0},{24,8},{1,17},{9,25},{17,1},{25,9},{2,18},{10... | collective-permute-start | bytes 786440 | tf_op jit(solution)/shard_map/send_share2/ppermute | solution.py:427
  91.8 13.5 %collective-permute-start.34 = (bf16[64,2048]{1,0:T(8,128)(2,1)S(1)}, bf16[64,2048]{1,0:T(8,128)(2,1)S(1)}, u32[]{:S(2)}, u32[]{:S(2)}) collective-permute-start(bf16[64,2048]{1,0:T(8,128)(2,1)S(1)} %fusion.t0), channel_id=1, source_target_pairs={{0,24},{8,16},{16,8},{24,0},{1,25},{9,17},{17,9},{25,1},{2,26},{10... | collective-permute-start | bytes 786440 | tf_op jit(solution)/shard_map/send_share3/ppermute | solution.py:427
  93.3 15.4 %collective-permute-start.28 = (bf16[8,128,128]{2,1,0:T(8,128)(2,1)S(1)}, bf16[8,128,128]{2,1,0:T(8,128)(2,1)S(1)}, u32[]{:S(2)}, u32[]{:S(2)}) collective-permute-start(bf16[8,128,128]{2,1,0:T(8,128)(2,1)S(1)} %collective-permute-done.27.near), channel_id=1, source_target_pairs={{0,1},{1,0},{2,3},{3,2},{4,5},{5,4},{6,7},{7,6},{8,9},{9,8},{10,11... | collective-permute-start | bytes 786440 | tf_op jit(solution)/shard_map/send_d_near_sib/ppermute | solution.py:427
  99.0 9.8 %collective-permute-start.30 = (bf16[8,128,128]{2,1,0:T(8,128)(2,1)S(1)}, bf16[8,128,128]{2,1,0:T(8,128)(2,1)S(1)}, u32[]{:S(2)}, u32[]{:S(2)}) collective-permute-start(bf16[8,128,128]{2,1,0:T(8,128)(2,1)S(1)} %collective-permute-done.29.far), channel_id=1, source_target_pairs={{0,1},{1,0},{2,3},{3,2},{4,5},{5,4},{6,7},{7,6},{8,9},{9,8},{10,11... | collective-permute-start | bytes 786440 | tf_op jit(solution)/shard_map/send_d_far_sib/ppermute | solution.py:427
  (19 other events, 163.3 us)

commit v4 on v3

--- a/solution.py
+++ b/solution.py
@@ -399,6 +399,11 @@
         out[pl.ds(pl.multiple_of(column * QUARTER, QUARTER), QUARTER), :] = t[...].astype(f32) * scale
 
 
+def finish_kernel(place, got, held, k_own, v_own, near, near_sib, far, far_sib, part_k, part_v, gq, gk, gv):
+    fill_kernel(place, got, held, gq)
+    outer_kernel(place, k_own, v_own, near, near_sib, far, far_sib, part_k, part_v, got, gk, gv)
+
+
 def after(x, *earlier):
     return lax.optimization_barrier((x, *earlier))[0]
 
@@ -532,20 +537,12 @@
         14 * state_flops,
     )
     parts_got = to_sib(parts_sent, "parts")
-    grad_queries = call(fill_kernel, [full], "fill_q", (place, parts_got, gq), 0)[0]
     terms = swapped(given, 1, "terms")
     d_near = swapped(after(d_state, terms), 1, "d_near")
     d_near_sib = to_sib(d_near, "d_near_sib")
     d_pair_state = d_state + d_near
     d_far = halfway(d_pair_state, -2, "d_far")
     d_far_sib = to_sib(d_far, "d_far_sib")
-    grad_kv = call(
-        outer_kernel,
-        [full, full],
-        "outer",
-        (place, key, value, d_near, d_near_sib, d_far, d_far_sib, part_k, part_v, parts_got),
-        2 * state_flops,
-    )
     pair = kept + terms.astype(f32)
     pair_terms = after(swapped(pair[QUARTER:].astype(bf16), 2, "pair_terms"), gq)
     share = (pair[:QUARTER] + pair_terms.astype(f32)).astype(bf16)
@@ -553,6 +550,13 @@
     share2 = across(share, 2, "share2")
     share3 = across(share, 3, "share3")
     scale = 1.0 / math.sqrt(lax.axis_size("dp") * lax.axis_size("ctx") * half)
+    grad_queries, *grad_kv = call(
+        finish_kernel,
+        [full, full, full],
+        "finish",
+        (place, parts_got, gq, key, value, d_near, d_near_sib, d_far, d_far_sib, part_k, part_v),
+        2 * state_flops,
+    )
     grad_weight = call(
         functools.partial(gathered_kernel, scale),
         [like(out_weight.shape, f32)],

time: 111 us -> 110 us (level)
  Pallas kernels: 22.3 us -> 21.1 us
    pallas_call x10 -> x9, Pallas kernels: 22.3 us -> 21.1 us  [call(): pl.pallas_call(kernel, out_shape=list(outs), grid=grid, in_specs=in_specs...]
  transfers between devices with their start and end apart: 35 -> 35, of which waited for: 12 -> 12; matrix products, arithmetic and copies ran while one was open for 2% -> 2% of each run, Pallas kernels for 15% -> 14%
where the time goes in v4:
time: 110 us
  waiting for transfers between devices  46.4 us (42%)
  starting transfers between devices  37.6 us (34%)
  Pallas kernels  21.1 us (19%)
  local copies, waits for them, and re-layouts  2.18 us (2%)
  other arithmetic  1.66 us (2%)
    ppermute x35, waiting for transfers between devices, sent(): return lax.ppermute(x, axis, pairs)  46.4 us
    ppermute x35, starting transfers between devices, sent(): return lax.ppermute(x, axis, pairs)  37.6 us
    pallas_call x9, Pallas kernels, call(): pl.pallas_call(kernel, out_shape=list(outs), grid=grid, in_specs=in_specs...  21.1 us
  transfers between devices with their start and end apart: 35, of which 12 were waited for; matrix products, arithmetic and copies ran while one was open for 2% of the time, Pallas kernels for 14%

profile of v4, /device:TPU:16, one launch (start us, length us, event | category | flops | bytes accessed | tf_op | source)
XLA Modules:
  0.0 109.9 jit_solution(17962043903181952566)
XLA Ops:
  7.5 1.6 %collective-permute-start.3 = (bf16[8,128,128]{2,1,0:T(8,128)(2,1)S(1)}, bf16[8,128,128]{2,1,0:T(8,128)(2,1)S(1)}, u32[]{:S(2)}, u32[]{:S(2)}) collective-permute-start(bf16[8,128,128]{2,1,0:T(8,128)(2,1)S(1)} %states.1), channel_id=1, source_target_pairs={{0,2},{1,3},{2,0},{3,1},{4,6},{5,7},{6,4},{7,5},{8,10},{9,11},{10,... | collective-permute-start | bytes 786440 | tf_op jit(solution)/shard_map/send_near/ppermute | solution.py:432
  9.6 5.8 %collective-permute-done.11.refs_4_.refs_8_ = bf16[128,2048]{1,0:T(8,128)(2,1)S(1)} collective-permute-done((bf16[128,2048]{1,0:T(8,128)(2,1)}, bf16[128,2048]{1,0:T(8,128)(2,1)S(1)}, u32[]{:S(2)}, u32[]{:S(2)}) %collective-permute-start.11) | collective-permute-done | bytes 524320 | tf_op jit(solution)/shard_map/send_cot2/ppermute | solution.py:432
  15.3 2.4 %collective-permute-start.13 = (bf16[128,2048]{1,0:T(8,128)(2,1)S(1)}, bf16[128,2048]{1,0:T(8,128)(2,1)S(1)}, u32[]{:S(2)}, u32[]{:S(2)}) collective-permute-start(bf16[128,2048]{1,0:T(8,128)(2,1)S(1)} %bitcast.36), channel_id=1, source_target_pairs={{0,24},{8,16},{16,8},{24,0},{1,25},{9,17},{17,9},{25,1},{2,26},{10... | collective-permute-start | bytes 1572872 | tf_op jit(solution)/shard_map/send_cot3/ppermute | solution.py:432
  21.0 2.9 %collective-permute-start.8 = (bf16[128,2048]{1,0:T(8,128)(2,1)S(1)}, bf16[128,2048]{1,0:T(8,128)(2,1)S(1)}, u32[]{:S(2)}, u32[]{:S(2)}) collective-permute-start(bf16[128,2048]{1,0:T(8,128)(2,1)S(1)} %pad_maximum_fusion.1.w_first), channel_id=1, source_target_pairs={{0,2},{1,3},{2,0},{3,1},{4,6},{5,7},{6,4},{7,5},{8,10},{9,11},{10,... | collective-permute-start | bytes 1572872 | tf_op jit(solution)/shard_map/send_w_second/ppermute | solution.py:432
  23.8 7.0 %collective-permute-done.4.far = bf16[8,128,128]{2,1,0:T(8,128)(2,1)S(1)} collective-permute-done((bf16[8,128,128]{2,1,0:T(8,128)(2,1)S(1)}, bf16[8,128,128]{2,1,0:T(8,128)(2,1)S(1)}, u32[]{:S(2)}, u32[]{:S(2)}) %collective-permute-start.4) | collective-permute-done | bytes 262176 | tf_op jit(solution)/shard_map/send_far/ppermute | solution.py:432
  31.4 2.4 %attend.1 = (f32[256,1024]{1,0:T(8,128)S(1)}, bf16[256,256]{1,0:T(8,128)(2,1)S(1)}, bf16[256,256]{1,0:T(8,128)(2,1)S(1)}, bf16[256,256]{1,0:T(8,128)(2,1)S(1)}, bf16[256,256]{1,0:T(8,128)(2,1)S(1)}) custom-call(s32[3]{0:T(128)S(1)} %pad_add_fusion.place, bf16[128,2048]{1,0:T(8,128)(2,1)S(1)} %bitcast.31, bf16[128,2048]{1,0:T(8,128)(2,1)S(1)} %collective-permute-done.2.q_sib, ...), custom_call_target="tpu_custom_call" | custom-call | tf_op jit(solution)/shard_map/attend/pallas_call | solution.py:180
  33.8 2.4 %collective-permute-start.16 = (bf16[256,256]{1,0:T(8,128)(2,1)S(1)}, bf16[256,256]{1,0:T(8,128)(2,1)S(1)}, u32[]{:S(2)}, u32[]{:S(2)}) collective-permute-start(bf16[256,256]{1,0:T(8,128)(2,1)S(1)} %get-tuple-element.67), channel_id=1, source_target_pairs={{0,24},{8,16},{16,8},{24,0},{1,25},{9,17},{17,9},{25,1},{2,26},{10... | collective-permute-start | bytes 393224 | tf_op jit(solution)/shard_map/send_n3/ppermute | solution.py:432
  36.2 5.0 %collective-permute-done.8.w_second = bf16[128,2048]{1,0:T(8,128)(2,1)S(1)} collective-permute-done((bf16[128,2048]{1,0:T(8,128)(2,1)S(1)}, bf16[128,2048]{1,0:T(8,128)(2,1)S(1)}, u32[]{:S(2)}, u32[]{:S(2)}) %collective-permute-start.8) | collective-permute-done | bytes 524320 | tf_op jit(solution)/shard_map/send_w_second/ppermute | solution.py:432
  44.2 2.8 %d_normed.1 = (bf16[256,256]{1,0:T(8,128)(2,1)S(1)}, bf16[256,256]{1,0:T(8,128)(2,1)S(1)}, bf16[256,256]{1,0:T(8,128)(2,1)S(1)}, bf16[256,256]{1,0:T(8,128)(2,1)S(1)}) custom-call(bf16[128,2048]{1,0:T(8,128)(2,1)S(1)} %pad_maximum_fusion.1.w_first, bf16[128,2048]{1,0:T(8,128)(2,1)S(1)} %collective-permute-done.8.w_second, bf16[128,2048]{1,0:T(8,128)(2,1)S(1)} %bitcast.38, ...), custom_call_target="tpu_custom_call" | custom-call | flops 1073741824 | bytes 5767168 | tf_op jit(solution)/shard_map/d_normed/pallas_call | solution.py:180
  47.6 3.3 %weight_terms.1 = (f32[128,2048]{1,0:T(8,128)S(1)}, bf16[128,2048]{1,0:T(8,128)(2,1)S(1)}) custom-call(bf16[256,256]{1,0:T(8,128)(2,1)S(1)} %get-tuple-element.56.refs_0_.n0, bf16[256,256]{1,0:T(8,128)(2,1)S(1)} %collective-permute-done.6.refs_1_.n1, bf16[256,256]{1,0:T(8,128)(2,1)S(1)} %collective-permute-done.15.refs_2_.n2, ...), custom_call_target="tpu_custom_call" | custom-call | flops 1073741824 | bytes 6291456 | tf_op jit(solution)/shard_map/weight_terms/pallas_call | solution.py:180
  51.0 2.6 %collective-permute-start.26 = (bf16[128,2048]{1,0:T(8,128)(2,1)S(1)}, bf16[128,2048]{1,0:T(8,128)(2,1)S(1)}, u32[]{:S(2)}, u32[]{:S(2)}) collective-permute-start(bf16[128,2048]{1,0:T(8,128)(2,1)S(1)} %get-tuple-element.69), channel_id=1, source_target_pairs={{0,2},{1,3},{2,0},{3,1},{4,6},{5,7},{6,4},{7,5},{8,10},{9,11},{10,... | collective-permute-start | bytes 1572872 | tf_op jit(solution)/shard_map/send_terms/ppermute | solution.py:432
  57.4 2.1 %mixed_terms.1 = (f32[128,2048]{1,0:T(8,128)S(1)}, bf16[128,2048]{1,0:T(8,128)(2,1)S(1)}, bf16[128,2048]{1,0:T(8,128)(2,1)S(1)}, bf16[128,2048]{1,0:T(8,128)(2,1)S(1)}) custom-call(bf16[256,256]{1,0:T(8,128)(2,1)S(1)} %get-tuple-element.56.refs_0_.n0, bf16[256,256]{1,0:T(8,128)(2,1)S(1)} %collective-permute-done.6.refs_1_.n1, ...), custom_call_target="tpu_custom_call" | custom-call | flops 1073741824 | bytes 5505024 | tf_op jit(solution)/shard_map/mixed_terms/pallas_call | solution.py:180
  59.5 1.5 %collective-permute-start.19 = (bf16[128,2048]{1,0:T(8,128)(2,1)S(1)}, bf16[128,2048]{1,0:T(8,128)(2,1)S(1)}, u32[]{:S(2)}, u32[]{:S(2)}) collective-permute-start(bf16[128,2048]{1,0:T(8,128)(2,1)S(1)} %get-tuple-element.73), channel_id=1, source_target_pairs={{0,8},{8,0},{16,24},{24,16},{1,9},{9,1},{17,25},{25,17},{2,10},{10... | collective-permute-start | bytes 1572872 | tf_op jit(solution)/shard_map/send_mixed1/ppermute | solution.py:432
  61.6 1.8 %collective-permute-done.23.r2 = bf16[256,256]{1,0:T(8,128)(2,1)S(1)} collective-permute-done((bf16[256,256]{1,0:T(8,128)(2,1)S(1)}, bf16[256,256]{1,0:T(8,128)(2,1)S(1)}, u32[]{:S(2)}, u32[]{:S(2)}) %collective-permute-start.23) | collective-permute-done | bytes 131104 | tf_op jit(solution)/shard_map/send_d2/ppermute | solution.py:432
  64.8 2.1 %d_attend.1 = (bf16[256,1024]{1,0:T(8,128)(2,1)S(1)}, bf16[8,128,128]{2,1,0:T(8,128)(2,1)S(1)}) custom-call(s32[3]{0:T(128)S(1)} %pad_add_fusion.place, bf16[128,2048]{1,0:T(8,128)(2,1)S(1)} %bitcast.32, bf16[128,2048]{1,0:T(8,128)(2,1)S(1)} %collective-permute-done.2.q_sib, f32[256,1024]{1,0:T(8,128)S(1)} %get-tuple-element.76.attended, ...), custom_call_target="tpu_custom_call" | custom-call | flops 134217728 | bytes 3416076 | tf_op jit(solution)/shard_map/d_attend/pallas_call | solution.py:180
  68.1 8.1 %collective-permute-done.27.near = bf16[8,128,128]{2,1,0:T(8,128)(2,1)S(1)} collective-permute-done((bf16[8,128,128]{2,1,0:T(8,128)(2,1)S(1)}, bf16[8,128,128]{2,1,0:T(8,128)(2,1)S(1)}, u32[]{:S(2)}, u32[]{:S(2)}) %collective-permute-start.27) | collective-permute-done | bytes 262176 | tf_op jit(solution)/shard_map/send_d_near/ppermute | solution.py:432
  76.3 5.2 %collective-permute-start.29 = (bf16[8,128,128]{2,1,0:T(8,128)(2,1)S(1)}, bf16[8,128,128]{2,1,0:T(8,128)(2,1)S(1)}, u32[]{:S(2)}, u32[]{:S(2)}) collective-permute-start(bf16[8,128,128]{2,1,0:T(8,128)(2,1)S(1)} %add.35), channel_id=1, source_target_pairs={{4,0},{5,1},{6,2},{7,3},{12,8},{13,9},{14,10},{15,11},{20,16},{21,... | collective-permute-start | bytes 786440 | tf_op jit(solution)/shard_map/send_d_far/ppermute | solution.py:432
  81.6 4.3 %collective-permute-done.21 = bf16[128,2048]{1,0:T(8,128)(2,1)S(1)} collective-permute-done((bf16[128,2048]{1,0:T(8,128)(2,1)S(1)}, bf16[128,2048]{1,0:T(8,128)(2,1)S(1)}, u32[]{:S(2)}, u32[]{:S(2)}) %collective-permute-start.21) | collective-permute-done | bytes 524320 | tf_op jit(solution)/shard_map/send_mixed3/ppermute | solution.py:432
  86.9 2.7 %inner.1 = (bf16[128,2048]{1,0:T(8,128)(2,1)S(1)}, f32[128,1024]{1,0:T(8,128)S(1)}, f32[128,1024]{1,0:T(8,128)S(1)}, bf16[3,128,1024]{2,1,0:T(8,128)(2,1)S(1)}) custom-call(s32[3]{0:T(128)S(1)} %pad_add_fusion.place, bf16[128,2048]{1,0:T(8,128)(2,1)S(1)} %bitcast.33, bf16[128,2048]{1,0:T(8,128)(2,1)S(1)} %collective-permute-done.2.q_sib, ...), custom_call_target="tpu_custom_call" | custom-call | flops 939524096 | bytes 6553612 | tf_op jit(solution)/shard_map/inner/pallas_call | solution.py:180
  89.8 1.6 %collective-permute-start.32 = (bf16[64,2048]{1,0:T(8,128)(2,1)S(1)}, bf16[64,2048]{1,0:T(8,128)(2,1)S(1)}, u32[]{:S(2)}, u32[]{:S(2)}) collective-permute-start(bf16[64,2048]{1,0:T(8,128)(2,1)S(1)} %fusion.t0), channel_id=1, source_target_pairs={{0,8},{8,0},{16,24},{24,16},{1,9},{9,1},{17,25},{25,17},{2,10},{10... | collective-permute-start | bytes 786440 | tf_op jit(solution)/shard_map/send_share1/ppermute | solution.py:432
  93.3 5.6 %collective-permute-done.32.t1 = bf16[64,2048]{1,0:T(8,128)(2,1)S(1)} collective-permute-done((bf16[64,2048]{1,0:T(8,128)(2,1)S(1)}, bf16[64,2048]{1,0:T(8,128)(2,1)S(1)}, u32[]{:S(2)}, u32[]{:S(2)}) %collective-permute-start.32) | collective-permute-done | bytes 262176 | tf_op jit(solution)/shard_map/send_share1/ppermute | solution.py:432
  99.0 6.4 %collective-permute-done.33.t2 = bf16[64,2048]{1,0:T(8,128)(2,1)S(1)} collective-permute-done((bf16[64,2048]{1,0:T(8,128)(2,1)S(1)}, bf16[64,2048]{1,0:T(8,128)(2,1)S(1)}, u32[]{:S(2)}, u32[]{:S(2)}) %collective-permute-start.33) | collective-permute-done | bytes 262176 | tf_op jit(solution)/shard_map/send_share2/ppermute | solution.py:432
  105.4 2.0 %grad_weight.1 = f32[256,2048]{1,0:T(8,128)} custom-call(s32[3]{0:T(128)S(1)} %pad_add_fusion.place, bf16[64,2048]{1,0:T(8,128)(2,1)S(1)} %fusion.t0, bf16[64,2048]{1,0:T(8,128)(2,1)S(1)} %collective-permute-done.32.t1, bf16[64,2048]{1,0:T(8,128)(2,1)S(1)} %collective-permute-done.33.t2, bf16[64,2048]{1,0:T(8,128)(2,1)S(1)} %collective-permute-done.34.t3), custom_call_target="tpu_custom_call" | custom-call | bytes 3145740 | tf_op jit(solution)/shard_map/grad_weight/pallas_call | solution.py:180
  107.4 2.5 %finish.1 = (bf16[128,2048]{1,0:T(8,128)(2,1)}, bf16[128,2048]{1,0:T(8,128)(2,1)}, bf16[128,2048]{1,0:T(8,128)(2,1)}) custom-call(s32[3]{0:T(128)S(1)} %pad_add_fusion.place, bf16[3,128,1024]{2,1,0:T(8,128)(2,1)S(1)} %collective-permute-done.25.got, bf16[128,2048]{1,0:T(8,128)(2,1)S(1)} %get-tuple-element.83.held, bf16[128,2048]{1,0:T(8,128)(2,1)S(1)} %bitcast.24, ...), custom_call_target="tpu_custom_call" | custom-call | flops 134217728 | bytes 6029324 | tf_op jit(solution)/shard_map/finish/pallas_call | solution.py:180
  (85 shorter events, 24.8 us)
Async XLA Ops:
  1.2 14.1 %collective-permute-start.11 = (bf16[128,2048]{1,0:T(8,128)(2,1)}, bf16[128,2048]{1,0:T(8,128)(2,1)S(1)}, u32[]{:S(2)}, u32[]{:S(2)}) collective-permute-start(bf16[128,2048]{1,0:T(8,128)(2,1)} %bitcast.34), channel_id=1, source_target_pairs={{0,16},{8,24},{16,0},{24,8},{1,17},{9,25},{17,1},{25,9},{2,18},{10... | collective-permute-start | bytes 1572872 | tf_op jit(solution)/shard_map/send_cot2/ppermute | solution.py:432
  2.7 18.2 %collective-permute-start.9 = (bf16[128,2048]{1,0:T(8,128)(2,1)}, bf16[128,2048]{1,0:T(8,128)(2,1)S(1)}, u32[]{:S(2)}, u32[]{:S(2)}) collective-permute-start(bf16[128,2048]{1,0:T(8,128)(2,1)} %bitcast.35), channel_id=1, source_target_pairs={{0,8},{8,0},{16,24},{24,16},{1,9},{9,1},{17,25},{25,17},{2,10},{10... | collective-permute-start | bytes 1572872 | tf_op jit(solution)/shard_map/send_cot1/ppermute | solution.py:432
  7.5 11.2 %collective-permute-start.3 = (bf16[8,128,128]{2,1,0:T(8,128)(2,1)S(1)}, bf16[8,128,128]{2,1,0:T(8,128)(2,1)S(1)}, u32[]{:S(2)}, u32[]{:S(2)}) collective-permute-start(bf16[8,128,128]{2,1,0:T(8,128)(2,1)S(1)} %states.1), channel_id=1, source_target_pairs={{0,2},{1,3},{2,0},{3,1},{4,6},{5,7},{6,4},{7,5},{8,10},{9,11},{10,... | collective-permute-start | bytes 786440 | tf_op jit(solution)/shard_map/send_near/ppermute | solution.py:432
  9.2 11.7 %collective-permute-start.7 = (bf16[64,2048]{1,0:T(8,128)(2,1)S(1)}, bf16[64,2048]{1,0:T(8,128)(2,1)S(1)}, u32[]{:S(2)}, u32[]{:S(2)}) collective-permute-start(bf16[64,2048]{1,0:T(8,128)(2,1)S(1)} %constant_dynamic-slice_fusion), channel_id=1, source_target_pairs={{0,4},{1,5},{2,6},{3,7},{4,0},{5,1},{6,2},{7,3},{8,12},{9,13},{10,... | collective-permute-start | bytes 786440 | tf_op jit(solution)/shard_map/send_w2/ppermute | solution.py:432
  15.3 15.5 %collective-permute-start.13 = (bf16[128,2048]{1,0:T(8,128)(2,1)S(1)}, bf16[128,2048]{1,0:T(8,128)(2,1)S(1)}, u32[]{:S(2)}, u32[]{:S(2)}) collective-permute-start(bf16[128,2048]{1,0:T(8,128)(2,1)S(1)} %bitcast.36), channel_id=1, source_target_pairs={{0,24},{8,16},{16,8},{24,0},{1,25},{9,17},{17,9},{25,1},{2,26},{10... | collective-permute-start | bytes 1572872 | tf_op jit(solution)/shard_map/send_cot3/ppermute | solution.py:432
  17.8 13.6 %collective-permute-start.2 = (bf16[128,2048]{1,0:T(8,128)(2,1)S(1)}, bf16[128,2048]{1,0:T(8,128)(2,1)S(1)}, u32[]{:S(2)}, u32[]{:S(2)}) collective-permute-start(bf16[128,2048]{1,0:T(8,128)(2,1)S(1)} %bitcast.30), channel_id=1, source_target_pairs={{0,1},{1,0},{2,3},{3,2},{4,5},{5,4},{6,7},{7,6},{8,9},{9,8},{10,11... | collective-permute-start | bytes 1572872 | tf_op jit(solution)/shard_map/send_query/ppermute | solution.py:432
  18.8 12.1 %collective-permute-start.4 = (bf16[8,128,128]{2,1,0:T(8,128)(2,1)S(1)}, bf16[8,128,128]{2,1,0:T(8,128)(2,1)S(1)}, u32[]{:S(2)}, u32[]{:S(2)}) collective-permute-start(bf16[8,128,128]{2,1,0:T(8,128)(2,1)S(1)} %add.30), channel_id=1, source_target_pairs={{0,4},{1,5},{2,6},{3,7},{8,12},{9,13},{10,14},{11,15},{16,20},{17,... | collective-permute-start | bytes 786440 | tf_op jit(solution)/shard_map/send_far/ppermute | solution.py:432
  20.9 12.9 %collective-permute-start.5 = (bf16[128,2048]{1,0:T(8,128)(2,1)S(1)}, bf16[128,2048]{1,0:T(8,128)(2,1)S(1)}, u32[]{:S(2)}, u32[]{:S(2)}) collective-permute-start(bf16[128,2048]{1,0:T(8,128)(2,1)S(1)} %bitcast.37), channel_id=1, source_target_pairs={{0,1},{1,0},{2,3},{3,2},{4,5},{5,4},{6,7},{7,6},{8,9},{9,8},{10,11... | collective-permute-start | bytes 1572872 | tf_op jit(solution)/shard_map/send_sib0/ppermute | solution.py:432
  21.0 20.2 %collective-permute-start.8 = (bf16[128,2048]{1,0:T(8,128)(2,1)S(1)}, bf16[128,2048]{1,0:T(8,128)(2,1)S(1)}, u32[]{:S(2)}, u32[]{:S(2)}) collective-permute-start(bf16[128,2048]{1,0:T(8,128)(2,1)S(1)} %pad_maximum_fusion.1.w_first), channel_id=1, source_target_pairs={{0,2},{1,3},{2,0},{3,1},{4,6},{5,7},{6,4},{7,5},{8,10},{9,11},{10,... | collective-permute-start | bytes 1572872 | tf_op jit(solution)/shard_map/send_w_second/ppermute | solution.py:432
  30.8 11.8 %collective-permute-start.10 = (bf16[128,2048]{1,0:T(8,128)(2,1)S(1)}, bf16[128,2048]{1,0:T(8,128)(2,1)S(1)}, u32[]{:S(2)}, u32[]{:S(2)}) collective-permute-start(bf16[128,2048]{1,0:T(8,128)(2,1)S(1)} %collective-permute-done.9.refs_2_.refs_6_), channel_id=1, source_target_pairs={{0,1},{1,0},{2,3},{3,2},{4,5},{5,4},{6,7},{7,6},{8,9},{9,8},{10,11... | collective-permute-start | bytes 1572872 | tf_op jit(solution)/shard_map/send_sib1/ppermute | solution.py:432
  30.8 13.4 %collective-permute-start.12 = (bf16[128,2048]{1,0:T(8,128)(2,1)S(1)}, bf16[128,2048]{1,0:T(8,128)(2,1)S(1)}, u32[]{:S(2)}, u32[]{:S(2)}) collective-permute-start(bf16[128,2048]{1,0:T(8,128)(2,1)S(1)} %collective-permute-done.11.refs_4_.refs_8_), channel_id=1, source_target_pairs={{0,1},{1,0},{2,3},{3,2},{4,5},{5,4},{6,7},{7,6},{8,9},{9,8},{10,11... | collective-permute-start | bytes 1572872 | tf_op jit(solution)/shard_map/send_sib2/ppermute | solution.py:432
  31.4 12.9 %collective-permute-start.14 = (bf16[128,2048]{1,0:T(8,128)(2,1)S(1)}, bf16[128,2048]{1,0:T(8,128)(2,1)S(1)}, u32[]{:S(2)}, u32[]{:S(2)}) collective-permute-start(bf16[128,2048]{1,0:T(8,128)(2,1)S(1)} %collective-permute-done.13.refs_6_.refs_10_), channel_id=1, source_target_pairs={{0,1},{1,0},{2,3},{3,2},{4,5},{5,4},{6,7},{7,6},{8,9},{9,8},{10,11... | collective-permute-start | bytes 1572872 | tf_op jit(solution)/shard_map/send_sib3/ppermute | solution.py:432
  33.8 13.2 %collective-permute-start.16 = (bf16[256,256]{1,0:T(8,128)(2,1)S(1)}, bf16[256,256]{1,0:T(8,128)(2,1)S(1)}, u32[]{:S(2)}, u32[]{:S(2)}) collective-permute-start(bf16[256,256]{1,0:T(8,128)(2,1)S(1)} %get-tuple-element.67), channel_id=1, source_target_pairs={{0,24},{8,16},{16,8},{24,0},{1,25},{9,17},{17,9},{25,1},{2,26},{10... | collective-permute-start | bytes 393224 | tf_op jit(solution)/shard_map/send_n3/ppermute | solution.py:432
  51.0 15.9 %collective-permute-start.26 = (bf16[128,2048]{1,0:T(8,128)(2,1)S(1)}, bf16[128,2048]{1,0:T(8,128)(2,1)S(1)}, u32[]{:S(2)}, u32[]{:S(2)}) collective-permute-start(bf16[128,2048]{1,0:T(8,128)(2,1)S(1)} %get-tuple-element.69), channel_id=1, source_target_pairs={{0,2},{1,3},{2,0},{3,1},{4,6},{5,7},{6,4},{7,5},{8,10},{9,11},{10,... | collective-permute-start | bytes 1572872 | tf_op jit(solution)/shard_map/send_terms/ppermute | solution.py:432
  59.5 22.0 %collective-permute-start.19 = (bf16[128,2048]{1,0:T(8,128)(2,1)S(1)}, bf16[128,2048]{1,0:T(8,128)(2,1)S(1)}, u32[]{:S(2)}, u32[]{:S(2)}) collective-permute-start(bf16[128,2048]{1,0:T(8,128)(2,1)S(1)} %get-tuple-element.73), channel_id=1, source_target_pairs={{0,8},{8,0},{16,24},{24,16},{1,9},{9,1},{17,25},{25,17},{2,10},{10... | collective-permute-start | bytes 1572872 | tf_op jit(solution)/shard_map/send_mixed1/ppermute | solution.py:432
  61.1 20.4 %collective-permute-start.20 = (bf16[128,2048]{1,0:T(8,128)(2,1)S(1)}, bf16[128,2048]{1,0:T(8,128)(2,1)S(1)}, u32[]{:S(2)}, u32[]{:S(2)}) collective-permute-start(bf16[128,2048]{1,0:T(8,128)(2,1)S(1)} %get-tuple-element.74), channel_id=1, source_target_pairs={{0,16},{8,24},{16,0},{24,8},{1,17},{9,25},{17,1},{25,9},{2,18},{10... | collective-permute-start | bytes 1572872 | tf_op jit(solution)/shard_map/send_mixed2/ppermute | solution.py:432
  63.4 22.4 %collective-permute-start.21 = (bf16[128,2048]{1,0:T(8,128)(2,1)S(1)}, bf16[128,2048]{1,0:T(8,128)(2,1)S(1)}, u32[]{:S(2)}, u32[]{:S(2)}) collective-permute-start(bf16[128,2048]{1,0:T(8,128)(2,1)S(1)} %get-tuple-element.75), channel_id=1, source_target_pairs={{0,24},{8,16},{16,8},{24,0},{1,25},{9,17},{17,9},{25,1},{2,26},{10... | collective-permute-start | bytes 1572872 | tf_op jit(solution)/shard_map/send_mixed3/ppermute | solution.py:432
  67.0 9.3 %collective-permute-start.27 = (bf16[8,128,128]{2,1,0:T(8,128)(2,1)S(1)}, bf16[8,128,128]{2,1,0:T(8,128)(2,1)S(1)}, u32[]{:S(2)}, u32[]{:S(2)}) collective-permute-start(bf16[8,128,128]{2,1,0:T(8,128)(2,1)S(1)} %get-tuple-element.85), channel_id=1, source_target_pairs={{0,2},{1,3},{2,0},{3,1},{4,6},{5,7},{6,4},{7,5},{8,10},{9,11},{10,... | collective-permute-start | bytes 786440 | tf_op jit(solution)/shard_map/send_d_near/ppermute | solution.py:432
  68.0 21.6 %collective-permute-start.31 = (bf16[64,2048]{1,0:T(8,128)(2,1)S(1)}, bf16[64,2048]{1,0:T(8,128)(2,1)S(1)}, u32[]{:S(2)}, u32[]{:S(2)}) collective-permute-start(bf16[64,2048]{1,0:T(8,128)(2,1)S(1)} %slice.35), channel_id=1, source_target_pairs={{0,4},{1,5},{2,6},{3,7},{4,0},{5,1},{6,2},{7,3},{8,12},{9,13},{10,... | collective-permute-start | bytes 786440 | tf_op jit(solution)/shard_map/send_pair_terms/ppermute | solution.py:432
  76.3 17.0 %collective-permute-start.29 = (bf16[8,128,128]{2,1,0:T(8,128)(2,1)S(1)}, bf16[8,128,128]{2,1,0:T(8,128)(2,1)S(1)}, u32[]{:S(2)}, u32[]{:S(2)}) collective-permute-start(bf16[8,128,128]{2,1,0:T(8,128)(2,1)S(1)} %add.35), channel_id=1, source_target_pairs={{4,0},{5,1},{6,2},{7,3},{12,8},{13,9},{14,10},{15,11},{20,16},{21,... | collective-permute-start | bytes 786440 | tf_op jit(solution)/shard_map/send_d_far/ppermute | solution.py:432
  89.6 17.7 %collective-permute-start.25 = (bf16[3,128,1024]{2,1,0:T(8,128)(2,1)S(1)}, bf16[3,128,1024]{2,1,0:T(8,128)(2,1)S(1)}, u32[]{:S(2)}, u32[]{:S(2)}) collective-permute-start(bf16[3,128,1024]{2,1,0:T(8,128)(2,1)S(1)} %get-tuple-element.82), channel_id=1, source_target_pairs={{0,1},{1,0},{2,3},{3,2},{4,5},{5,4},{6,7},{7,6},{8,9},{9,8},{10,11... | collective-permute-start | bytes 2359304 | tf_op jit(solution)/shard_map/send_parts/ppermute | solution.py:432
  91.3 14.0 %collective-permute-start.33 = (bf16[64,2048]{1,0:T(8,128)(2,1)S(1)}, bf16[64,2048]{1,0:T(8,128)(2,1)S(1)}, u32[]{:S(2)}, u32[]{:S(2)}) collective-permute-start(bf16[64,2048]{1,0:T(8,128)(2,1)S(1)} %fusion.t0), channel_id=1, source_target_pairs={{0,16},{8,24},{16,0},{24,8},{1,17},{9,25},{17,1},{25,9},{2,18},{10... | collective-permute-start | bytes 786440 | tf_op jit(solution)/shard_map/send_share2/ppermute | solution.py:432
  91.8 13.5 %collective-permute-start.34 = (bf16[64,2048]{1,0:T(8,128)(2,1)S(1)}, bf16[64,2048]{1,0:T(8,128)(2,1)S(1)}, u32[]{:S(2)}, u32[]{:S(2)}) collective-permute-start(bf16[64,2048]{1,0:T(8,128)(2,1)S(1)} %fusion.t0), channel_id=1, source_target_pairs={{0,24},{8,16},{16,8},{24,0},{1,25},{9,17},{17,9},{25,1},{2,26},{10... | collective-permute-start | bytes 786440 | tf_op jit(solution)/shard_map/send_share3/ppermute | solution.py:432
  93.3 14.0 %collective-permute-start.28 = (bf16[8,128,128]{2,1,0:T(8,128)(2,1)S(1)}, bf16[8,128,128]{2,1,0:T(8,128)(2,1)S(1)}, u32[]{:S(2)}, u32[]{:S(2)}) collective-permute-start(bf16[8,128,128]{2,1,0:T(8,128)(2,1)S(1)} %collective-permute-done.27.near), channel_id=1, source_target_pairs={{0,1},{1,0},{2,3},{3,2},{4,5},{5,4},{6,7},{7,6},{8,9},{9,8},{10,11... | collective-permute-start | bytes 786440 | tf_op jit(solution)/shard_map/send_d_near_sib/ppermute | solution.py:432
  (19 other events, 162.4 us)

commit v5 on v4

--- a/solution.py
+++ b/solution.py
@@ -419,7 +419,7 @@
     state_flops = 2 * heads * 2 * half * HEAD * HEAD
     pack, full = like((2 * half, PAIR), bf16), like((half, width), bf16)
     part = like((half, width // 2), f32)
-    step = 512
+    step = 1024
 
     def column_spec(rows, columns):
         return pl.BlockSpec((rows, columns), lambda i: (0, i))
@@ -471,7 +471,7 @@
     sib1 = to_sib(cot1, "sib1")
     cot2 = across(cot, 2, "cot2")
     sib2 = to_sib(after(cot2, far), "sib2")
-    cot3 = across(after(cot, cot2), 3, "cot3")
+    cot3 = across(after(cot, cot1, cot2), 3, "cot3")
     sib3 = to_sib(cot3, "sib3")
     cot_parts = [cot, sib0, cot1, sib1, cot2, sib2, cot3, sib3]
     d_packs = call(
@@ -518,9 +518,9 @@
     for x in mixed_got:
         mixed = mixed + x.astype(f32)
     mixed = mixed.astype(bf16)
-    d1 = across(after(d_packs[1], given), 1, "d1")
-    d2 = across(after(d_packs[2], given), 2, "d2")
-    d3 = across(after(d_packs[3], given), 3, "d3")
+    d1 = across(d_packs[1], 1, "d1")
+    d2 = across(d_packs[2], 2, "d2")
+    d3 = across(d_packs[3], 3, "d3")
     d_got = (d_packs[0], d1, d2, d3)
     d_attended, d_state = call(
         d_attend_kernel,

time: 110 us -> 110 us (level); the launches traced: 110 us -> 108 us
  waiting for transfers between devices: 46.4 us -> 44.9 us
    ppermute x35, waiting for transfers between devices: 46.4 us -> 44.9 us  [sent(): return lax.ppermute(x, axis, pairs)]
  transfers between devices with their start and end apart: 35 -> 35, of which waited for: 12 -> 14; matrix products, arithmetic and copies ran while one was open for 2% -> 2% of each run, Pallas kernels for 14% -> 14%
where the time goes in v5:
time: 110 us; the launch traced here: 108 us
  waiting for transfers between devices  44.9 us (41%)
  starting transfers between devices  38.3 us (35%)
  Pallas kernels  20.4 us (19%)
  local copies, waits for them, and re-layouts  2.18 us (2%)
  other arithmetic  1.66 us (2%)
    ppermute x35, waiting for transfers between devices, sent(): return lax.ppermute(x, axis, pairs)  44.9 us
    ppermute x35, starting transfers between devices, sent(): return lax.ppermute(x, axis, pairs)  38.3 us
    pallas_call x9, Pallas kernels, call(): pl.pallas_call(kernel, out_shape=list(outs), grid=grid, in_specs=in_specs...  20.4 us
  transfers between devices with their start and end apart: 35, of which 14 were waited for; matrix products, arithmetic and copies ran while one was open for 2% of the time, Pallas kernels for 14%

profile of v5, /device:TPU:16, one launch (start us, length us, event | category | flops | bytes accessed | tf_op | source)
XLA Modules:
  0.0 108.3 jit_solution(3065437256135123284)
XLA Ops:
  1.2 1.5 %collective-permute-start.11 = (bf16[128,2048]{1,0:T(8,128)(2,1)}, bf16[128,2048]{1,0:T(8,128)(2,1)S(1)}, u32[]{:S(2)}, u32[]{:S(2)}) collective-permute-start(bf16[128,2048]{1,0:T(8,128)(2,1)} %bitcast.34), channel_id=1, source_target_pairs={{0,16},{8,24},{16,0},{24,8},{1,17},{9,25},{17,1},{25,9},{2,18},{10... | collective-permute-start | bytes 1572872 | tf_op jit(solution)/shard_map/send_cot2/ppermute | solution.py:432
  2.7 1.5 %collective-permute-start.9 = (bf16[128,2048]{1,0:T(8,128)(2,1)}, bf16[128,2048]{1,0:T(8,128)(2,1)S(1)}, u32[]{:S(2)}, u32[]{:S(2)}) collective-permute-start(bf16[128,2048]{1,0:T(8,128)(2,1)} %bitcast.35), channel_id=1, source_target_pairs={{0,8},{8,0},{16,24},{24,16},{1,9},{9,1},{17,25},{25,17},{2,10},{10... | collective-permute-start | bytes 1572872 | tf_op jit(solution)/shard_map/send_cot1/ppermute | solution.py:432
  7.5 1.6 %collective-permute-start.3 = (bf16[8,128,128]{2,1,0:T(8,128)(2,1)S(1)}, bf16[8,128,128]{2,1,0:T(8,128)(2,1)S(1)}, u32[]{:S(2)}, u32[]{:S(2)}) collective-permute-start(bf16[8,128,128]{2,1,0:T(8,128)(2,1)S(1)} %states.1), channel_id=1, source_target_pairs={{0,2},{1,3},{2,0},{3,1},{4,6},{5,7},{6,4},{7,5},{8,10},{9,11},{10,... | collective-permute-start | bytes 786440 | tf_op jit(solution)/shard_map/send_near/ppermute | solution.py:432
  9.6 5.8 %collective-permute-done.11.refs_4_.refs_8_ = bf16[128,2048]{1,0:T(8,128)(2,1)S(1)} collective-permute-done((bf16[128,2048]{1,0:T(8,128)(2,1)}, bf16[128,2048]{1,0:T(8,128)(2,1)S(1)}, u32[]{:S(2)}, u32[]{:S(2)}) %collective-permute-start.11) | collective-permute-done | bytes 524320 | tf_op jit(solution)/shard_map/send_cot2/ppermute | solution.py:432
  21.0 2.9 %collective-permute-start.8 = (bf16[128,2048]{1,0:T(8,128)(2,1)S(1)}, bf16[128,2048]{1,0:T(8,128)(2,1)S(1)}, u32[]{:S(2)}, u32[]{:S(2)}) collective-permute-start(bf16[128,2048]{1,0:T(8,128)(2,1)S(1)} %pad_maximum_fusion.1.w_first), channel_id=1, source_target_pairs={{0,2},{1,3},{2,0},{3,1},{4,6},{5,7},{6,4},{7,5},{8,10},{9,11},{10,... | collective-permute-start | bytes 1572872 | tf_op jit(solution)/shard_map/send_w_second/ppermute | solution.py:432
  23.8 7.0 %collective-permute-done.4.far = bf16[8,128,128]{2,1,0:T(8,128)(2,1)S(1)} collective-permute-done((bf16[8,128,128]{2,1,0:T(8,128)(2,1)S(1)}, bf16[8,128,128]{2,1,0:T(8,128)(2,1)S(1)}, u32[]{:S(2)}, u32[]{:S(2)}) %collective-permute-start.4) | collective-permute-done | bytes 262176 | tf_op jit(solution)/shard_map/send_far/ppermute | solution.py:432
  31.4 2.4 %attend.1 = (f32[256,1024]{1,0:T(8,128)S(1)}, bf16[256,256]{1,0:T(8,128)(2,1)S(1)}, bf16[256,256]{1,0:T(8,128)(2,1)S(1)}, bf16[256,256]{1,0:T(8,128)(2,1)S(1)}, bf16[256,256]{1,0:T(8,128)(2,1)S(1)}) custom-call(s32[3]{0:T(128)S(1)} %pad_add_fusion.place, bf16[128,2048]{1,0:T(8,128)(2,1)S(1)} %bitcast.31, bf16[128,2048]{1,0:T(8,128)(2,1)S(1)} %collective-permute-done.2.q_sib, ...), custom_call_target="tpu_custom_call" | custom-call | tf_op jit(solution)/shard_map/attend/pallas_call | solution.py:180
  33.8 2.4 %collective-permute-start.16 = (bf16[256,256]{1,0:T(8,128)(2,1)S(1)}, bf16[256,256]{1,0:T(8,128)(2,1)S(1)}, u32[]{:S(2)}, u32[]{:S(2)}) collective-permute-start(bf16[256,256]{1,0:T(8,128)(2,1)S(1)} %get-tuple-element.64), channel_id=1, source_target_pairs={{0,24},{8,16},{16,8},{24,0},{1,25},{9,17},{17,9},{25,1},{2,26},{10... | collective-permute-start | bytes 393224 | tf_op jit(solution)/shard_map/send_n3/ppermute | solution.py:432
  36.2 3.9 %collective-permute-done.8.w_second = bf16[128,2048]{1,0:T(8,128)(2,1)S(1)} collective-permute-done((bf16[128,2048]{1,0:T(8,128)(2,1)S(1)}, bf16[128,2048]{1,0:T(8,128)(2,1)S(1)}, u32[]{:S(2)}, u32[]{:S(2)}) %collective-permute-start.8) | collective-permute-done | bytes 524320 | tf_op jit(solution)/shard_map/send_w_second/ppermute | solution.py:432
  41.6 1.5 %collective-permute-start.6 = (bf16[256,256]{1,0:T(8,128)(2,1)S(1)}, bf16[256,256]{1,0:T(8,128)(2,1)S(1)}, u32[]{:S(2)}, u32[]{:S(2)}) collective-permute-start(bf16[256,256]{1,0:T(8,128)(2,1)S(1)} %get-tuple-element.54), channel_id=1, source_target_pairs={{0,8},{8,0},{16,24},{24,16},{1,9},{9,1},{17,25},{25,17},{2,10},{10... | collective-permute-start | bytes 393224 | tf_op jit(solution)/shard_map/send_n1/ppermute | solution.py:432
  43.2 2.8 %d_normed.1 = (bf16[256,256]{1,0:T(8,128)(2,1)S(1)}, bf16[256,256]{1,0:T(8,128)(2,1)S(1)}, bf16[256,256]{1,0:T(8,128)(2,1)S(1)}, bf16[256,256]{1,0:T(8,128)(2,1)S(1)}) custom-call(bf16[128,2048]{1,0:T(8,128)(2,1)S(1)} %pad_maximum_fusion.1.w_first, bf16[128,2048]{1,0:T(8,128)(2,1)S(1)} %collective-permute-done.8.w_second, bf16[128,2048]{1,0:T(8,128)(2,1)S(1)} %bitcast.38, ...), custom_call_target="tpu_custom_call" | custom-call | flops 1073741824 | bytes 5767168 | tf_op jit(solution)/shard_map/d_normed/pallas_call | solution.py:180
  46.6 2.9 %weight_terms.1 = (f32[128,2048]{1,0:T(8,128)S(1)}, bf16[128,2048]{1,0:T(8,128)(2,1)S(1)}) custom-call(bf16[256,256]{1,0:T(8,128)(2,1)S(1)} %get-tuple-element.53.refs_0_.n0, bf16[256,256]{1,0:T(8,128)(2,1)S(1)} %collective-permute-done.6.refs_1_.n1, bf16[256,256]{1,0:T(8,128)(2,1)S(1)} %collective-permute-done.15.refs_2_.n2, ...), custom_call_target="tpu_custom_call" | custom-call | flops 1073741824 | bytes 6291456 | tf_op jit(solution)/shard_map/weight_terms/pallas_call | solution.py:180
  49.6 3.0 %collective-permute-start.26 = (bf16[128,2048]{1,0:T(8,128)(2,1)S(1)}, bf16[128,2048]{1,0:T(8,128)(2,1)S(1)}, u32[]{:S(2)}, u32[]{:S(2)}) collective-permute-start(bf16[128,2048]{1,0:T(8,128)(2,1)S(1)} %get-tuple-element.66), channel_id=1, source_target_pairs={{0,2},{1,3},{2,0},{3,1},{4,6},{5,7},{6,4},{7,5},{8,10},{9,11},{10,... | collective-permute-start | bytes 1572872 | tf_op jit(solution)/shard_map/send_terms/ppermute | solution.py:432
  56.4 1.8 %mixed_terms.1 = (f32[128,2048]{1,0:T(8,128)S(1)}, bf16[128,2048]{1,0:T(8,128)(2,1)S(1)}, bf16[128,2048]{1,0:T(8,128)(2,1)S(1)}, bf16[128,2048]{1,0:T(8,128)(2,1)S(1)}) custom-call(bf16[256,256]{1,0:T(8,128)(2,1)S(1)} %get-tuple-element.53.refs_0_.n0, bf16[256,256]{1,0:T(8,128)(2,1)S(1)} %collective-permute-done.6.refs_1_.n1, ...), custom_call_target="tpu_custom_call" | custom-call | flops 1073741824 | bytes 5505024 | tf_op jit(solution)/shard_map/mixed_terms/pallas_call | solution.py:180
  61.0 3.5 %collective-permute-start.21 = (bf16[128,2048]{1,0:T(8,128)(2,1)S(1)}, bf16[128,2048]{1,0:T(8,128)(2,1)S(1)}, u32[]{:S(2)}, u32[]{:S(2)}) collective-permute-start(bf16[128,2048]{1,0:T(8,128)(2,1)S(1)} %get-tuple-element.72), channel_id=1, source_target_pairs={{0,24},{8,16},{16,8},{24,0},{1,25},{9,17},{17,9},{25,1},{2,26},{10... | collective-permute-start | bytes 1572872 | tf_op jit(solution)/shard_map/send_mixed3/ppermute | solution.py:432
  64.5 2.1 %d_attend.1 = (bf16[256,1024]{1,0:T(8,128)(2,1)S(1)}, bf16[8,128,128]{2,1,0:T(8,128)(2,1)S(1)}) custom-call(s32[3]{0:T(128)S(1)} %pad_add_fusion.place, bf16[128,2048]{1,0:T(8,128)(2,1)S(1)} %bitcast.32, bf16[128,2048]{1,0:T(8,128)(2,1)S(1)} %collective-permute-done.2.q_sib, f32[256,1024]{1,0:T(8,128)S(1)} %get-tuple-element.73.attended, ...), custom_call_target="tpu_custom_call" | custom-call | flops 134217728 | bytes 3416076 | tf_op jit(solution)/shard_map/d_attend/pallas_call | solution.py:180
  67.2 8.8 %collective-permute-done.27.near = bf16[8,128,128]{2,1,0:T(8,128)(2,1)S(1)} collective-permute-done((bf16[8,128,128]{2,1,0:T(8,128)(2,1)S(1)}, bf16[8,128,128]{2,1,0:T(8,128)(2,1)S(1)}, u32[]{:S(2)}, u32[]{:S(2)}) %collective-permute-start.27) | collective-permute-done | bytes 262176 | tf_op jit(solution)/shard_map/send_d_near/ppermute | solution.py:432
  76.0 4.4 %collective-permute-start.29 = (bf16[8,128,128]{2,1,0:T(8,128)(2,1)S(1)}, bf16[8,128,128]{2,1,0:T(8,128)(2,1)S(1)}, u32[]{:S(2)}, u32[]{:S(2)}) collective-permute-start(bf16[8,128,128]{2,1,0:T(8,128)(2,1)S(1)} %add.35), channel_id=1, source_target_pairs={{4,0},{5,1},{6,2},{7,3},{12,8},{13,9},{14,10},{15,11},{20,16},{21,... | collective-permute-start | bytes 786440 | tf_op jit(solution)/shard_map/send_d_far/ppermute | solution.py:432
  80.5 3.0 %collective-permute-done.20 = bf16[128,2048]{1,0:T(8,128)(2,1)S(1)} collective-permute-done((bf16[128,2048]{1,0:T(8,128)(2,1)S(1)}, bf16[128,2048]{1,0:T(8,128)(2,1)S(1)}, u32[]{:S(2)}, u32[]{:S(2)}) %collective-permute-start.20) | collective-permute-done | bytes 524320 | tf_op jit(solution)/shard_map/send_mixed2/ppermute | solution.py:432
  85.9 2.7 %inner.1 = (bf16[128,2048]{1,0:T(8,128)(2,1)S(1)}, f32[128,1024]{1,0:T(8,128)S(1)}, f32[128,1024]{1,0:T(8,128)S(1)}, bf16[3,128,1024]{2,1,0:T(8,128)(2,1)S(1)}) custom-call(s32[3]{0:T(128)S(1)} %pad_add_fusion.place, bf16[128,2048]{1,0:T(8,128)(2,1)S(1)} %bitcast.33, bf16[128,2048]{1,0:T(8,128)(2,1)S(1)} %collective-permute-done.2.q_sib, ...), custom_call_target="tpu_custom_call" | custom-call | flops 939524096 | bytes 6553612 | tf_op jit(solution)/shard_map/inner/pallas_call | solution.py:180
  92.3 5.6 %collective-permute-done.32.t1 = bf16[64,2048]{1,0:T(8,128)(2,1)S(1)} collective-permute-done((bf16[64,2048]{1,0:T(8,128)(2,1)S(1)}, bf16[64,2048]{1,0:T(8,128)(2,1)S(1)}, u32[]{:S(2)}, u32[]{:S(2)}) %collective-permute-start.32) | collective-permute-done | bytes 262176 | tf_op jit(solution)/shard_map/send_share1/ppermute | solution.py:432
  97.9 4.8 %collective-permute-done.33.t2 = bf16[64,2048]{1,0:T(8,128)(2,1)S(1)} collective-permute-done((bf16[64,2048]{1,0:T(8,128)(2,1)S(1)}, bf16[64,2048]{1,0:T(8,128)(2,1)S(1)}, u32[]{:S(2)}, u32[]{:S(2)}) %collective-permute-start.33) | collective-permute-done | bytes 262176 | tf_op jit(solution)/shard_map/send_share2/ppermute | solution.py:432
  103.8 2.0 %grad_weight.1 = f32[256,2048]{1,0:T(8,128)} custom-call(s32[3]{0:T(128)S(1)} %pad_add_fusion.place, bf16[64,2048]{1,0:T(8,128)(2,1)S(1)} %fusion.t0, bf16[64,2048]{1,0:T(8,128)(2,1)S(1)} %collective-permute-done.32.t1, bf16[64,2048]{1,0:T(8,128)(2,1)S(1)} %collective-permute-done.33.t2, bf16[64,2048]{1,0:T(8,128)(2,1)S(1)} %collective-permute-done.34.t3), custom_call_target="tpu_custom_call" | custom-call | bytes 3145740 | tf_op jit(solution)/shard_map/grad_weight/pallas_call | solution.py:180
  105.8 2.5 %finish.1 = (bf16[128,2048]{1,0:T(8,128)(2,1)}, bf16[128,2048]{1,0:T(8,128)(2,1)}, bf16[128,2048]{1,0:T(8,128)(2,1)}) custom-call(s32[3]{0:T(128)S(1)} %pad_add_fusion.place, bf16[3,128,1024]{2,1,0:T(8,128)(2,1)S(1)} %collective-permute-done.25.got, bf16[128,2048]{1,0:T(8,128)(2,1)S(1)} %get-tuple-element.77.held, bf16[128,2048]{1,0:T(8,128)(2,1)S(1)} %bitcast.24, ...), custom_call_target="tpu_custom_call" | custom-call | flops 134217728 | bytes 6029324 | tf_op jit(solution)/shard_map/finish/pallas_call | solution.py:180
  (85 shorter events, 26.8 us)
Async XLA Ops:
  1.2 14.1 %collective-permute-start.11 = (bf16[128,2048]{1,0:T(8,128)(2,1)}, bf16[128,2048]{1,0:T(8,128)(2,1)S(1)}, u32[]{:S(2)}, u32[]{:S(2)}) collective-permute-start(bf16[128,2048]{1,0:T(8,128)(2,1)} %bitcast.34), channel_id=1, source_target_pairs={{0,16},{8,24},{16,0},{24,8},{1,17},{9,25},{17,1},{25,9},{2,18},{10... | collective-permute-start | bytes 1572872 | tf_op jit(solution)/shard_map/send_cot2/ppermute | solution.py:432
  2.7 13.8 %collective-permute-start.9 = (bf16[128,2048]{1,0:T(8,128)(2,1)}, bf16[128,2048]{1,0:T(8,128)(2,1)S(1)}, u32[]{:S(2)}, u32[]{:S(2)}) collective-permute-start(bf16[128,2048]{1,0:T(8,128)(2,1)} %bitcast.35), channel_id=1, source_target_pairs={{0,8},{8,0},{16,24},{24,16},{1,9},{9,1},{17,25},{25,17},{2,10},{10... | collective-permute-start | bytes 1572872 | tf_op jit(solution)/shard_map/send_cot1/ppermute | solution.py:432
  7.5 11.2 %collective-permute-start.3 = (bf16[8,128,128]{2,1,0:T(8,128)(2,1)S(1)}, bf16[8,128,128]{2,1,0:T(8,128)(2,1)S(1)}, u32[]{:S(2)}, u32[]{:S(2)}) collective-permute-start(bf16[8,128,128]{2,1,0:T(8,128)(2,1)S(1)} %states.1), channel_id=1, source_target_pairs={{0,2},{1,3},{2,0},{3,1},{4,6},{5,7},{6,4},{7,5},{8,10},{9,11},{10,... | collective-permute-start | bytes 786440 | tf_op jit(solution)/shard_map/send_near/ppermute | solution.py:432
  9.2 11.7 %collective-permute-start.7 = (bf16[64,2048]{1,0:T(8,128)(2,1)S(1)}, bf16[64,2048]{1,0:T(8,128)(2,1)S(1)}, u32[]{:S(2)}, u32[]{:S(2)}) collective-permute-start(bf16[64,2048]{1,0:T(8,128)(2,1)S(1)} %constant_dynamic-slice_fusion), channel_id=1, source_target_pairs={{0,4},{1,5},{2,6},{3,7},{4,0},{5,1},{6,2},{7,3},{8,12},{9,13},{10,... | collective-permute-start | bytes 786440 | tf_op jit(solution)/shard_map/send_w2/ppermute | solution.py:432
  16.6 14.2 %collective-permute-start.13 = (bf16[128,2048]{1,0:T(8,128)(2,1)S(1)}, bf16[128,2048]{1,0:T(8,128)(2,1)S(1)}, u32[]{:S(2)}, u32[]{:S(2)}) collective-permute-start(bf16[128,2048]{1,0:T(8,128)(2,1)S(1)} %bitcast.36), channel_id=1, source_target_pairs={{0,24},{8,16},{16,8},{24,0},{1,25},{9,17},{17,9},{25,1},{2,26},{10... | collective-permute-start | bytes 1572872 | tf_op jit(solution)/shard_map/send_cot3/ppermute | solution.py:432
  18.0 13.3 %collective-permute-start.2 = (bf16[128,2048]{1,0:T(8,128)(2,1)S(1)}, bf16[128,2048]{1,0:T(8,128)(2,1)S(1)}, u32[]{:S(2)}, u32[]{:S(2)}) collective-permute-start(bf16[128,2048]{1,0:T(8,128)(2,1)S(1)} %bitcast.30), channel_id=1, source_target_pairs={{0,1},{1,0},{2,3},{3,2},{4,5},{5,4},{6,7},{7,6},{8,9},{9,8},{10,11... | collective-permute-start | bytes 1572872 | tf_op jit(solution)/shard_map/send_query/ppermute | solution.py:432
  18.8 12.0 %collective-permute-start.4 = (bf16[8,128,128]{2,1,0:T(8,128)(2,1)S(1)}, bf16[8,128,128]{2,1,0:T(8,128)(2,1)S(1)}, u32[]{:S(2)}, u32[]{:S(2)}) collective-permute-start(bf16[8,128,128]{2,1,0:T(8,128)(2,1)S(1)} %add.30), channel_id=1, source_target_pairs={{0,4},{1,5},{2,6},{3,7},{8,12},{9,13},{10,14},{11,15},{16,20},{17,... | collective-permute-start | bytes 786440 | tf_op jit(solution)/shard_map/send_far/ppermute | solution.py:432
  20.1 13.7 %collective-permute-start.5 = (bf16[128,2048]{1,0:T(8,128)(2,1)S(1)}, bf16[128,2048]{1,0:T(8,128)(2,1)S(1)}, u32[]{:S(2)}, u32[]{:S(2)}) collective-permute-start(bf16[128,2048]{1,0:T(8,128)(2,1)S(1)} %bitcast.37), channel_id=1, source_target_pairs={{0,1},{1,0},{2,3},{3,2},{4,5},{5,4},{6,7},{7,6},{8,9},{9,8},{10,11... | collective-permute-start | bytes 1572872 | tf_op jit(solution)/shard_map/send_sib0/ppermute | solution.py:432
  21.0 19.2 %collective-permute-start.8 = (bf16[128,2048]{1,0:T(8,128)(2,1)S(1)}, bf16[128,2048]{1,0:T(8,128)(2,1)S(1)}, u32[]{:S(2)}, u32[]{:S(2)}) collective-permute-start(bf16[128,2048]{1,0:T(8,128)(2,1)S(1)} %pad_maximum_fusion.1.w_first), channel_id=1, source_target_pairs={{0,2},{1,3},{2,0},{3,1},{4,6},{5,7},{6,4},{7,5},{8,10},{9,11},{10,... | collective-permute-start | bytes 1572872 | tf_op jit(solution)/shard_map/send_w_second/ppermute | solution.py:432
  30.8 10.8 %collective-permute-start.10 = (bf16[128,2048]{1,0:T(8,128)(2,1)S(1)}, bf16[128,2048]{1,0:T(8,128)(2,1)S(1)}, u32[]{:S(2)}, u32[]{:S(2)}) collective-permute-start(bf16[128,2048]{1,0:T(8,128)(2,1)S(1)} %collective-permute-done.9.refs_2_.refs_6_), channel_id=1, source_target_pairs={{0,1},{1,0},{2,3},{3,2},{4,5},{5,4},{6,7},{7,6},{8,9},{9,8},{10,11... | collective-permute-start | bytes 1572872 | tf_op jit(solution)/shard_map/send_sib1/ppermute | solution.py:432
  30.8 12.4 %collective-permute-start.12 = (bf16[128,2048]{1,0:T(8,128)(2,1)S(1)}, bf16[128,2048]{1,0:T(8,128)(2,1)S(1)}, u32[]{:S(2)}, u32[]{:S(2)}) collective-permute-start(bf16[128,2048]{1,0:T(8,128)(2,1)S(1)} %collective-permute-done.11.refs_4_.refs_8_), channel_id=1, source_target_pairs={{0,1},{1,0},{2,3},{3,2},{4,5},{5,4},{6,7},{7,6},{8,9},{9,8},{10,11... | collective-permute-start | bytes 1572872 | tf_op jit(solution)/shard_map/send_sib2/ppermute | solution.py:432
  31.3 11.9 %collective-permute-start.14 = (bf16[128,2048]{1,0:T(8,128)(2,1)S(1)}, bf16[128,2048]{1,0:T(8,128)(2,1)S(1)}, u32[]{:S(2)}, u32[]{:S(2)}) collective-permute-start(bf16[128,2048]{1,0:T(8,128)(2,1)S(1)} %collective-permute-done.13.refs_6_.refs_10_), channel_id=1, source_target_pairs={{0,1},{1,0},{2,3},{3,2},{4,5},{5,4},{6,7},{7,6},{8,9},{9,8},{10,11... | collective-permute-start | bytes 1572872 | tf_op jit(solution)/shard_map/send_sib3/ppermute | solution.py:432
  33.8 12.2 %collective-permute-start.16 = (bf16[256,256]{1,0:T(8,128)(2,1)S(1)}, bf16[256,256]{1,0:T(8,128)(2,1)S(1)}, u32[]{:S(2)}, u32[]{:S(2)}) collective-permute-start(bf16[256,256]{1,0:T(8,128)(2,1)S(1)} %get-tuple-element.64), channel_id=1, source_target_pairs={{0,24},{8,16},{16,8},{24,0},{1,25},{9,17},{17,9},{25,1},{2,26},{10... | collective-permute-start | bytes 393224 | tf_op jit(solution)/shard_map/send_n3/ppermute | solution.py:432
  49.6 17.0 %collective-permute-start.26 = (bf16[128,2048]{1,0:T(8,128)(2,1)S(1)}, bf16[128,2048]{1,0:T(8,128)(2,1)S(1)}, u32[]{:S(2)}, u32[]{:S(2)}) collective-permute-start(bf16[128,2048]{1,0:T(8,128)(2,1)S(1)} %get-tuple-element.66), channel_id=1, source_target_pairs={{0,2},{1,3},{2,0},{3,1},{4,6},{5,7},{6,4},{7,5},{8,10},{9,11},{10,... | collective-permute-start | bytes 1572872 | tf_op jit(solution)/shard_map/send_terms/ppermute | solution.py:432
  55.2 9.3 %collective-permute-start.24 = (bf16[256,256]{1,0:T(8,128)(2,1)S(1)}, bf16[256,256]{1,0:T(8,128)(2,1)S(1)}, u32[]{:S(2)}, u32[]{:S(2)}) collective-permute-start(bf16[256,256]{1,0:T(8,128)(2,1)S(1)} %get-tuple-element.60), channel_id=1, source_target_pairs={{0,24},{8,16},{16,8},{24,0},{1,25},{9,17},{17,9},{25,1},{2,26},{10... | collective-permute-start | bytes 393224 | tf_op jit(solution)/shard_map/send_d3/ppermute | solution.py:432
  58.3 22.2 %collective-permute-start.19 = (bf16[128,2048]{1,0:T(8,128)(2,1)S(1)}, bf16[128,2048]{1,0:T(8,128)(2,1)S(1)}, u32[]{:S(2)}, u32[]{:S(2)}) collective-permute-start(bf16[128,2048]{1,0:T(8,128)(2,1)S(1)} %get-tuple-element.70), channel_id=1, source_target_pairs={{0,8},{8,0},{16,24},{24,16},{1,9},{9,1},{17,25},{25,17},{2,10},{10... | collective-permute-start | bytes 1572872 | tf_op jit(solution)/shard_map/send_mixed1/ppermute | solution.py:432
  59.3 24.1 %collective-permute-start.20 = (bf16[128,2048]{1,0:T(8,128)(2,1)S(1)}, bf16[128,2048]{1,0:T(8,128)(2,1)S(1)}, u32[]{:S(2)}, u32[]{:S(2)}) collective-permute-start(bf16[128,2048]{1,0:T(8,128)(2,1)S(1)} %get-tuple-element.71), channel_id=1, source_target_pairs={{0,16},{8,24},{16,0},{24,8},{1,17},{9,25},{17,1},{25,9},{2,18},{10... | collective-permute-start | bytes 1572872 | tf_op jit(solution)/shard_map/send_mixed2/ppermute | solution.py:432
  61.0 23.8 %collective-permute-start.21 = (bf16[128,2048]{1,0:T(8,128)(2,1)S(1)}, bf16[128,2048]{1,0:T(8,128)(2,1)S(1)}, u32[]{:S(2)}, u32[]{:S(2)}) collective-permute-start(bf16[128,2048]{1,0:T(8,128)(2,1)S(1)} %get-tuple-element.72), channel_id=1, source_target_pairs={{0,24},{8,16},{16,8},{24,0},{1,25},{9,17},{17,9},{25,1},{2,26},{10... | collective-permute-start | bytes 1572872 | tf_op jit(solution)/shard_map/send_mixed3/ppermute | solution.py:432
  67.1 21.5 %collective-permute-start.31 = (bf16[64,2048]{1,0:T(8,128)(2,1)S(1)}, bf16[64,2048]{1,0:T(8,128)(2,1)S(1)}, u32[]{:S(2)}, u32[]{:S(2)}) collective-permute-start(bf16[64,2048]{1,0:T(8,128)(2,1)S(1)} %slice.35), channel_id=1, source_target_pairs={{0,4},{1,5},{2,6},{3,7},{4,0},{5,1},{6,2},{7,3},{8,12},{9,13},{10,... | collective-permute-start | bytes 786440 | tf_op jit(solution)/shard_map/send_pair_terms/ppermute | solution.py:432
  76.0 16.2 %collective-permute-start.29 = (bf16[8,128,128]{2,1,0:T(8,128)(2,1)S(1)}, bf16[8,128,128]{2,1,0:T(8,128)(2,1)S(1)}, u32[]{:S(2)}, u32[]{:S(2)}) collective-permute-start(bf16[8,128,128]{2,1,0:T(8,128)(2,1)S(1)} %add.35), channel_id=1, source_target_pairs={{4,0},{5,1},{6,2},{7,3},{12,8},{13,9},{14,10},{15,11},{20,16},{21,... | collective-permute-start | bytes 786440 | tf_op jit(solution)/shard_map/send_d_far/ppermute | solution.py:432
  88.6 17.2 %collective-permute-start.25 = (bf16[3,128,1024]{2,1,0:T(8,128)(2,1)S(1)}, bf16[3,128,1024]{2,1,0:T(8,128)(2,1)S(1)}, u32[]{:S(2)}, u32[]{:S(2)}) collective-permute-start(bf16[3,128,1024]{2,1,0:T(8,128)(2,1)S(1)} %get-tuple-element.76), channel_id=1, source_target_pairs={{0,1},{1,0},{2,3},{3,2},{4,5},{5,4},{6,7},{7,6},{8,9},{9,8},{10,11... | collective-permute-start | bytes 2359304 | tf_op jit(solution)/shard_map/send_parts/ppermute | solution.py:432
  89.7 13.0 %collective-permute-start.33 = (bf16[64,2048]{1,0:T(8,128)(2,1)S(1)}, bf16[64,2048]{1,0:T(8,128)(2,1)S(1)}, u32[]{:S(2)}, u32[]{:S(2)}) collective-permute-start(bf16[64,2048]{1,0:T(8,128)(2,1)S(1)} %fusion.t0), channel_id=1, source_target_pairs={{0,16},{8,24},{16,0},{24,8},{1,17},{9,25},{17,1},{25,9},{2,18},{10... | collective-permute-start | bytes 786440 | tf_op jit(solution)/shard_map/send_share2/ppermute | solution.py:432
  91.1 12.7 %collective-permute-start.34 = (bf16[64,2048]{1,0:T(8,128)(2,1)S(1)}, bf16[64,2048]{1,0:T(8,128)(2,1)S(1)}, u32[]{:S(2)}, u32[]{:S(2)}) collective-permute-start(bf16[64,2048]{1,0:T(8,128)(2,1)S(1)} %fusion.t0), channel_id=1, source_target_pairs={{0,24},{8,16},{16,8},{24,0},{1,25},{9,17},{17,9},{25,1},{2,26},{10... | collective-permute-start | bytes 786440 | tf_op jit(solution)/shard_map/send_share3/ppermute | solution.py:432
  92.3 13.5 %collective-permute-start.28 = (bf16[8,128,128]{2,1,0:T(8,128)(2,1)S(1)}, bf16[8,128,128]{2,1,0:T(8,128)(2,1)S(1)}, u32[]{:S(2)}, u32[]{:S(2)}) collective-permute-start(bf16[8,128,128]{2,1,0:T(8,128)(2,1)S(1)} %collective-permute-done.27.near), channel_id=1, source_target_pairs={{0,1},{1,0},{2,3},{3,2},{4,5},{5,4},{6,7},{7,6},{8,9},{9,8},{10,11... | collective-permute-start | bytes 786440 | tf_op jit(solution)/shard_map/send_d_near_sib/ppermute | solution.py:432
  (19 other events, 162.1 us)
